TPU v7x, 32 devices: a whole 2x2x4 slice. The times are simulated.
32 devices in a mesh: dp: 4 (over z), fsdp: 8 (over y, x, core).
Axes of the slice: x: 2, y: 2, z: 4, core: 2. Of those that a mesh axis runs over, the one named last changes fastest.
Arguments:
- tokens: bfloat16 [12288, 1024], P(('dp', 'fsdp')), may hold values from -6 to 6
- cotangent: bfloat16 [12288, 1024], P(('dp', 'fsdp')), may hold values from -6 to 6
- lengths: int32 [4, 4], P('dp'), may hold values from 1 to 2689, 3072 in all within a row
- adapter_index: int32 [4, 4], P('dp'), may hold values from 0 to 7
- routes: int32 [12288, 8], P(('dp', 'fsdp')), may hold values from 0 to 15, all different within a row; in each aligned block of 384 rows (0 to 383, 384 to 767, ...) at most 256 rows name the same one
- deal: int32 [4], replicated, may hold values from 0 to 3, as said below
- norm_gain_pair: bfloat16 [1024, 2], P(('dp', 'fsdp')), may hold values from 0.5 to 1.5
- query_weight: bfloat16 [1024, 1024], P(('dp', 'fsdp')), may hold values from -0.1875 to 0.1875
- key_weight: bfloat16 [1024, 512], P(('dp', 'fsdp')), may hold values from -0.1875 to 0.1875
- value_weight: bfloat16 [1024, 512], P(('dp', 'fsdp')), may hold values from -0.1875 to 0.1875
- output_weight_transposed: bfloat16 [1024, 1024], P(('dp', 'fsdp')), may hold values from -1.5 to 1.5
- router_weight: bfloat16 [1024, 16], P(('dp', 'fsdp')), may hold values from -0.09375 to 0.09375
- expert_input_weight: bfloat16 [1024, 16, 1024], P(None, 'fsdp'), may hold values from -0.1875 to 0.1875
- expert_output_weight: bfloat16 [1024, 16, 512], P(None, 'fsdp'), may hold values from -0.75 to 0.75
- adapter_input_factors: bfloat16 [7, 1024, 128], replicated, may hold values from -0.1875 to 0.1875
- adapter_down_first: bfloat16 [512, 128], replicated, may hold values from -0.75 to 0.75
- adapter_wide_second: bfloat16 [3, 128, 1024], replicated, may hold values from -0.75 to 0.75
- adapter_key_value_second: bfloat16 [2, 128, 512], replicated, may hold values from -0.75 to 0.75
- adapter_hidden_second: bfloat16 [2, 128, 512], replicated, may hold values from -0.75 to 0.75
- adapter_router_second: bfloat16 [128, 16], replicated, may hold values from -0.3125 to 0.3125
Outputs:
- layer_out: bfloat16 [12288, 1024], P(('dp', 'fsdp'))
- input_grad: float32 [12288, 1024], P(('dp', 'fsdp'))
- adapter_input_gradient: float32 [7, 1024, 128], replicated
- grad_lora_down_a: float32 [512, 128], replicated
- grad_lora_wide_b: float32 [3, 128, 1024], replicated
- grad_lora_kv_b: float32 [2, 128, 512], replicated
- grad_lora_ff_b: float32 [2, 128, 512], replicated
- grad_lora_route_b: float32 [128, 16], replicated
Inputs may be any that keep to these rules, and one draw needn't show every extreme that they name: `lengths`: each row sums to 3072, and its largest entry is 2689. `routes`: each token names 8 different experts; among the rows of one device no expert is named more than 256 times. Each group number appears once; for some dealt group g, deal[g] is (g + 2) mod 4.
All inputs are finite; a program needn't handle non-finite values.
Results may differ from a plain program's by a relative error of at most 0.019.
Values may be sent and summed in bfloat16 or wider, within the bound.
A program may use at most 320 MiB of HBM per device.

v0:
```python
import math

import jax
import jax.numpy as jnp
from jax import lax
from jax.sharding import PartitionSpec as P

MODEL_WIDTH = 1024
HEADS = 16
KEY_VALUE_HEADS = 8
HEAD_WIDTH = 64
HIDDEN_UNITS = 512
TOPK = 8
EXPERT_COUNT = 16
ADAPTER_COUNT = 8
ADAPTER_RANK = 16
CAP = 256


EPSILON = 1e-06
ROPE_BASE = 10000.0
MASKED = -1e30


def matrix_product(first_op, second_op):
    return jnp.dot(first_op, second_op, preferred_element_type=jnp.float32)


def contract_matrices(first_op, second_op, first_dim, second_dim):
    return lax.dot_general(
        first_op,
        second_op,
        (((first_dim,), (second_dim,)), ((), ())),
        preferred_element_type=jnp.float32,
    )


def token_meta(sequence_lengths, selected_experts, row_index):
    offsets = jnp.cumsum(sequence_lengths) - sequence_lengths
    seq_number = jnp.sum((row_index[:, None] >= offsets[None, 1:]).astype(jnp.int32), axis=1)
    onehot = seq_number[:, None] == jnp.arange(sequence_lengths.shape[0], dtype=jnp.int32)[None, :]
    seq_start = jnp.sum(jnp.where(onehot, offsets[None, :], 0), axis=1)
    adapter_pick = jnp.sum(jnp.where(onehot, selected_experts[None, :], 0), axis=1)
    return (seq_start, adapter_pick)


def rope_tables(position):
    half_dim = HEAD_WIDTH // 2
    frequency = ROPE_BASE ** (-jnp.arange(half_dim, dtype=jnp.float32) / half_dim)
    angles = position.astype(jnp.float32)[:, None] * frequency[None, :]
    return (jnp.cos(angles), jnp.sin(angles))


def rotate(tensor, cosine_table, sine_table):
    rows_here = tensor.shape[0]
    head_view = tensor.reshape(rows_here, -1, HEAD_WIDTH)
    half_dim = HEAD_WIDTH // 2
    first_half = head_view[..., :half_dim]
    second_half = head_view[..., half_dim:]
    cos_view = cosine_table[:, None, :]
    sin_view = sine_table[:, None, :]
    turned = jnp.concatenate(
        [
            first_half * cos_view - second_half * sin_view,
            second_half * cos_view + first_half * sin_view,
        ],
        axis=-1,
    )
    return turned.reshape(rows_here, -1)


def experts_forward_pass(
    row_input, row_lifted, input_weights, output_weights, adapter_hidden_second, adapter_down_first
):
    stacked_width = row_lifted.shape[2] // 2
    gate_lifted = matrix_product(row_lifted[..., :stacked_width], adapter_hidden_second[0]).astype(
        jnp.bfloat16
    )
    upward_lifted = matrix_product(
        row_lifted[..., stacked_width:], adapter_hidden_second[1]
    ).astype(jnp.bfloat16)
    lifted_rows = jnp.concatenate([gate_lifted, upward_lifted], axis=-1).astype(jnp.float32)
    preactivation = (
        jnp.einsum("tep,pty->tey", row_input, input_weights, preferred_element_type=jnp.float32)
        + lifted_rows
    )
    width = preactivation.shape[2] // 2
    inner_activation = (
        jax.nn.silu(preactivation[..., :width]) * preactivation[..., width:]
    ).astype(jnp.bfloat16)
    result = jnp.einsum(
        "yut,jyt->yuj", inner_activation, output_weights, preferred_element_type=jnp.float32
    ).astype(jnp.bfloat16)
    reduced_output = matrix_product(inner_activation, adapter_down_first).astype(jnp.bfloat16)
    return (result, reduced_output, preactivation)


def experts_backward_pass(
    result_gradient,
    reduced_output_gradient,
    preactivation,
    input_weights,
    output_weights,
    adapter_down_first,
):
    width = preactivation.shape[2] // 2
    gate_part = preactivation[..., :width]
    up_part = preactivation[..., width:]
    squashed = jax.nn.sigmoid(gate_part)
    activated = gate_part * squashed
    inner_activation = (activated * up_part).astype(jnp.bfloat16)
    inner_grad = jnp.einsum(
        "tep,pty->tey", result_gradient, output_weights, preferred_element_type=jnp.float32
    ) + contract_matrices(reduced_output_gradient, adapter_down_first, 2, 1)
    gate_grad = (inner_grad * up_part * squashed * (1.0 + gate_part * (1.0 - squashed))).astype(
        jnp.bfloat16
    )
    up_grad = (inner_grad * activated).astype(jnp.bfloat16)
    paired_gradients = jnp.concatenate([gate_grad, up_grad], axis=-1)
    row_grad = jnp.einsum(
        "yut,jyt->yuj", paired_gradients, input_weights, preferred_element_type=jnp.float32
    ).astype(jnp.bfloat16)
    down_first_factor_gradient = jnp.einsum(
        "dlj,dlc->jc", inner_activation, reduced_output_gradient, preferred_element_type=jnp.float32
    )
    return (row_grad, paired_gradients, down_first_factor_gradient)


def local(
    tokens,
    cotangent,
    lengths,
    adapter_index,
    routes,
    deal,
    norm_gain_pair,
    query_weight,
    key_weight,
    value_weight,
    output_weight_transposed,
    router_weight,
    expert_input_weight,
    expert_output_weight,
    adapter_input_factors,
    adapter_down_first,
    adapter_wide_second,
    adapter_key_value_second,
    adapter_hidden_second,
    adapter_router_second,
):
    shards = lax.axis_size("fsdp")
    group_count = lax.axis_size("dp")
    rows_here = tokens.shape[0]
    group_rows = rows_here * shards
    stacked_width = ADAPTER_COUNT * ADAPTER_RANK
    group_heads = HEADS // KEY_VALUE_HEADS
    score_scale = HEAD_WIDTH ** (-0.5)
    my_group = lax.axis_index("dp")
    group_ids = jnp.arange(group_count, dtype=jnp.int32)
    source_group = jnp.sum(jnp.where(group_ids == my_group, deal, 0))
    target_group = jnp.sum(jnp.where(deal == my_group, group_ids, 0))
    send_mask = (group_ids == target_group)[:, None, None]
    zero_half = jnp.zeros((), jnp.bfloat16)
    dealt_rows = (
        lax.all_to_all(
            jnp.where(send_mask, tokens[None], zero_half),
            "dp",
            split_axis=0,
            concat_axis=0,
            tiled=True,
        ),
        lax.all_to_all(
            jnp.where(send_mask, cotangent[None], zero_half),
            "dp",
            split_axis=0,
            concat_axis=0,
            tiled=True,
        ),
    )
    tokens = lax.dynamic_index_in_dim(dealt_rows[0], source_group, 0, keepdims=False)
    cotangent = lax.dynamic_index_in_dim(dealt_rows[1], source_group, 0, keepdims=False)
    my_index = lax.axis_index("fsdp") * rows_here + jnp.arange(rows_here, dtype=jnp.int32)
    my_start, my_pick = token_meta(lengths[0], adapter_index[0], my_index)
    stacked_mask = (
        jnp.arange(stacked_width, dtype=jnp.int32)[None, :] // ADAPTER_RANK == my_pick[:, None]
    ).astype(jnp.float32)
    halved_mask = stacked_mask.astype(jnp.bfloat16)
    cosine_table, sine_table = rope_tables(my_index - my_start)
    frozen_weights = (
        lax.all_gather(norm_gain_pair, ("dp", "fsdp"), axis=0, tiled=True),
        lax.all_gather(query_weight, ("dp", "fsdp"), axis=0, tiled=True),
        lax.all_gather(key_weight, ("dp", "fsdp"), axis=0, tiled=True),
        lax.all_gather(value_weight, ("dp", "fsdp"), axis=0, tiled=True),
        lax.all_gather(output_weight_transposed, ("dp", "fsdp"), axis=0, tiled=True),
        lax.all_gather(router_weight, ("dp", "fsdp"), axis=0, tiled=True),
    )
    gains, complete_query, complete_key, complete_value, complete_output, complete_router = (
        frozen_weights
    )
    input_weights, output_weights = (
        lax.all_gather(expert_input_weight, "fsdp", axis=1, tiled=True),
        lax.all_gather(expert_output_weight, "fsdp", axis=1, tiled=True),
    )
    input_value = tokens.astype(jnp.float32)
    gain_one = gains[:, 0].astype(jnp.float32)
    gain_two = gains[:, 1].astype(jnp.float32)
    inv_one = lax.rsqrt(jnp.mean(input_value * input_value, axis=1, keepdims=True) + EPSILON)
    normed_input = (input_value * inv_one * gain_one).astype(jnp.bfloat16)
    first_lowrank_state = jnp.einsum(
        "pg,igv->piv", normed_input, adapter_input_factors[0:3], preferred_element_type=jnp.float32
    )
    first_lowrank = (first_lowrank_state * stacked_mask[:, None, :]).astype(jnp.bfloat16)
    query_before_rotation = matrix_product(normed_input, complete_query) + matrix_product(
        first_lowrank[:, 0], adapter_wide_second[0]
    )
    key_before_rotation = matrix_product(normed_input, complete_key) + matrix_product(
        first_lowrank[:, 1], adapter_key_value_second[0]
    )
    value_before_output = matrix_product(normed_input, complete_value) + matrix_product(
        first_lowrank[:, 2], adapter_key_value_second[1]
    )
    query_rows = rotate(query_before_rotation, cosine_table, sine_table).astype(jnp.bfloat16)
    key_rows = rotate(key_before_rotation, cosine_table, sine_table).astype(jnp.bfloat16)
    value_rows = value_before_output.astype(jnp.bfloat16)
    all_keys, all_values = (
        lax.all_gather(key_rows, "fsdp", axis=0, tiled=True),
        lax.all_gather(value_rows, "fsdp", axis=0, tiled=True),
    )
    block_rows = math.gcd(group_rows, 512)
    blocks = group_rows // block_rows
    key_blocks = all_keys.reshape(blocks, block_rows, KEY_VALUE_HEADS, HEAD_WIDTH)
    value_blocks = all_values.reshape(blocks, block_rows, KEY_VALUE_HEADS, HEAD_WIDTH)
    block_first = jnp.arange(blocks, dtype=jnp.int32) * block_rows
    query_heads = query_rows.reshape(rows_here, KEY_VALUE_HEADS, group_heads, HEAD_WIDTH)
    last_query = my_index[-1]
    first_start = jnp.min(my_start)

    def scored(key_blk, first_row):
        key_index = first_row + jnp.arange(block_rows, dtype=jnp.int32)
        visible = (key_index[None, :] <= my_index[:, None]) & (
            key_index[None, :] >= my_start[:, None]
        )
        raw_scores = (
            jnp.einsum("qkgd,nkd->kgqn", query_heads, key_blk, preferred_element_type=jnp.float32)
            * score_scale
        )
        masked_scores = jnp.where(visible[None, None], raw_scores, MASKED)
        return (masked_scores.reshape(HEADS, rows_here, block_rows), visible)

    def active(first_row):
        return (first_row <= last_query) & (first_row + block_rows - 1 >= first_start)

    def stat_step(carry_in, block_item):
        key_blk, first_row = block_item

        def stat_update(stats_now):
            running_max, running_sum = stats_now
            scores, visible = scored(key_blk, first_row)
            new_max = jnp.maximum(running_max, jnp.max(scores, axis=2))
            weights_now = jnp.where(visible[None], jnp.exp(scores - new_max[:, :, None]), 0.0)
            return (
                new_max,
                running_sum * jnp.exp(running_max - new_max) + jnp.sum(weights_now, axis=2),
            )

        return (
            lax.cond(active(first_row), stat_update, lambda stats_now: stats_now, carry_in),
            None,
        )

    start_stats = (
        jnp.full((HEADS, rows_here), MASKED, jnp.float32),
        jnp.zeros((HEADS, rows_here), jnp.float32),
    )
    (running_max, running_sum), _ = lax.scan(stat_step, start_stats, (key_blocks, block_first))

    def probs_of(key_blk, first_row):
        scores, visible = scored(key_blk, first_row)
        return jnp.where(
            visible[None], jnp.exp(scores - running_max[:, :, None]) / running_sum[:, :, None], 0.0
        )

    def mix_step(carry_in, block_item):
        key_blk, value_blk, first_row = block_item

        def mix_update(mixed_out):
            probabilities = probs_of(key_blk, first_row).reshape(
                KEY_VALUE_HEADS, group_heads, rows_here, block_rows
            )
            return mixed_out + jnp.einsum(
                "kgqn,nkd->qkgd",
                probabilities.astype(jnp.bfloat16),
                value_blk,
                preferred_element_type=jnp.float32,
            )

        return (
            lax.cond(active(first_row), mix_update, lambda mixed_out: mixed_out, carry_in),
            None,
        )

    zero_heads = jnp.zeros((rows_here, KEY_VALUE_HEADS, group_heads, HEAD_WIDTH), jnp.float32)
    mixed_out, _ = lax.scan(mix_step, zero_heads, (key_blocks, value_blocks, block_first))
    attention_output = mixed_out.reshape(rows_here, -1).astype(jnp.bfloat16)
    output_lowrank = (
        matrix_product(attention_output, adapter_input_factors[6]) * stacked_mask
    ).astype(jnp.bfloat16)
    hidden_state = (
        input_value
        + contract_matrices(attention_output, complete_output, 1, 1)
        + matrix_product(output_lowrank, adapter_wide_second[1])
    )
    inv_two = lax.rsqrt(jnp.mean(hidden_state * hidden_state, axis=1, keepdims=True) + EPSILON)
    second_normed_input = (hidden_state * inv_two * gain_two).astype(jnp.bfloat16)
    second_z = jnp.einsum(
        "pg,igv->piv",
        second_normed_input,
        adapter_input_factors[3:6],
        preferred_element_type=jnp.float32,
    )
    second_lowrank = (second_z * stacked_mask[:, None, :]).astype(jnp.bfloat16)
    router_logits = matrix_product(second_normed_input, complete_router) + matrix_product(
        second_lowrank[:, 0], adapter_router_second
    )
    picks = routes[:, :, None] == jnp.arange(EXPERT_COUNT, dtype=jnp.int32)[None, None, :]
    gates = jax.nn.softmax(
        jnp.sum(jnp.where(picks, router_logits[:, None, :], 0.0), axis=2), axis=1
    )
    flat_pick = picks.reshape(rows_here * TOPK, EXPERT_COUNT).astype(jnp.int32)
    earlier = jnp.cumsum(flat_pick, axis=0) - flat_pick
    slot_index = jnp.sum(earlier * flat_pick, axis=1) + routes.reshape(-1) * CAP
    token_of = jnp.arange(rows_here * TOPK, dtype=jnp.int32) // TOPK
    source = jnp.zeros((EXPERT_COUNT * CAP,), jnp.int32).at[slot_index].set(token_of)
    filled = jnp.zeros((EXPERT_COUNT * CAP,), jnp.bool_).at[slot_index].set(True)
    row_input = jnp.where(filled[:, None], second_normed_input[source], zero_half)
    row_lifted = jnp.where(
        filled[:, None], second_lowrank[source, 1:3].reshape(-1, 2 * stacked_width), zero_half
    )
    result, reduced_output, preactivation = experts_forward_pass(
        row_input.reshape(EXPERT_COUNT, CAP, -1),
        row_lifted.reshape(EXPERT_COUNT, CAP, -1),
        input_weights,
        output_weights,
        adapter_hidden_second,
        adapter_down_first,
    )
    result = result.reshape(EXPERT_COUNT * CAP, -1)
    reduced_output = reduced_output.reshape(EXPERT_COUNT * CAP, -1)
    result_k = result[slot_index].reshape(rows_here, TOPK, -1)
    reduced_k = reduced_output[slot_index].reshape(rows_here, TOPK, -1)
    experts_combined_sum = jnp.sum(gates[:, :, None] * result_k, axis=1)
    combined = jnp.sum(gates[:, :, None] * reduced_k, axis=1)
    down_lowrank = (combined * stacked_mask).astype(jnp.bfloat16)
    layer_output_sum = (
        hidden_state + experts_combined_sum + matrix_product(down_lowrank, adapter_wide_second[2])
    )
    refetched = (
        lax.all_gather(norm_gain_pair, ("dp", "fsdp"), axis=0, tiled=True),
        lax.all_gather(query_weight, ("dp", "fsdp"), axis=0, tiled=True),
        lax.all_gather(key_weight, ("dp", "fsdp"), axis=0, tiled=True),
        lax.all_gather(value_weight, ("dp", "fsdp"), axis=0, tiled=True),
        lax.all_gather(output_weight_transposed, ("dp", "fsdp"), axis=0, tiled=True),
        lax.all_gather(router_weight, ("dp", "fsdp"), axis=0, tiled=True),
    )
    gains_back, query_back, key_back, value_back, output_backward, router_back = refetched
    back_in, back_out = (
        lax.all_gather(expert_input_weight, "fsdp", axis=1, tiled=True),
        lax.all_gather(expert_output_weight, "fsdp", axis=1, tiled=True),
    )
    grad_out = cotangent.astype(jnp.float32)
    grad_wide_down = contract_matrices(down_lowrank, cotangent, 0, 0)
    down_projection_gradient = (
        contract_matrices(cotangent, adapter_wide_second[2], 1, 1).astype(jnp.bfloat16)
        * halved_mask
    )
    down_grad_value = down_projection_gradient.astype(jnp.float32)
    gate_grad = jnp.sum(grad_out[:, None, :] * result_k, axis=2) + jnp.sum(
        down_grad_value[:, None, :] * reduced_k, axis=2
    )
    result_gradient = (gates[:, :, None] * grad_out[:, None, :]).astype(jnp.bfloat16)
    reduced_output_gradient = (gates[:, :, None] * down_grad_value[:, None, :]).astype(jnp.bfloat16)
    slot_result_grad = (
        jnp.zeros((EXPERT_COUNT * CAP, MODEL_WIDTH), jnp.bfloat16)
        .at[slot_index]
        .set(result_gradient.reshape(-1, MODEL_WIDTH))
    )
    slot_reduced_grad = (
        jnp.zeros((EXPERT_COUNT * CAP, stacked_width), jnp.bfloat16)
        .at[slot_index]
        .set(reduced_output_gradient.reshape(-1, stacked_width))
    )
    row_grad, paired_gradients, down_first_factor_gradient = experts_backward_pass(
        slot_result_grad.reshape(EXPERT_COUNT, CAP, -1),
        slot_reduced_grad.reshape(EXPERT_COUNT, CAP, -1),
        preactivation,
        back_in,
        back_out,
        adapter_down_first,
    )
    row_grad = row_grad.reshape(EXPERT_COUNT * CAP, -1)
    paired_gradients = paired_gradients.reshape(EXPERT_COUNT * CAP, -1)
    row_grad_k = row_grad[slot_index].reshape(rows_here, TOPK, -1)
    paired_keys = paired_gradients[slot_index].reshape(rows_here, TOPK, -1)
    normed_two_grad = jnp.sum(row_grad_k.astype(jnp.float32), axis=1)
    lift_gate_grad = jnp.einsum(
        "jex,ox->jo",
        paired_keys[..., :HIDDEN_UNITS],
        adapter_hidden_second[0],
        preferred_element_type=jnp.float32,
    )
    lift_up_grad = jnp.einsum(
        "jex,ox->jo",
        paired_keys[..., HIDDEN_UNITS:],
        adapter_hidden_second[1],
        preferred_element_type=jnp.float32,
    )
    hidden_factor_gradient = jnp.stack(
        [
            jnp.einsum(
                "ts,tkf->sf",
                second_lowrank[:, 1],
                paired_keys[..., :HIDDEN_UNITS],
                preferred_element_type=jnp.float32,
            ),
            jnp.einsum(
                "ts,tkf->sf",
                second_lowrank[:, 2],
                paired_keys[..., HIDDEN_UNITS:],
                preferred_element_type=jnp.float32,
            ),
        ]
    )
    gate_logit = gates * (gate_grad - jnp.sum(gates * gate_grad, axis=1, keepdims=True))
    router_logit_gradient = jnp.sum(jnp.where(picks, gate_logit[:, :, None], 0.0), axis=1).astype(
        jnp.bfloat16
    )
    normed_two_grad = normed_two_grad + contract_matrices(router_logit_gradient, router_back, 1, 1)
    router_lowrank_gradient = contract_matrices(router_logit_gradient, adapter_router_second, 1, 1)
    router_factor_gradient = contract_matrices(second_lowrank[:, 0], router_logit_gradient, 0, 0)
    second_factor_gradient = (
        jnp.stack([router_lowrank_gradient, lift_gate_grad, lift_up_grad], axis=1).astype(
            jnp.bfloat16
        )
        * halved_mask[:, None, :]
    )
    input_gradient_second = jnp.einsum(
        "td,tsr->sdr",
        second_normed_input,
        second_factor_gradient,
        preferred_element_type=jnp.float32,
    )
    normed_two_grad = normed_two_grad + jnp.einsum(
        "kxb,xvb->kv",
        second_factor_gradient,
        adapter_input_factors[3:6],
        preferred_element_type=jnp.float32,
    )
    weighted_two = gains_back[:, 1].astype(jnp.float32) * normed_two_grad
    hidden_grad = (
        grad_out
        + inv_two * weighted_two
        - hidden_state * inv_two**3 * jnp.mean(weighted_two * hidden_state, axis=1, keepdims=True)
    )
    output_gradient = hidden_grad.astype(jnp.bfloat16)
    grad_wide_out = contract_matrices(output_lowrank, output_gradient, 0, 0)
    output_lowrank_gradient = (
        contract_matrices(output_gradient, adapter_wide_second[1], 1, 1).astype(jnp.bfloat16)
        * halved_mask
    )
    input_gradient_output = contract_matrices(attention_output, output_lowrank_gradient, 0, 0)
    attention_output_gradient = (
        matrix_product(output_gradient, output_backward)
        + contract_matrices(output_lowrank_gradient, adapter_input_factors[6], 1, 1)
    ).astype(jnp.bfloat16)
    grad_heads = attention_output_gradient.reshape(
        rows_here, KEY_VALUE_HEADS, group_heads, HEAD_WIDTH
    )
    row_delta = jnp.transpose(
        jnp.sum(grad_heads.astype(jnp.float32) * mixed_out, axis=3), (1, 2, 0)
    ).reshape(HEADS, rows_here)

    def back_step(carry_in, block_item):
        key_blk, value_blk, first_row = block_item

        def back_update(query_grad):
            probabilities = probs_of(key_blk, first_row)
            prob_grad = jnp.einsum(
                "qkgd,nkd->kgqn", grad_heads, value_blk, preferred_element_type=jnp.float32
            ).reshape(HEADS, rows_here, block_rows)
            score_grad = (
                (probabilities * (prob_grad - row_delta[:, :, None]))
                .astype(jnp.bfloat16)
                .reshape(KEY_VALUE_HEADS, group_heads, rows_here, block_rows)
            )
            low_probs = probabilities.astype(jnp.bfloat16).reshape(
                KEY_VALUE_HEADS, group_heads, rows_here, block_rows
            )
            query_grad = (
                query_grad
                + jnp.einsum(
                    "kgqn,nkd->qkgd", score_grad, key_blk, preferred_element_type=jnp.float32
                )
                * score_scale
            )
            key_grad = (
                jnp.einsum(
                    "kgqn,qkgd->nkd", score_grad, query_heads, preferred_element_type=jnp.float32
                )
                * score_scale
            )
            value_grad = jnp.einsum(
                "kgqn,qkgd->nkd", low_probs, grad_heads, preferred_element_type=jnp.float32
            )
            return (query_grad, key_grad, value_grad)

        def skipped(query_grad):
            empty_grad = jnp.zeros((block_rows, KEY_VALUE_HEADS, HEAD_WIDTH), jnp.float32)
            return (query_grad, empty_grad, empty_grad)

        query_grad, key_grad, value_grad = lax.cond(
            active(first_row), back_update, skipped, carry_in
        )
        return (query_grad, (key_grad, value_grad))

    query_grad, (key_grads, value_grads) = lax.scan(
        back_step, zero_heads, (key_blocks, value_blocks, block_first)
    )
    mine_keys, mine_values = (
        lax.psum_scatter(
            key_grads.reshape(group_rows, -1).astype(jnp.bfloat16),
            "fsdp",
            scatter_dimension=0,
            tiled=True,
        ).astype(jnp.float32),
        lax.psum_scatter(
            value_grads.reshape(group_rows, -1).astype(jnp.bfloat16),
            "fsdp",
            scatter_dimension=0,
            tiled=True,
        ).astype(jnp.float32),
    )
    query_before_rotation_gradient = rotate(
        query_grad.reshape(rows_here, -1), cosine_table, -sine_table
    ).astype(jnp.bfloat16)
    key_before_rotation_gradient = rotate(mine_keys, cosine_table, -sine_table).astype(jnp.bfloat16)
    value_before_output_gradient = mine_values.astype(jnp.bfloat16)
    normed_grad = (
        contract_matrices(query_before_rotation_gradient, query_back, 1, 1)
        + contract_matrices(key_before_rotation_gradient, key_back, 1, 1)
        + contract_matrices(value_before_output_gradient, value_back, 1, 1)
    )
    first_factor_gradient = (
        jnp.stack(
            [
                contract_matrices(query_before_rotation_gradient, adapter_wide_second[0], 1, 1),
                contract_matrices(key_before_rotation_gradient, adapter_key_value_second[0], 1, 1),
                contract_matrices(value_before_output_gradient, adapter_key_value_second[1], 1, 1),
            ],
            axis=1,
        ).astype(jnp.bfloat16)
        * halved_mask[:, None, :]
    )
    input_gradient_first = jnp.einsum(
        "td,tsr->sdr", normed_input, first_factor_gradient, preferred_element_type=jnp.float32
    )
    normed_grad = normed_grad + jnp.einsum(
        "kxb,xvb->kv",
        first_factor_gradient,
        adapter_input_factors[0:3],
        preferred_element_type=jnp.float32,
    )
    grad_wide_query = contract_matrices(first_lowrank[:, 0], query_before_rotation_gradient, 0, 0)
    key_value_gradient = jnp.stack(
        [
            contract_matrices(first_lowrank[:, 1], key_before_rotation_gradient, 0, 0),
            contract_matrices(first_lowrank[:, 2], value_before_output_gradient, 0, 0),
        ]
    )
    weighted_one = gains_back[:, 0].astype(jnp.float32) * normed_grad
    input_grad = (
        hidden_grad
        + inv_one * weighted_one
        - input_value * inv_one**3 * jnp.mean(weighted_one * input_value, axis=1, keepdims=True)
    )
    back_mask = (group_ids == source_group)[:, None, None]
    zero_full = jnp.zeros((), jnp.float32)
    going_home = (
        lax.all_to_all(
            jnp.where(back_mask, layer_output_sum[None], zero_full).astype(jnp.bfloat16),
            "dp",
            split_axis=0,
            concat_axis=0,
            tiled=True,
        ).astype(jnp.float32),
        lax.all_to_all(
            jnp.where(back_mask, input_grad[None], zero_full).astype(jnp.bfloat16),
            "dp",
            split_axis=0,
            concat_axis=0,
            tiled=True,
        ).astype(jnp.float32),
    )
    layer_out = lax.dynamic_index_in_dim(going_home[0], target_group, 0, keepdims=False).astype(
        jnp.bfloat16
    )
    input_grad = lax.dynamic_index_in_dim(going_home[1], target_group, 0, keepdims=False)
    adapter_input_gradient = jnp.concatenate(
        [input_gradient_first, input_gradient_second, input_gradient_output[None]], axis=0
    )
    wide_factor_gradient = jnp.stack([grad_wide_query, grad_wide_out, grad_wide_down])
    adapter_total = lax.psum(
        (
            adapter_input_gradient,
            down_first_factor_gradient,
            wide_factor_gradient,
            key_value_gradient,
            hidden_factor_gradient,
            router_factor_gradient,
        ),
        ("dp", "fsdp"),
    )
    return (
        layer_out,
        input_grad,
        adapter_total[0],
        adapter_total[1],
        adapter_total[2],
        adapter_total[3],
        adapter_total[4],
        adapter_total[5],
    )


def solution(mesh):
    placed = (
        P(("dp", "fsdp"), None),
        P(("dp", "fsdp"), None),
        P("dp", None),
        P("dp", None),
        P(("dp", "fsdp"), None),
        P(),
        P(("dp", "fsdp"), None),
        P(("dp", "fsdp"), None),
        P(("dp", "fsdp"), None),
        P(("dp", "fsdp"), None),
        P(("dp", "fsdp"), None),
        P(("dp", "fsdp"), None),
        P(None, "fsdp", None),
        P(None, "fsdp", None),
        P(),
        P(),
        P(),
        P(),
        P(),
        P(),
    )
    return jax.shard_map(
        local,
        mesh=mesh,
        in_specs=placed,
        out_specs=(P(("dp", "fsdp"), None), P(("dp", "fsdp"), None), P(), P(), P(), P(), P(), P()),
        check_vma=False,
    )
```

profile of v0, /device:TPU:0, one launch (start us, length us, event | category | flops | bytes accessed | tf_op | source)
XLA Modules:
  0.0 1450.9 jit_solution(2147578679582832061)
XLA Ops:
  24.0 84.3 %all-gather = bf16[32,32,2]{1,2,0:T(2,128)(2,1)S(1)} all-gather(bf16[1,32,2]{1,2,0:T(2,128)(2,1)S(1)} %bitcast.441), channel_id=1, replica_groups=mesh['dp'=4,'fsdp'=8] {'dp','fsdp'}, dimensions={0}, use_global_device_ids=true | all-gather | bytes 4224 | tf_op jit(solution)/shard_map/all_gather | solution.py:190
  126.3 28.8 %all-gather.17.cloned.1.call-done = bf16[1024,512]{1,0:T(8,128)(2,1)} async-done(((bf16[32,512]{1,0:T(8,128)(2,1)}), bf16[1024,512]{1,0:T(8,128)(2,1)}) %all-gather.17.cloned.1.call-update) | async-done | bytes 1048592 | tf_op jit(solution)/shard_map/all_gather | solution.py:193
  174.5 87.5 %all-gather.1 = bf16[32,32,16]{1,2,0:T(8,128)(2,1)S(1)} all-gather(bf16[1,32,16]{1,2,0:T(8,128)(2,1)S(1)} %bitcast.439), channel_id=1, replica_groups=mesh['dp'=4,'fsdp'=8] {'dp','fsdp'}, dimensions={0}, use_global_device_ids=true | all-gather | bytes 33792 | tf_op jit(solution)/shard_map/all_gather | solution.py:195
  279.0 12.3 scatter_custom_fusion.1
  291.3 13.4 scatter_custom_fusion
  333.2 8.9 reshape.1046
  349.6 33.6 %while.57 = (s32[]{:T(128)}, f32[16,384]{1,0:T(8,128)S(1)}, f32[16,384]{1,0:T(8,128)S(1)}, s32[6]{0:T(128)S(1)}, s32[]{:T(128)}, /*index=5*/s32[]{:T(128)}, s32[...) while((s32[]{:T(128)}, f32[16,384]{1,0:T(8,128)S(1)}, ...), condition=%wide.region_13.14_spmd.clone, body=%wide.region_8.13_spmd.clone.sunk | while | flops 428422016 | bytes 27545888 | solution.py:275
  352.7 15.1 %conditional.9 = ((f32[16,384]{1,0:T(8,128)S(1)}, f32[16,384]{1,0:T(8,128)S(1)})) conditional(s32[]{:T(128)} %convert_element_type.485, (f32[16,384]{1,0:T(8,128)S(1)}, f32[16,384]{1,0:T(8,128)S(1)}) %tuple.221, (s32[]{:T(128)}, s32[]{:T(128)}, s32[384]{0:T(512)S(1)}, bf16[6,512,8,64]{1,3,2,0:T(8,128)(2,1)}, s32[]{:T(128)}, ...), branch_computations={%region_9.9_spmd, %region_10.12_spmd} | conditional | flops 428422016 | bytes 27544096 | solution.py:267
  383.4 25.5 %while.58 = (s32[]{:T(128)}, f32[384,8,2,64]{0,3,2,1:T(8,128)S(1)}, s32[6]{0:T(128)S(1)}, s32[]{:T(128)}, s32[]{:T(128)}, /*index=5*/s32[384]{0:T(512)S(1)}, bf1...) while((s32[]{:T(128)}, f32[384,8,2,64]{0,3,2,1:T(8,128)S(1)}, ...), condition=%wide.region_17.18_spmd.clone, body=%wide.region_14.17_spmd.clone.sunk | while | flops 825164672 | bytes 5534495 | solution.py:303
  421.7 20.5 %scatter_custom_fusion.2 = bf16[4096,1024]{1,0:T(8,128)(2,1)} fusion(s32[3072]{0:T(1024)} %bitcast.434, f32[384,1024]{1,0:T(8,128)S(1)} %copy-done.17, f32[3072]{0:T(1024)S(1)} %div.96, bf16[]{:T(256)} %constant.244.clone.1), kind=kCustom, calls=%fused_computation.91 | custom fusion | flops 6291456 | bytes 9974272 | tf_op jit(solution)/shard_map/scatter | solution.py:385
  442.2 10.9 scatter_custom_fusion.3
  453.1 40.4 %gather_fusion.1 = bf16[4096,2,128]{2,0,1:T(8,128)(2,1)} fusion(bf16[384,3,128]{2,0,1:T(8,128)(2,1)S(1)} %fusion.81, s32[4096]{0:T(1024)S(1)} %copy-done.6), kind=kCustom, calls=%fused_computation.1 | custom fusion | bytes 4227072 | tf_op jit(solution)/shard_map/gather | solution.py:337
  503.8 18.3 %gather_fusion = bf16[4096,1024]{1,0:T(8,128)(2,1)} fusion(bf16[384,1024]{1,0:T(8,128)(2,1)S(1)} %multiply_convert_fusion.3, s32[4096]{0:T(1024)S(1)} %copy-done.87), kind=kCustom, calls=%fused_computation | custom fusion | bytes 16793600 | tf_op jit(solution)/shard_map/gather | solution.py:335
  535.3 8.6 all-gather.23.cloned.1.call-done
  543.9 26.7 %convert_add_fusion = f32[16,256,1024]{2,1,0:T(8,128)} fusion(bf16[1024,16,1024]{2,0,1:T(8,128)(2,1)} %all-gather.23.cloned.1.call-done, bf16[16,256,512]{2,1,0:T(8,128)(2,1)} %convolution_convert_fusion.2, bf16[16,256,512]{2,1,0:T(8,128)(2,1)} %convolution_convert_fusion.3, bf16[16,256,1024]{2,1,0:T(8,128)(2,1)} %bitcast.407, ...), kind=kOutput, calls=%fused_computation.73 | convolution fusion | flops 8615100416 | bytes 67112960 | tf_op jit(solution)/shard_map/tep,pty->tey/dot_general | solution.py:84
  570.5 65.1 %all-gather.25.cloned.1.call-done = bf16[1024,16,512]{2,0,1:T(8,128)(2,1)} async-done(((bf16[1024,2,512]{2,0,1:T(8,128)(2,1)}), bf16[1024,16,512]{2,0,1:T(8,128)(2,1)}) %all-gather.25.cloned.1.call-update) | async-done | bytes 16777232 | tf_op jit(solution)/shard_map/all_gather | solution.py:202
  635.7 25.7 %multiply_convert_fusion.1 = (bf16[16,256,512]{2,1,0:T(8,128)(2,1)}, bf16[16,256,512]{2,1,0:T(8,128)(2,1)}, bf16[16,256,512]{2,1,0:T(8,128)(2,1)}) fusion(f32[16,256,1024]{2,1,0:T(8,128)} %convert_add_fusion, f32[16,256,512]{2,1,0:T(8,128)} %fusion.136, bf16[16,256,1024]{2,1,0:T(8,128)(2,1)} %bitcast.408, ...), kind=kOutput, calls=%fused_computation.83 | convolution fusion | flops 4328521728 | bytes 62914560 | tf_op jit(solution)/shard_map/tep,pty->tey/dot_general | solution.py:112
  664.8 11.5 gather_fusion.3
  679.2 11.6 convolution_convert_fusion.1
  690.8 20.4 %gather_fusion.2 = bf16[3072,1024]{1,0:T(8,128)(2,1)} fusion(bf16[4096,1024]{1,0:T(8,128)(2,1)} %bitcast.397, s32[3072]{0:T(1024)S(1)} %copy-done.71), kind=kCustom, calls=%fused_computation.2 | custom fusion | bytes 12595200 | tf_op jit(solution)/shard_map/gather | solution.py:349
  728.1 20.5 %gather_fusion.5 = bf16[3072,1024]{1,0:T(8,128)(2,1)} fusion(bf16[4096,1024]{1,0:T(8,128)(2,1)} %bitcast.398, s32[3072]{0:T(1024)S(1)} %copy-done.71), kind=kCustom, calls=%fused_computation.5 | custom fusion | bytes 12595200 | tf_op jit(solution)/shard_map/gather | solution.py:403
  755.7 19.8 %convolution_convert_fusion = bf16[16,256,1024]{2,1,0:T(8,128)(2,1)} fusion(bf16[1024,16,1024]{2,0,1:T(8,128)(2,1)} %all-gather.23.cloned.1.call-done, bf16[16,256,512]{2,1,0:T(8,128)(2,1)} %get-tuple-element.1446, bf16[16,256,512]{2,1,0:T(8,128)(2,1)} %get-tuple-element.1445), kind=kOutput, calls=%fused_computation.89 | convolution fusion | flops 8610906112 | bytes 50331648 | tf_op jit(solution)/shard_map/yut,jyt->yuj/dot_general | solution.py:120
  775.5 20.6 %gather_fusion.4 = bf16[3072,1024]{1,0:T(8,128)(2,1)} fusion(bf16[4096,1024]{1,0:T(8,128)(2,1)} %bitcast.399, s32[3072]{0:T(1024)S(1)} %copy-done.71), kind=kCustom, calls=%fused_computation.4 | custom fusion | bytes 12595200 | tf_op jit(solution)/shard_map/gather | solution.py:402
  813.9 57.4 %while.59 = (s32[]{:T(128)}, f32[384,8,2,64]{0,3,2,1:T(8,128)S(1)}, bf16[6,512,8,64]{1,3,2,0:T(8,128)(2,1)}, bf16[6,512,8,64]{1,3,2,0:T(8,128)(2,1)}, s32[6]{0:T...) while((s32[]{:T(128)}, f32[384,8,2,64]{0,3,2,1:T(8,128)S(1)}, ...), condition=%wide.region_43.44_spmd.clone, body=%wide.region_40.43_spmd.clone.sunk | while | flops 2043478912 | bytes 68212576 | solution.py:525
  817.3 16.8 %conditional.11 = (f32[384,8,2,64]{0,3,2,1:T(8,128)S(1)}, bf16[1,512,8,64]{1,3,2,0:T(8,128)(2,1)}, bf16[1,512,8,64]{1,3,2,0:T(8,128)(2,1)}) conditional(s32[]{:T(128)} %convert_element_type.487, f32[384,8,2,64]{0,3,2,1:T(8,128)S(1)} %get-tuple-element.1833, (s32[]{:T(128)}, s32[]{:T(128)}, s32[384]{0:T(512)S(1)}, ...), branch_computations={%region_41.41_spmd, %region_42.42_spmd} | conditional | flops 2043478912 | bytes 66113056 | solution.py:520
  879.2 9.3 reshape.1042
  896.9 9.3 reshape.1044
  911.9 154.0 %reduce-scatter.7.cloned.1.call-done = bf16[384,512]{1,0:T(8,128)(2,1)} async-done(((bf16[3072,512]{1,0:T(8,128)(2,1)}), bf16[384,512]{1,0:T(8,128)(2,1)}) %reduce-scatter.7.cloned.1.call-update) | async-done | bytes 393232
  1071.0 45.4 %reduce-scatter.9.cloned.1.call-done = bf16[384,512]{1,0:T(8,128)(2,1)} async-done(((bf16[3072,512]{1,0:T(8,128)(2,1)}), bf16[384,512]{1,0:T(8,128)(2,1)}) %reduce-scatter.9.cloned.1.call-update) | async-done | bytes 393232
  1143.7 60.7 %all-to-all-done.3 = bf16[4,384,1024]{2,1,0:T(8,128)(2,1)} async-done(((bf16[4,384,1024]{2,1,0:T(8,128)(2,1)}), bf16[4,384,1024]{2,1,0:T(8,128)(2,1)}, u32[]{:S(2)}, u32[]{:S(2)}) %all-to-all-start.3) | async-done | bytes 3145760 | tf_op jit(solution)/shard_map/all_to_all | solution.py:595
  1223.2 98.3 %psum.47 = f32[128,16]{0,1:T(8,128)} all-reduce(f32[128,16]{0,1:T(8,128)S(1)} %fusion.157), channel_id=1, replica_groups=mesh['dp'=4,'fsdp'=8] {'dp','fsdp'}, use_global_device_ids=true, to_apply=%region_52.53 | all-reduce | flops 2048 | bytes 16384 | tf_op jit(solution)/shard_map/psum | solution.py:611
  1321.6 109.4 %all-reduce.4.cloned.1.call-done = (f32[7,1024,128]{1,2,0:T(8,128)}, f32[512,128]{1,0:T(8,128)}, f32[3,128,1024]{2,1,0:T(8,128)}, f32[2,128,512]{2,1,0:T(8,128)}, f32[2,128,512]{2,1,0:T(8,128)}) async-done(((f32[7,1024,128]{1,2,0:T(8,128)}, f32[512,128]{1,0:T(8,128)}, f32[3,128,1024]{2,1,0:T(8,128)}, f32[2,128,512]{2,1,0:T(8,128)}, f32[2,128,512]{2,1,0:T(8,128)}), (f32[7,1024,128]{1,2,0:T(8,128)}, ...) | async-done | bytes 6553616 | tf_op jit(solution)/shard_map/psum | solution.py:611
  (506 shorter events, 359.4 us)
Async XLA Ops:
  7.2 523.5 %copy-start = (bf16[512,128]{1,0:T(8,128)(2,1)S(1)}, bf16[512,128]{1,0:T(8,128)(2,1)}, u32[]{:S(2)}) copy-start(bf16[512,128]{1,0:T(8,128)(2,1)} %param.47) | copy-start | bytes 393220
  7.2 109.8 %all-gather.11.cloned.1.call-start = ((), (), s32[]{:S(2)}) async-start(), calls=%async_computation.6 | async-start | bytes 1081344 | tf_op jit(solution)/shard_map/all_gather | solution.py:192
  14.5 94.7 %copy-start.105 = (s32[1,4]{1,0:T(1,128)S(1)}, s32[1,4]{1,0:T(1,128)}, u32[]{:S(2)}) copy-start(s32[1,4]{1,0:T(1,128)} %param.35) | copy-start | bytes 52
  14.5 97.6 %all-to-all-start = ((bf16[4,384,1024]{2,1,0:T(8,128)(2,1)}), bf16[4,384,1024]{2,1,0:T(8,128)(2,1)S(1)}, u32[]{:S(2)}, u32[]{:S(2)}) async-start(bf16[4,384,1024]{2,1,0:T(8,128)(2,1)} %get-tuple-element.1474), calls=%async_computation | async-start | bytes 6291456 | tf_op jit(solution)/shard_map/all_to_all | solution.py:165
  21.0 134.2 %all-gather.17.cloned.1.call-start = ((), (), s32[]{:S(2)}) async-start(), calls=%async_computation.9 | async-start | bytes 1081344 | tf_op jit(solution)/shard_map/all_gather | solution.py:193
  21.7 287.3 %all-gather.15.cloned.1.call-start = ((), (), s32[]{:S(2)}) async-start(), calls=%async_computation.8 | async-start | bytes 2162688 | tf_op jit(solution)/shard_map/all_gather | solution.py:191
  22.4 297.8 %all-gather.13.cloned.1.call-start = ((), (), s32[]{:S(2)}) async-start(), calls=%async_computation.7 | async-start | bytes 3538944 | tf_op jit(solution)/shard_map/all_gather | solution.py:226
  109.3 208.7 %copy-start.81 = (s32[384]{0:T(512)}, s32[384]{0:T(512)S(1)}, u32[]{:S(2)}) copy-start(s32[384]{0:T(512)S(1)} %get-tuple-element.1354) | copy-start | bytes 4612
  110.5 198.5 %copy-start.85 = (f32[1024,1]{0,1:T(1,128)}, f32[1024,1]{0,1:T(1,128)S(1)}, u32[]{:S(2)}) copy-start(f32[1024,1]{0,1:T(1,128)S(1)} %get-tuple-element.1459) | copy-start | bytes 12292
  111.4 203.8 %copy-start.41 = (f32[384,32]{0,1:T(8,128)}, f32[384,32]{0,1:T(8,128)S(1)}, u32[]{:S(2)}) copy-start(f32[384,32]{0,1:T(8,128)S(1)} %get-tuple-element.1462) | copy-start | bytes 147460
  112.1 196.9 %copy-start.14 = (bf16[4,384,1024]{2,1,0:T(8,128)(2,1)}, bf16[4,384,1024]{2,1,0:T(8,128)(2,1)S(1)}, u32[]{:S(2)}) copy-start(bf16[4,384,1024]{2,1,0:T(8,128)(2,1)S(1)} %all-to-all-done) | copy-start | bytes 9437188
  113.2 42.0 %copy-start.91 = (f32[384]{0:T(512)}, f32[384]{0:T(512)S(1)}, u32[]{:S(2)}) copy-start(f32[384]{0:T(512)S(1)} %get-tuple-element.1466) | copy-start | bytes 4612
  124.2 208.9 %all-gather.19.cloned.1.call-start = ((), (), s32[]{:S(2)}) async-start(), calls=%async_computation.10 | async-start | bytes 3538944 | tf_op jit(solution)/shard_map/all_gather | solution.py:227
  158.0 256.3 %all-gather.21.cloned.1.call-start = ((), (), s32[]{:S(2)}) async-start(), calls=%async_computation.11 | async-start | bytes 2162688 | tf_op jit(solution)/shard_map/all_gather | solution.py:194
  158.6 385.3 %all-gather.23.cloned.1.call-start = ((), (), s32[]{:S(2)}) async-start(), calls=%async_computation.12 | async-start | bytes 37748736 | tf_op jit(solution)/shard_map/all_gather | solution.py:201
  164.2 471.5 %all-gather.25.cloned.1.call-start = ((), (), s32[]{:S(2)}) async-start(), calls=%async_computation.13 | async-start | bytes 18874368 | tf_op jit(solution)/shard_map/all_gather | solution.py:202
  167.5 148.0 %all-to-all-start.2 = ((bf16[4,384,1024]{2,1,0:T(8,128)(2,1)}), bf16[4,384,1024]{2,1,0:T(8,128)(2,1)}, u32[]{:S(2)}, u32[]{:S(2)}) async-start(bf16[4,384,1024]{2,1,0:T(8,128)(2,1)} %get-tuple-element.1473), calls=%async_computation.2 | async-start | bytes 6291456 | tf_op jit(solution)/shard_map/all_to_all | solution.py:172
  172.2 893.7 %reduce-scatter.7.cloned.1.call-start = ((), (), s32[]{:S(2)}) async-start(), calls=%async_computation.14 | async-start | bytes 3538944
  279.0 34.2 %copy-start.88 = (s32[3072,1]{0,1:T(1,128)}, s32[3072,1]{0,1:T(1,128)S(1)}, u32[]{:S(2)}) copy-start(s32[3072,1]{0,1:T(1,128)S(1)} %compare_select_fusion.1) | copy-start | bytes 36868
  419.1 84.7 %copy-start.2 = (bf16[384,1024]{1,0:T(8,128)(2,1)}, bf16[384,1024]{1,0:T(8,128)(2,1)S(1)}, u32[]{:S(2)}) copy-start(bf16[384,1024]{1,0:T(8,128)(2,1)S(1)} %multiply_convert_fusion.3) | copy-start | bytes 2359300
  720.0 85.1 %copy-start.53 = (bf16[384,1,128]{2,0,1:T(8,128)(2,1)}, bf16[384,1,128]{2,0,1:T(8,128)(2,1)S(1)}, u32[]{:S(2)}) copy-start(bf16[384,1,128]{2,0,1:T(8,128)(2,1)S(1)} %fusion.85) | copy-start | bytes 294916
  755.7 48.8 %copy-start.30 = (bf16[384,512]{1,0:T(8,128)(2,1)}, bf16[384,512]{1,0:T(8,128)(2,1)S(1)}, u32[]{:S(2)}) copy-start(bf16[384,512]{1,0:T(8,128)(2,1)S(1)} %get-tuple-element.1348) | copy-start | bytes 1179652
  755.7 49.1 %copy-start.31 = (bf16[384,512]{1,0:T(8,128)(2,1)}, bf16[384,512]{1,0:T(8,128)(2,1)S(1)}, u32[]{:S(2)}) copy-start(bf16[384,512]{1,0:T(8,128)(2,1)S(1)} %get-tuple-element.1349) | copy-start | bytes 1179652
  888.5 227.8 %reduce-scatter.9.cloned.1.call-start = ((), (), s32[]{:S(2)}) async-start(), calls=%async_computation.15 | async-start | bytes 3538944
  911.9 157.3 %copy-start.29 = (bf16[1024,512]{1,0:T(8,128)(2,1)S(1)}, bf16[1024,512]{1,0:T(8,128)(2,1)}, u32[]{:S(2)}) copy-start(bf16[1024,512]{1,0:T(8,128)(2,1)} %all-gather.11.cloned.1.call-done) | copy-start | bytes 3145732
  1067.2 49.2 %copy-start.46 = (bf16[2,128,512]{2,1,0:T(8,128)(2,1)S(1)}, bf16[2,128,512]{2,1,0:T(8,128)(2,1)}, u32[]{:S(2)}) copy-start(bf16[2,128,512]{2,1,0:T(8,128)(2,1)} %param.49) | copy-start | bytes 786436
  1069.2 50.5 %copy-start.36 = (bf16[384,128]{1,0:T(8,128)(2,1)S(1)}, bf16[384,128]{1,0:T(8,128)(2,1)}, u32[]{:S(2)}) copy-start(bf16[384,128]{1,0:T(8,128)(2,1)} %get-tuple-element.1463) | copy-start | bytes 294916
  1069.2 50.5 %copy-start.86 = (f32[1024,1]{0,1:T(1,128)S(1)}, f32[1024,1]{0,1:T(1,128)}, u32[]{:S(2)}) copy-start(f32[1024,1]{0,1:T(1,128)} %copy-done.85) | copy-start | bytes 12292
  1071.0 48.8 %copy-start.55 = (bf16[384,1,128]{2,0,1:T(8,128)(2,1)S(1)}, bf16[384,1,128]{2,0,1:T(8,128)(2,1)}, u32[]{:S(2)}) copy-start(bf16[384,1,128]{2,0,1:T(8,128)(2,1)} %fusion.90) | copy-start | bytes 294916
  1128.6 75.9 %all-to-all-start.3 = ((bf16[4,384,1024]{2,1,0:T(8,128)(2,1)}), bf16[4,384,1024]{2,1,0:T(8,128)(2,1)}, u32[]{:S(2)}, u32[]{:S(2)}) async-start(bf16[4,384,1024]{2,1,0:T(8,128)(2,1)} %get-tuple-element.1471), calls=%async_computation.3 | async-start | bytes 6291456 | tf_op jit(solution)/shard_map/all_to_all | solution.py:595
  1204.4 234.1 %all-to-all-start.1 = ((bf16[4,384,1024]{2,1,0:T(8,128)(2,1)}), bf16[4,384,1024]{2,1,0:T(8,128)(2,1)}, u32[]{:S(2)}, u32[]{:S(2)}) async-start(bf16[4,384,1024]{2,1,0:T(8,128)(2,1)} %get-tuple-element.1472), calls=%async_computation.1 | async-start | bytes 6291456 | tf_op jit(solution)/shard_map/all_to_all | solution.py:588
  1209.2 221.7 %all-reduce.4.cloned.1.call-start = ((), (), s32[]{:S(2)}) async-start(), calls=%async_computation.16 | async-start | bytes 13107200 | tf_op jit(solution)/shard_map/psum | solution.py:611
  (94 other events, 515.5 us)
Sparse Core Ops, SparseCore 0:
  10.9 89.6 all-gather.10
  103.5 51.6 all-gather.16
  158.1 96.0 all-gather.14
  256.5 31.9 all-gather.12
  290.8 32.3 all-gather.18
  325.9 56.3 all-gather.20
  384.2 159.6 all-gather.22
  545.8 89.8 all-gather.24
  888.7 177.1 reduce-scatter.6
  1070.1 46.2 reduce-scatter.8
  1221.2 209.7 all-reduce.3
where the time goes:
time: 1460 us; the launch traced here: 1450 us
  waiting for transfers between devices  475 us (33%)
  local copies, waits for them, and re-layouts  300 us (21%)
  blocking collectives  270 us (18%)
  matrix products  192 us (13%)
  other arithmetic  127 us (9%)
  loops' own time  45.3 us (3%)
  starting transfers between devices  21.3 us (1%)
  between operations  19.5 us (1%)
    unnamed x13, waiting for transfers between devices  202 us
    psum x1, waiting for transfers between devices, local(): lax.psum((adapter_input_gradient, down_first_factor_gradient, wide_factor...  109 us
    psum x1, blocking collectives, local(): lax.psum((adapter_input_gradient, down_first_factor_gradient, wide_factor...  98.3 us
    all_gather x1, blocking collectives, local(): lax.all_gather(router_weight, ('dp', 'fsdp'), axis=0, tiled=True)  87.5 us
    all_gather x1, blocking collectives, local(): lax.all_gather(norm_gain_pair, ('dp', 'fsdp'), axis=0, tiled=True)  84.3 us
    unnamed x239, local copies, waits for them, and re-layouts  70.1 us
    all_gather x1, waiting for transfers between devices, local(): lax.all_gather(expert_output_weight, 'fsdp', axis=1, tiled=True)  65.1 us
    all_to_all x1, waiting for transfers between devices, local(): lax.all_to_all(jnp.where(back_mask, input_grad[None], zero_full).astype(j...  60.7 us
  transfers between devices with their start and end apart: 15, of which 7 were waited for; matrix products, arithmetic and copies ran while one was open for 25% of the time, Pallas kernels for 0%

commit v1 on v0

v1 whole, which is shorter than its diff:
```python
import functools

import jax
import jax.numpy as jnp
from jax import lax
from jax.experimental import pallas as pl
from jax.experimental.pallas import tpu as pltpu
from jax.sharding import PartitionSpec as P

MODEL_WIDTH = 1024
HEADS = 16
KEY_VALUE_HEADS = 8
HEAD_WIDTH = 64
HIDDEN_UNITS = 512
TOPK = 8
EXPERT_COUNT = 16
ADAPTER_COUNT = 8
ADAPTER_RANK = 16
STACKED = ADAPTER_COUNT * ADAPTER_RANK

EPSILON = 1e-06
ROPE_BASE = 10000.0
MASKED = -1e30
BLOCK = 256
LANES = 128

BF = jnp.bfloat16
F32 = jnp.float32


def dot(a, b, ca=1, cb=0):
    return lax.dot_general(a, b, (((ca,), (cb,)), ((), ())), preferred_element_type=F32)


def splits(v):
    hi = v.astype(BF).astype(F32)
    rest = v - hi
    mid = rest.astype(BF).astype(F32)
    return hi, mid, rest - mid


def lane_of(shape):
    return lax.broadcasted_iota(jnp.int32, shape, len(shape) - 1)


def row_of(shape):
    return lax.broadcasted_iota(jnp.int32, shape, 0)


def attend_kernel(heads, lens_ref, qkv_ref, out_ref, q_ref, k_ref, v_ref):
    total = qkv_ref.shape[0]
    count = total // BLOCK
    rows = heads * BLOCK
    nseq = lens_ref.shape[1]
    half = HEAD_WIDTH

    def prepare(i, carry):
        at = pl.ds(pl.multiple_of(i * BLOCK, BLOCK), BLOCK)
        low = lane_of((BLOCK, LANES)) < half
        lane = lane_of((BLOCK, LANES))
        row = row_of((BLOCK, LANES)) + i * BLOCK
        first = jnp.int32(0)
        seq = jnp.zeros((BLOCK, LANES), jnp.bool_)
        for s in range(nseq):
            last = first + lens_ref[0, s]
            seq = seq | ((lane == s) & (row >= first) & (row < last))
            first = last
        queries = qkv_ref[at, 0:LANES].astype(F32) * (HEAD_WIDTH ** -0.5)
        pair = qkv_ref[at, LANES : 2 * LANES].astype(F32)
        turned = pltpu.roll(pair, half, 1)
        marks = jnp.where(seq, 1.0, 0.0).astype(BF)
        for h in range(heads):
            mine = jnp.where(low if h == 0 else ~low, queries, 0.0).astype(BF)
            base = pl.ds(pl.multiple_of(i * rows + h * BLOCK, BLOCK), BLOCK)
            q_ref[base, 0:LANES] = mine
            q_ref[base, LANES : 2 * LANES] = marks
        k_ref[at, 0:LANES] = jnp.where(low, pair, turned).astype(BF)
        far = jnp.where(lane < nseq, jnp.where(seq, 0.0, MASKED), 0.0)
        k_ref[at, LANES : 2 * LANES] = jnp.where(
            (lane >= nseq) & (lane < nseq + 3), 1.0, far
        ).astype(BF)
        v_ref[at, 0:LANES] = jnp.where(low, turned, pair).astype(BF)
        v_ref[at, LANES : 2 * LANES] = jnp.ones((BLOCK, LANES), BF)
        return carry

    lax.fori_loop(0, count, prepare, 0)

    def one_block(i, carry):
        at = pl.ds(pl.multiple_of(i * BLOCK, BLOCK), BLOCK)
        base = pl.ds(pl.multiple_of(i * rows, rows), rows)
        first = jnp.int32(0)
        start = jnp.int32(0)
        for s in range(nseq):
            start = jnp.where(i * BLOCK >= first, first, start)
            first = first + lens_ref[0, s]
        queries = q_ref[base, :]

        def step(j, state, diagonal):
            top, acc = state
            here = pl.ds(pl.multiple_of(j * BLOCK, BLOCK), BLOCK)
            scores = dot(queries, k_ref[here, :], 1, 1)
            if diagonal:
                row = jnp.concatenate([row_of((BLOCK, BLOCK))] * heads, axis=0)
                scores = jnp.where(lane_of((rows, BLOCK)) <= row, scores, MASKED)
            new_top = jnp.maximum(top, jnp.max(scores, axis=1, keepdims=True))
            weights = jnp.exp(scores - new_top).astype(BF)
            acc = acc * jnp.exp(top - new_top) + dot(weights, v_ref[here, :])
            return new_top, acc

        state = (jnp.full((rows, 1), MASKED, F32), jnp.zeros((rows, 2 * LANES), F32))
        state = lax.fori_loop(start // BLOCK, i, lambda j, s: step(j, s, False), state)
        top, acc = step(i, state, True)
        weight = acc[:, LANES:]
        mixed = acc[:, :LANES] / weight
        hi, mid, lo = splits(-(top + jnp.log(weight)))
        lane = lane_of((rows, LANES))
        marks = q_ref[base, LANES : 2 * LANES].astype(F32)
        marks = jnp.where(lane == nseq, hi, marks)
        marks = jnp.where(lane == nseq + 1, mid, marks)
        marks = jnp.where(lane == nseq + 2, lo, marks)
        q_ref[base, LANES : 2 * LANES] = marks.astype(BF)
        if heads == 1:
            out_ref[at, :] = mixed.astype(BF)
        else:
            low = lane_of((BLOCK, LANES)) < half
            out_ref[at, :] = jnp.where(low, mixed[:BLOCK], mixed[BLOCK:]).astype(BF)
        return carry

    lax.fori_loop(0, count, one_block, 0)


def attend(lens, qkv, heads):
    total = qkv.shape[0]
    vmem = pl.BlockSpec(memory_space=pltpu.VMEM)
    return pl.pallas_call(
        functools.partial(attend_kernel, heads),
        out_shape=(
            jax.ShapeDtypeStruct((total, LANES), BF),
            jax.ShapeDtypeStruct((heads * total, 2 * LANES), BF),
            jax.ShapeDtypeStruct((total, 2 * LANES), BF),
            jax.ShapeDtypeStruct((total, 2 * LANES), BF),
        ),
        in_specs=[pl.BlockSpec(memory_space=pltpu.SMEM), vmem],
        out_specs=(vmem,) * 4,
        compiler_params=pltpu.CompilerParams(vmem_limit_bytes=48 << 20),
        name="attend",
    )(lens, qkv)


def attend_back_kernel(
    heads, lens_ref, q_ref, k_ref, v_ref, out_ref, grad_ref, back_ref, g_ref, dq_ref
):
    total = out_ref.shape[0]
    count = total // BLOCK
    rows = heads * BLOCK
    nseq = lens_ref.shape[1]
    half = HEAD_WIDTH
    low = lane_of((BLOCK, LANES)) < half
    lane = lane_of((BLOCK, LANES))

    def prepare(i, carry):
        at = pl.ds(pl.multiple_of(i * BLOCK, BLOCK), BLOCK)
        grad = grad_ref[at, :].astype(F32)
        both = grad * out_ref[at, :].astype(F32)
        for h in range(heads):
            part = low if h == 0 else ~low
            delta = jnp.sum(jnp.where(part, both, 0.0), axis=1, keepdims=True)
            hi, mid, lo = splits(-delta)
            extra = jnp.where(lane == 0, hi, jnp.where(lane == 1, mid, jnp.where(lane == 2, lo, 0.0)))
            base = pl.ds(pl.multiple_of(i * rows + h * BLOCK, BLOCK), BLOCK)
            g_ref[base, 0:LANES] = jnp.where(part, grad, 0.0).astype(BF)
            g_ref[base, LANES : 2 * LANES] = extra.astype(BF)
            dq_ref[base, :] = jnp.zeros((BLOCK, LANES), F32)
        return carry

    lax.fori_loop(0, count, prepare, 0)

    def one_block(j, carry):
        here = pl.ds(pl.multiple_of(j * BLOCK, BLOCK), BLOCK)
        final = (j + 1) * BLOCK - 1
        first = jnp.int32(0)
        stop = jnp.int32(0)
        for s in range(nseq):
            last = first + lens_ref[0, s]
            stop = jnp.where(final >= first, last, stop)
            first = last
        keys = k_ref[here, :]
        values = v_ref[here, :]

        def step(i, state, diagonal):
            dk, dv = state
            base = pl.ds(pl.multiple_of(i * rows, rows), rows)
            queries = q_ref[base, :]
            grads = g_ref[base, :]
            weights = jnp.exp(dot(keys, queries, 1, 1))
            if diagonal:
                column = jnp.concatenate([lane_of((BLOCK, BLOCK))] * heads, axis=1)
                weights = jnp.where(row_of((BLOCK, rows)) <= column, weights, 0.0)
            slope = (weights * dot(values, grads, 1, 1)).astype(BF)
            dv = dv + dot(weights.astype(BF), grads[:, :LANES])
            dk = dk + dot(slope, queries[:, :LANES])
            dq_ref[base, :] += dot(slope, keys[:, :LANES], 0, 0)
            return dk, dv

        zero = jnp.zeros((BLOCK, LANES), F32)
        state = step(j, (zero, zero), True)
        dk, dv = lax.fori_loop(
            j + 1, (stop - 1) // BLOCK + 1, lambda i, s: step(i, s, False), state
        )
        back_ref[here, LANES : 2 * LANES] = jnp.where(
            low, dk + pltpu.roll(dk, half, 1), dv + pltpu.roll(dv, half, 1)
        ).astype(BF)
        return carry

    lax.fori_loop(0, count, one_block, 0)

    def finish(i, carry):
        at = pl.ds(pl.multiple_of(i * BLOCK, BLOCK), BLOCK)
        base = pl.multiple_of(i * rows, rows)
        mine = dq_ref[pl.ds(base, BLOCK), :]
        if heads == 2:
            mine = jnp.where(low, mine, dq_ref[pl.ds(base + BLOCK, BLOCK), :])
        back_ref[at, 0:LANES] = (mine * (HEAD_WIDTH ** -0.5)).astype(BF)
        return carry

    lax.fori_loop(0, count, finish, 0)


def attend_back(lens, q, k, v, out, grad, heads):
    total = out.shape[0]
    vmem = pl.BlockSpec(memory_space=pltpu.VMEM)
    return pl.pallas_call(
        functools.partial(attend_back_kernel, heads),
        out_shape=jax.ShapeDtypeStruct((total, 2 * LANES), BF),
        in_specs=[pl.BlockSpec(memory_space=pltpu.SMEM)] + [vmem] * 5,
        out_specs=vmem,
        scratch_shapes=[
            pltpu.VMEM((heads * total, 2 * LANES), BF),
            pltpu.VMEM((heads * total, LANES), F32),
        ],
        compiler_params=pltpu.CompilerParams(vmem_limit_bytes=56 << 20),
        name="attend_back",
    )(lens, q, k, v, out, grad)


def experts_kernel(
    first_expert_ref,
    n2_ref,
    grad_ref,
    mask_ref,
    win_ref,
    wout_ref,
    wide_ref,
    hid_ref,
    down_ref,
    spread_ref,
    fold_ref,
    out_ref,
    back_ref,
    gdown_ref,
    ghid_ref,
):
    local_experts = win_ref.shape[0]
    rows = n2_ref.shape[0]
    width = HIDDEN_UNITS
    step = pl.program_id(0)
    lane = lane_of((rows, LANES))
    n2 = n2_ref[:, :MODEL_WIDTH]
    side = n2_ref[:, MODEL_WIDTH:]
    grad = grad_ref[...]
    mask = mask_ref[...].astype(F32)
    lows = dot(side, spread_ref[...])
    low_gate = (lows[:, :STACKED] * mask).astype(BF)
    low_up = (lows[:, STACKED:] * mask).astype(BF)
    lift_gate = dot(low_gate, hid_ref[0])
    lift_up = dot(low_up, hid_ref[1])
    down_grad = (dot(grad, wide_ref[...], 1, 1) * mask).astype(BF)
    from_down = dot(down_grad, down_ref[...], 1, 1)
    side_full = side.astype(F32)
    total_inner = jnp.zeros((rows, width), F32)
    total_gate = jnp.zeros((rows, width), F32)
    total_up = jnp.zeros((rows, width), F32)
    out = jnp.zeros((rows, MODEL_WIDTH), F32)
    back = jnp.zeros((rows, MODEL_WIDTH), F32)
    extra = jnp.zeros((rows, LANES), F32)
    for e in range(local_experts):
        name = first_expert_ref[0] + e
        at_high, at_low = lane == name, lane == name + EXPERT_COUNT
        gate = jnp.sum(jnp.where(at_high | at_low, side_full, 0.0), axis=1, keepdims=True)
        pre_gate = dot(n2, win_ref[e, :, :width]) + lift_gate
        pre_up = dot(n2, win_ref[e, :, width:]) + lift_up
        pulled = dot(grad, wout_ref[e]) + from_down
        squashed = jax.nn.sigmoid(pre_gate)
        active = pre_gate * squashed
        inner = active * pre_up
        gate_grad = jnp.sum(inner * pulled, axis=1, keepdims=True)
        high = gate_grad.astype(BF).astype(F32)
        extra = extra + jnp.where(at_high, high, 0.0) + jnp.where(at_low, gate_grad - high, 0.0)
        gated = inner * gate
        pulled = pulled * gate
        grad_gate = pulled * pre_up * (squashed + active * (1.0 - squashed))
        grad_up = pulled * active
        gated_low = gated.astype(BF)
        gate_low = grad_gate.astype(BF)
        up_low = grad_up.astype(BF)
        out = out + dot(gated_low, wout_ref[e], 1, 1)
        back = (
            back
            + dot(gate_low, win_ref[e, :, :width], 1, 1)
            + dot(up_low, win_ref[e, :, width:], 1, 1)
        )
        total_inner = total_inner + gated
        total_gate = total_gate + grad_gate
        total_up = total_up + grad_up
    total_inner = total_inner.astype(BF)
    total_gate = total_gate.astype(BF)
    total_up = total_up.astype(BF)
    small = jnp.concatenate(
        [
            (dot(total_gate, hid_ref[0], 1, 1) * mask).astype(BF),
            (dot(total_up, hid_ref[1], 1, 1) * mask).astype(BF),
            (dot(total_inner, down_ref[...]) * mask).astype(BF),
        ],
        axis=1,
    )
    extra = extra + dot(small, fold_ref[...])
    out_ref[...] = out.astype(BF)
    back_ref[:, :MODEL_WIDTH] = back.astype(BF)
    back_ref[:, MODEL_WIDTH:] = extra.astype(BF)
    gdown = dot(total_inner, down_grad, 0, 0)
    ghid_gate = dot(low_gate, total_gate, 0, 0)
    ghid_up = dot(low_up, total_up, 0, 0)

    @pl.when(step == 0)
    def _():
        gdown_ref[...] = gdown
        ghid_ref[0] = ghid_gate
        ghid_ref[1] = ghid_up

    @pl.when(step != 0)
    def _():
        gdown_ref[...] += gdown
        ghid_ref[0] += ghid_gate
        ghid_ref[1] += ghid_up


def experts(first, n2, grad, mask, win, wout, wide, hid, down, rows):
    total = n2.shape[0]
    side = n2.shape[1]
    source = jnp.arange(LANES, dtype=jnp.int32)
    place = jnp.arange(STACKED, dtype=jnp.int32) % ADAPTER_RANK
    spread = jnp.concatenate(
        [(source[:, None] == offset + place[None, :]) for offset in (32, 48)], axis=1
    ).astype(BF)
    fold = jnp.concatenate(
        [(source[None, :] == offset + place[:, None]) for offset in (32, 48, 64)], axis=0
    ).astype(BF)

    def whole(array):
        return pl.BlockSpec(
            array.shape, lambda i: (0,) * array.ndim, pipeline_mode=pl.Buffered(1)
        )

    def block(columns):
        return pl.BlockSpec((rows, columns), lambda i: (i, 0))

    return pl.pallas_call(
        experts_kernel,
        grid=(total // rows,),
        out_shape=(
            jax.ShapeDtypeStruct((total, MODEL_WIDTH), BF),
            jax.ShapeDtypeStruct((total, side), BF),
            jax.ShapeDtypeStruct((HIDDEN_UNITS, STACKED), F32),
            jax.ShapeDtypeStruct((2, STACKED, HIDDEN_UNITS), F32),
        ),
        in_specs=[
            pl.BlockSpec(memory_space=pltpu.SMEM),
            block(side),
            block(MODEL_WIDTH),
            block(STACKED),
            whole(win),
            whole(wout),
            whole(wide),
            whole(hid),
            whole(down),
            whole(spread),
            whole(fold),
        ],
        out_specs=(
            block(MODEL_WIDTH),
            block(side),
            pl.BlockSpec((HIDDEN_UNITS, STACKED), lambda i: (0, 0)),
            pl.BlockSpec((2, STACKED, HIDDEN_UNITS), lambda i: (0, 0, 0)),
        ),
        compiler_params=pltpu.CompilerParams(vmem_limit_bytes=56 << 20),
        name="experts",
    )(first, n2, grad, mask, win, wout, wide, hid, down, spread, fold)


def plane_gather(rows):
    return lax.all_gather(rows, "fsdp", axis=0, tiled=True)


def plane_scatter(rows):
    return lax.psum_scatter(rows, "fsdp", scatter_dimension=0, tiled=True)


def plane_swap(blocks):
    return lax.all_to_all(blocks, "fsdp", split_axis=0, concat_axis=0, tiled=True)


def gather_all(rows):
    return lax.all_gather(rows, ("dp", "fsdp"), axis=0, tiled=True)


def rotate(tensor, cosine, sine):
    rows = tensor.shape[0]
    view = tensor.reshape(rows, -1, 2, HEAD_WIDTH // 2)
    first, second = view[:, :, 0], view[:, :, 1]
    c, s = cosine[:, None, :], sine[:, None, :]
    turned = jnp.stack([first * c - second * s, second * c + first * s], axis=2)
    return turned.reshape(rows, -1)


def local(
    tokens,
    cotangent,
    lengths,
    adapter_index,
    routes,
    deal,
    norm_gain_pair,
    query_weight,
    key_weight,
    value_weight,
    output_weight_transposed,
    router_weight,
    expert_input_weight,
    expert_output_weight,
    factors,
    down_first,
    wide,
    kv_second,
    hidden_second,
    router_second,
):
    shards = lax.axis_size("fsdp")
    groups = lax.axis_size("dp")
    rows = tokens.shape[0]
    total = rows * shards
    heads = HEADS // shards
    share = max(1, shards // KEY_VALUE_HEADS)
    me = lax.axis_index("fsdp")

    group_ids = jnp.arange(groups, dtype=jnp.int32)
    dealt = jnp.sum(jnp.where(deal == lax.axis_index("dp"), group_ids, 0))

    def of_group(array):
        everything = lax.all_gather(array, "dp", axis=0, tiled=False)
        return lax.dynamic_index_in_dim(everything, dealt, 0, keepdims=False)

    lens = of_group(lengths)
    chosen = of_group(adapter_index)[0]
    routes = of_group(routes)

    offsets = jnp.cumsum(lens[0]) - lens[0]
    index = jnp.arange(total, dtype=jnp.int32)
    ends = offsets + lens[0]
    inside = (index[:, None] >= offsets[None, :]) & (index[:, None] < ends[None, :])
    pick = jnp.sum(jnp.where(inside, chosen[None, :], 0), axis=1)
    begin = jnp.sum(jnp.where(inside, offsets[None, :], 0), axis=1)
    group_mask = (
        jnp.arange(STACKED, dtype=jnp.int32)[None, :] // ADAPTER_RANK == pick[:, None]
    ).astype(BF)
    mask_low = lax.dynamic_slice_in_dim(group_mask, me * rows, rows, 0)
    mask = mask_low.astype(F32)
    position = lax.dynamic_slice_in_dim(index - begin, me * rows, rows, 0)
    half = HEAD_WIDTH // 2
    frequency = ROPE_BASE ** (-jnp.arange(half, dtype=F32) / half)
    angles = position.astype(F32)[:, None] * frequency[None, :]
    cosine, sine = jnp.cos(angles), jnp.sin(angles)

    packed = jnp.concatenate(
        [
            query_weight,
            key_weight,
            value_weight,
            output_weight_transposed,
            router_weight,
            norm_gain_pair,
            jnp.zeros((router_weight.shape[0], LANES - EXPERT_COUNT - 2), BF),
        ],
        axis=1,
    )
    packed = gather_all(packed)
    in_width = 2 * MODEL_WIDTH
    in_weight = packed[:, :in_width]
    out_weight = packed[:, in_width : in_width + MODEL_WIDTH]
    router = packed[:, 3 * MODEL_WIDTH : 3 * MODEL_WIDTH + EXPERT_COUNT]
    gains = packed[:, 3 * MODEL_WIDTH + EXPERT_COUNT : 3 * MODEL_WIDTH + EXPERT_COUNT + 2].astype(F32)

    win = jnp.transpose(expert_input_weight, (1, 0, 2))
    wout = jnp.transpose(expert_output_weight, (1, 0, 2))
    all_grad = plane_gather(cotangent)

    x = tokens.astype(F32)
    r1 = lax.rsqrt(jnp.mean(x * x, axis=1, keepdims=True) + EPSILON)
    normed = (x * r1 * gains[:, 0]).astype(BF)
    first_low = [(dot(normed, factors[s]) * mask).astype(BF) for s in range(3)]
    mixed = dot(normed, in_weight)
    query = rotate(mixed[:, :MODEL_WIDTH] + dot(first_low[0], wide[0]), cosine, sine)
    split = MODEL_WIDTH + KEY_VALUE_HEADS * HEAD_WIDTH
    keys = rotate(mixed[:, MODEL_WIDTH:split] + dot(first_low[1], kv_second[0]), cosine, sine)
    values = mixed[:, split:] + dot(first_low[2], kv_second[1])

    def by_head(array, count, repeat):
        array = array.astype(BF).reshape(rows, count, -1).transpose(1, 0, 2)
        return jnp.repeat(array, repeat, axis=0) if repeat > 1 else array

    query = by_head(query, shards, 1)
    if query.shape[2] < LANES:
        query = jnp.pad(query, ((0, 0), (0, 0), (0, LANES - query.shape[2])))
    parts = jnp.concatenate(
        [query, by_head(keys, KEY_VALUE_HEADS, share), by_head(values, KEY_VALUE_HEADS, share)],
        axis=2,
    )
    qkv = plane_swap(parts).reshape(total, -1)
    attended, q_kept, k_kept, v_kept = attend(lens, qkv, heads)

    def home(array, columns):
        swapped = plane_swap(array.reshape(shards, rows, -1))
        return swapped[:, :, :columns].transpose(1, 0, 2).reshape(rows, -1)

    mine = home(attended, heads * HEAD_WIDTH)
    out_low = (dot(mine, factors[6]) * mask).astype(BF)
    hidden = x + dot(mine, out_weight, 1, 1) + dot(out_low, wide[1])
    r2 = lax.rsqrt(jnp.mean(hidden * hidden, axis=1, keepdims=True) + EPSILON)
    normed_two = (hidden * r2 * gains[:, 1]).astype(BF)
    second_low = [(dot(normed_two, factors[3 + s]) * mask).astype(BF) for s in range(3)]
    logits = dot(normed_two, router) + dot(second_low[0], router_second)
    chosen_experts = jnp.sum(
        (routes[:, :, None] == jnp.arange(EXPERT_COUNT, dtype=jnp.int32)).astype(F32), axis=1
    )
    picked = chosen_experts > 0
    peak = jnp.max(jnp.where(picked, logits, MASKED), axis=1, keepdims=True)
    lifted = jnp.where(picked, jnp.exp(logits - peak), 0.0)
    gates = lifted / jnp.sum(lifted, axis=1, keepdims=True)

    def compact(array):
        return jnp.sum(array.astype(F32).reshape(rows, ADAPTER_COUNT, ADAPTER_RANK), axis=1)

    def expand(array):
        return jnp.tile(array, (1, ADAPTER_COUNT))

    gate_high = gates.astype(BF).astype(F32)
    side = jnp.concatenate(
        [
            gate_high,
            gates - gate_high,
            compact(second_low[1]),
            compact(second_low[2]),
            jnp.zeros((rows, LANES - 64), F32),
        ],
        axis=1,
    ).astype(BF)
    everyone = plane_gather(jnp.concatenate([normed_two, side], axis=1))
    local_experts = win.shape[0]
    out_part, back_part, g_down_a, g_ff = experts(
        (me * local_experts).astype(jnp.int32)[None],
        everyone,
        all_grad,
        group_mask,
        win,
        wout,
        wide[2],
        hidden_second,
        down_first,
        rows,
    )
    out_sum = plane_scatter(out_part).astype(F32)
    back_sum = plane_scatter(back_part).astype(F32)

    grad = cotangent.astype(F32)
    extra = back_sum[:, MODEL_WIDTH:]
    gate_grad = extra[:, 0:16] + extra[:, 16:32]
    down_low = (expand(extra[:, 64:80]) * mask).astype(BF)
    layer_out = (hidden + out_sum + dot(down_low, wide[2])).astype(BF)
    g_wide_down = dot(down_low, cotangent, 0, 0)
    logit_grad = (
        gates * (gate_grad - jnp.sum(gates * gate_grad, axis=1, keepdims=True))
    ).astype(BF)
    g_route = dot(second_low[0], logit_grad, 0, 0)
    second_grad = [
        (dot(logit_grad, router_second, 1, 1) * mask).astype(BF),
        (expand(extra[:, 32:48]) * mask).astype(BF),
        (expand(extra[:, 48:64]) * mask).astype(BF),
    ]
    normed_two_grad = back_sum[:, :MODEL_WIDTH] + dot(logit_grad, router, 1, 1)
    for s in range(3):
        normed_two_grad = normed_two_grad + dot(second_grad[s], factors[3 + s], 1, 1)
    g_second = [dot(normed_two, second_grad[s], 0, 0) for s in range(3)]
    w2 = gains[:, 1] * normed_two_grad
    hidden_grad = grad + r2 * w2 - hidden * r2**3 * jnp.mean(w2 * hidden, axis=1, keepdims=True)
    out_grad = hidden_grad.astype(BF)
    g_wide_out = dot(out_low, out_grad, 0, 0)
    out_low_grad = (dot(out_grad, wide[1], 1, 1) * mask).astype(BF)
    g_factor_out = dot(mine, out_low_grad, 0, 0)
    attended_grad = (dot(out_grad, out_weight) + dot(out_low_grad, factors[6], 1, 1)).astype(BF)
    to_heads = by_head(attended_grad, shards, 1)
    if to_heads.shape[2] < LANES:
        to_heads = jnp.pad(to_heads, ((0, 0), (0, 0), (0, LANES - to_heads.shape[2])))
    head_grad = plane_swap(to_heads).reshape(total, -1)
    qkv_grad = attend_back(lens, q_kept, k_kept, v_kept, attended, head_grad, heads)
    qkv_grad = plane_swap(qkv_grad.reshape(shards, rows, -1)).astype(F32)

    def joined(array):
        array = array.reshape(shards // share, share, rows, -1).sum(1)
        return array.transpose(1, 0, 2).reshape(rows, -1)

    query_grad = qkv_grad[:, :, : heads * HEAD_WIDTH].transpose(1, 0, 2).reshape(rows, -1)
    query_grad = rotate(query_grad, cosine, -sine).astype(BF)
    keys_grad = rotate(joined(qkv_grad[:, :, LANES : LANES + 64]), cosine, -sine).astype(BF)
    values_grad = joined(qkv_grad[:, :, LANES + 64 :]).astype(BF)
    mixed_grad = jnp.concatenate([query_grad, keys_grad, values_grad], axis=1)
    normed_grad = dot(mixed_grad, in_weight, 1, 1)
    first_grad = [
        (dot(query_grad, wide[0], 1, 1) * mask).astype(BF),
        (dot(keys_grad, kv_second[0], 1, 1) * mask).astype(BF),
        (dot(values_grad, kv_second[1], 1, 1) * mask).astype(BF),
    ]
    for s in range(3):
        normed_grad = normed_grad + dot(first_grad[s], factors[s], 1, 1)
    g_first = [dot(normed, first_grad[s], 0, 0) for s in range(3)]
    g_wide_query = dot(first_low[0], query_grad, 0, 0)
    g_kv = [dot(first_low[1], keys_grad, 0, 0), dot(first_low[2], values_grad, 0, 0)]
    w1 = gains[:, 0] * normed_grad
    input_grad = hidden_grad + r1 * w1 - x * r1**3 * jnp.mean(w1 * x, axis=1, keepdims=True)

    sums = lax.psum(
        (
            jnp.stack(g_first + g_second + [g_factor_out]),
            g_down_a,
            jnp.stack([g_wide_query, g_wide_out, g_wide_down]),
            jnp.stack(g_kv),
            g_ff,
            g_route,
        ),
        ("dp", "fsdp"),
    )
    return (layer_out, input_grad) + tuple(sums)


def solution(mesh):
    rows = P(("dp", "fsdp"), None)
    placed = (
        (rows, rows, P("dp", None), P("dp", None), rows, P())
        + (rows,) * 6
        + (P(None, "fsdp", None),) * 2
        + (P(),) * 6
    )
    return jax.shard_map(
        local,
        mesh=mesh,
        in_specs=placed,
        out_specs=(rows, rows) + (P(),) * 6,
        check_vma=False,
    )
```

time: 1460 us -> 743 us (0.51)
  local copies, waits for them, and re-layouts: 300 us -> 47 us
  waiting for transfers between devices: 475 us -> 263 us
  Pallas kernels: 0 us -> 164 us
  matrix products: 192 us -> 64.4 us
  blocking collectives: 270 us -> 147 us
  other arithmetic: 127 us -> 18.5 us
  loops' own time: 45.3 us -> 0 us
    unnamed x13 -> x6, waiting for transfers between devices: 202 us -> 0.78 us
    pallas_call x0 -> x3, Pallas kernels: none -> 164 us  [the longest x1 63.7 us: experts(): pl.pallas_call(experts_kernel, grid=(total // rows,), out_shape=(jax.Shap...]
    gather x7 -> x0, local copies, waits for them, and re-layouts: 138 us -> none  [the longest x2 46.2 us: local(): second_lowrank[source, 1:3].reshape(-1, 2 * stacked_width)]
    all_gather x2 -> x3, blocking collectives: 172 us -> 39.1 us  [of_group(): everything = lax.all_gather(array, 'dp', axis=0, tiled=False)]
    dot_general x57 -> x44, matrix products: 192 us -> 64.4 us  [dot(): lax.dot_general(a, b, (((ca,), (cb,)), ((), ())), preferred_element_type=...]
    all_to_all x0 -> x2, blocking collectives: none -> 60.2 us  [plane_swap(): lax.all_to_all(blocks, 'fsdp', split_axis=0, concat_axis=0, tiled=True)]
    reduce_scatter x0 -> x2, waiting for transfers between devices: none -> 53.8 us  [plane_scatter(): return lax.psum_scatter(rows, 'fsdp', scatter_dimension=0, tiled=True)]
    psum x1, blocking collectives: 98.3 us -> 47.5 us  [local(): lax.psum((jnp.stack(g_first + g_second + [g_factor_out]), g_down_a, jnp.s...]
  transfers between devices with their start and end apart: 15 -> 8, of which waited for: 7 -> 5; matrix products, arithmetic and copies ran while one was open for 25% -> 15% of each run, Pallas kernels for 0% -> 13%
where the time goes in v1:
time: 743 us; the launch traced here: 741 us
  waiting for transfers between devices  263 us (35%)
  Pallas kernels  164 us (22%)
  blocking collectives  147 us (20%)
  matrix products  64.4 us (9%)
  local copies, waits for them, and re-layouts  47 us (6%)
  starting transfers between devices  19.9 us (3%)
  other arithmetic  18.5 us (2%)
  between operations  17.4 us (2%)
    psum x1, waiting for transfers between devices, local(): lax.psum((jnp.stack(g_first + g_second + [g_factor_out]), g_down_a, jnp.s...  106 us
    dot_general x44, matrix products, dot(): lax.dot_general(a, b, (((ca,), (cb,)), ((), ())), preferred_element_type=...  64.4 us
    pallas_call x1, Pallas kernels, experts(): pl.pallas_call(experts_kernel, grid=(total // rows,), out_shape=(jax.Shap...  63.7 us
    all_to_all x2, blocking collectives, plane_swap(): lax.all_to_all(blocks, 'fsdp', split_axis=0, concat_axis=0, tiled=True)  60.2 us
    reduce_scatter x2, waiting for transfers between devices, plane_scatter(): return lax.psum_scatter(rows, 'fsdp', scatter_dimension=0, tiled=True)  53.8 us
    pallas_call x1, Pallas kernels, attend_back(): pl.pallas_call(functools.partial(attend_back_kernel, heads), out_shape=ja...  52 us
    pallas_call x1, Pallas kernels, attend(): pl.pallas_call(functools.partial(attend_kernel, heads), out_shape=(jax.Sh...  47.9 us
    psum x1, blocking collectives, local(): lax.psum((jnp.stack(g_first + g_second + [g_factor_out]), g_down_a, jnp.s...  47.5 us
  transfers between devices with their start and end apart: 8, of which 5 were waited for; matrix products, arithmetic and copies ran while one was open for 15% of the time, Pallas kernels for 13%

profile of v1, /device:TPU:0, one launch (start us, length us, event | category | flops | bytes accessed | tf_op | source)
XLA Modules:
  0.0 740.9 jit_solution(2919102342207274263)
XLA Ops:
  11.3 12.7 %all-gather.3 = s32[4,1,4]{2,1,0:T(1,128)S(1)} all-gather(s32[1,1,4]{2,1,0:T(1,128)} %bitcast.239), channel_id=2, replica_groups=mesh['dp'=4,'fsdp'=8] {'dp'}, dimensions={0}, use_global_device_ids=true | all-gather | bytes 80 | tf_op jit(solution)/shard_map/all_gather | solution.py:459
  24.0 7.7 %all-gather.4 = s32[4,1,4]{2,1,0:T(1,128)S(1)} all-gather(s32[1,1,4]{2,1,0:T(1,128)} %bitcast.240), channel_id=3, replica_groups=mesh['dp'=4,'fsdp'=8] {'dp'}, dimensions={0}, use_global_device_ids=true | all-gather | bytes 80 | tf_op jit(solution)/shard_map/all_gather | solution.py:459
  38.6 46.3 %all-gather.9.cloned.1.call-done = bf16[1024,3200]{1,0:T(8,128)(2,1)} async-done(((bf16[32,3200]{1,0:T(8,128)(2,1)}), bf16[1024,3200]{1,0:T(8,128)(2,1)}) %all-gather.9.cloned.1.call-update) | async-done | bytes 6553616 | tf_op jit(solution)/shard_map/all_gather | solution.py:413
  87.9 4.1 fusion.2
  96.2 3.0 slice_add_fusion.1
  99.2 1.9 copy.93
  107.5 39.3 %all_to_all.20 = bf16[8,384,256]{1,2,0:T(8,128)(2,1)} all-to-all(bf16[8,384,256]{1,2,0:T(8,128)(2,1)S(1)} %pad_maximum_fusion), channel_id=1, replica_groups=mesh['dp'=4,'fsdp'=8] {'fsdp'}, dimensions={0} | all-to-all | bytes 3145728 | tf_op jit(solution)/shard_map/all_to_all | solution.py:409
  146.8 1.7 copy.96
  148.5 47.9 %attend.1 = (bf16[3072,128]{1,0:T(8,128)(2,1)S(1)}, bf16[6144,256]{1,0:T(8,128)(2,1)}, bf16[3072,256]{1,0:T(8,128)(2,1)S(1)}, bf16[3072,256]{1,0:T(8,128)(2,1)S(1)}) custom-call(s32[1,4]{1,0:T(1,128)S(1)} %get-tuple-element.57.lens_ref, bf16[3072,256]{1,0:T(8,128)(2,1)S(1)} %bitcast.206), custom_call_target="tpu_custom_call" | custom-call | tf_op jit(solution)/shard_map/attend/pallas_call | solution.py:135
  200.0 3.5 all-to-all-start.1
  203.6 18.7 %all-gather.2 = s32[1536,8]{0,1:T(8,128)S(1)} all-gather(s32[384,8]{0,1:T(8,128)S(1)} %copy-done.63), channel_id=4, replica_groups=mesh['dp'=4,'fsdp'=8] {'dp'}, dimensions={0}, use_global_device_ids=true | all-gather | bytes 61440 | tf_op jit(solution)/shard_map/all_gather | solution.py:459
  225.5 2.9 multiply_reduce_fusion.1
  236.4 1.8 concatenate.23
  238.3 3.4 copy.126
  241.7 3.4 copy.125
  248.3 40.7 %all-gather.11.cloned.1.call-done.n2_ref = bf16[3072,1152]{1,0:T(8,128)(2,1)} async-done(((bf16[384,1152]{1,0:T(8,128)(2,1)}), bf16[3072,1152]{1,0:T(8,128)(2,1)}) %all-gather.11.cloned.1.call-update) | async-done | bytes 7077904 | tf_op jit(solution)/shard_map/all_gather | solution.py:401
  289.0 63.7 %experts.1 = (bf16[3072,1024]{1,0:T(8,128)(2,1)}, bf16[3072,1152]{1,0:T(8,128)(2,1)}, f32[512,128]{1,0:T(8,128)}, f32[2,128,512]{2,1,0:T(8,128)}) custom-call(s32[1]{0:T(128)} %bitcast.28.first_expert_ref, bf16[3072,1152]{1,0:T(8,128)(2,1)} %all-gather.11.cloned.1.call-done.n2_ref, bf16[3072,1024]{1,0:T(8,128)(2,1)} %all-gather.13.cloned.1.call-done.grad_ref, ...), custom_call_target="tpu_custom_call" | custom-call | tf_op jit(solution)/shard_map/experts/pallas_call | solution.py:367
  352.7 11.9 %reduce-scatter.3.cloned.1.call-start = ((), (), s32[]{:S(2)}) async-start(), calls=%async_computation.9 | async-start | bytes 7077888 | tf_op jit(solution)/shard_map/reduce_scatter | solution.py:405
  364.7 53.8 %reduce-scatter.5.cloned.1.call-done = bf16[384,1152]{1,0:T(8,128)(2,1)} async-done(((bf16[3072,1152]{1,0:T(8,128)(2,1)}), bf16[384,1152]{1,0:T(8,128)(2,1)}) %reduce-scatter.5.cloned.1.call-update) | async-done | bytes 884752 | tf_op jit(solution)/shard_map/reduce_scatter | solution.py:405
  428.6 2.7 multiply_reduce_fusion
  435.1 2.8 fusion.28
  438.1 20.8 %all_to_all.21 = bf16[8,384,128]{2,1,0:T(8,128)(2,1)} all-to-all(bf16[8,384,128]{2,1,0:T(8,128)(2,1)S(1)} %bitcast.222), channel_id=1, replica_groups=mesh['dp'=4,'fsdp'=8] {'fsdp'}, dimensions={0} | all-to-all | bytes 1572864 | tf_op jit(solution)/shard_map/all_to_all | solution.py:409
  458.9 52.0 %attend_back.1 = bf16[3072,256]{1,0:T(8,128)(2,1)} custom-call(s32[1,4]{1,0:T(1,128)} %copy-done.5, bf16[6144,256]{1,0:T(8,128)(2,1)} %get-tuple-element.19.q_ref, bf16[3072,256]{1,0:T(8,128)(2,1)} %copy-done.3, bf16[3072,256]{1,0:T(8,128)(2,1)} %copy-done.4, bf16[3072,128]{1,0:T(8,128)(2,1)} %copy-done.2, bf16[3072,128]{1,0:T(8,128)(2,1)} %bitcast.219), custom_call_target="tpu_custom_call" | custom-call | tf_op jit(solution)/shard_map/attend_back/pallas_call | solution.py:232
  510.9 2.6 copy.116
  513.5 4.3 all-to-all-start.3
  519.5 2.4 convolution_bitcast_fusion
  523.0 15.9 %all-to-all-done.3 = bf16[8,384,256]{1,2,0:T(8,128)(2,1)} async-done(((bf16[8,384,256]{1,2,0:T(8,128)(2,1)}), bf16[8,384,256]{1,2,0:T(8,128)(2,1)}, u32[]{:S(2)}, u32[]{:S(2)}) %all-to-all-start.3) | async-done | bytes 1572896 | tf_op jit(solution)/shard_map/all_to_all | solution.py:409
  559.7 47.5 %psum.47 = f32[128,16]{0,1:T(8,128)} all-reduce(f32[128,16]{0,1:T(8,128)S(1)} %fusion.136), channel_id=1, replica_groups=mesh['dp'=4,'fsdp'=8] {'dp','fsdp'}, use_global_device_ids=true, to_apply=%region_21.22 | all-reduce | flops 2048 | bytes 16384 | tf_op jit(solution)/shard_map/psum | solution.py:639
  607.3 2.6 add_convert_fusion.1
  612.8 4.1 fusion
  620.1 105.8 %all-reduce.3.cloned.1.call-done = (f32[7,1024,128]{2,1,0:T(8,128)}, f32[512,128]{1,0:T(8,128)}, f32[3,128,1024]{2,1,0:T(8,128)}, f32[2,128,512]{2,1,0:T(8,128)}, f32[2,128,512]{2,1,0:T(8,128)}) async-done(((f32[7,1024,128]{2,1,0:T(8,128)}, f32[512,128]{1,0:T(8,128)}, f32[3,128,1024]{2,1,0:T(8,128)}, f32[2,128,512]{2,1,0:T(8,128)}, f32[2,128,512]{2,1,0:T(8,128)}), (f32[7,1024,128]{2,1,0:T(8,128)}, ...) | async-done | bytes 6553616 | tf_op jit(solution)/shard_map/psum | solution.py:639
  725.9 4.2 copy.139
  (264 shorter events, 87.4 us)
Async XLA Ops:
  7.2 228.5 %copy-start = (bf16[128,16]{0,1:T(8,128)(2,1)S(1)}, bf16[128,16]{0,1:T(8,128)(2,1)}, u32[]{:S(2)}) copy-start(bf16[128,16]{0,1:T(8,128)(2,1)} %param.39) | copy-start | bytes 12292
  7.2 28.3 %copy-start.12 = (bf16[384,1024]{1,0:T(8,128)(2,1)S(1)}, bf16[384,1024]{1,0:T(8,128)(2,1)}, u32[]{:S(2)}) copy-start(bf16[384,1024]{1,0:T(8,128)(2,1)} %param.20) | copy-start | bytes 2359300
  7.2 77.7 %all-gather.9.cloned.1.call-start = ((), (), s32[]{:S(2)}) async-start(), calls=%async_computation.6 | async-start | bytes 6758400 | tf_op jit(solution)/shard_map/all_gather | solution.py:413
  10.5 237.8 %all-gather.13.cloned.1.call-start = ((), (), s32[]{:S(2)}) async-start(), calls=%async_computation.8 | async-start | bytes 7077888 | tf_op jit(solution)/shard_map/all_gather | solution.py:401
  35.0 113.5 %copy-start.5 = (s32[1,4]{1,0:T(1,128)}, s32[1,4]{1,0:T(1,128)S(1)}, u32[]{:S(2)}) copy-start(s32[1,4]{1,0:T(1,128)S(1)} %get-tuple-element.57.lens_ref) | copy-start | bytes 52
  36.3 57.9 %copy-start.65 = (f32[384]{0:T(512)}, f32[384]{0:T(512)S(1)}, u32[]{:S(2)}) copy-start(f32[384]{0:T(512)S(1)} %get-tuple-element.53) | copy-start | bytes 4612
  38.6 194.4 %copy-start.9 = (bf16[3072,128]{1,0:T(8,128)(2,1)}, bf16[3072,128]{1,0:T(8,128)(2,1)S(1)}, u32[]{:S(2)}) copy-start(bf16[3072,128]{1,0:T(8,128)(2,1)S(1)} %compare_convert_fusion.mask_ref) | copy-start | bytes 2359300
  87.9 4.1 copy-start.58
  87.9 5.8 copy-start.36
  198.8 4.8 copy-start.63
  200.0 22.5 %all-to-all-start.1 = ((bf16[8,384,128]{1,2,0:T(8,128)(2,1)}), bf16[8,384,128]{1,2,0:T(8,128)(2,1)S(1)}, u32[]{:S(2)}, u32[]{:S(2)}) async-start(bf16[8,384,128]{1,2,0:T(8,128)(2,1)} %copy.97), calls=%async_computation.1 | async-start | bytes 1572864 | tf_op jit(solution)/shard_map/all_to_all | solution.py:409
  203.5 85.5 %all-gather.11.cloned.1.call-start = ((), (), s32[]{:S(2)}) async-start(), calls=%async_computation.7 | async-start | bytes 7962624 | tf_op jit(solution)/shard_map/all_gather | solution.py:401
  224.1 4.2 copy-start.53
  234.3 3.9 copy-start.55
  238.2 180.2 %reduce-scatter.5.cloned.1.call-start = ((), (), s32[]{:S(2)}) async-start(), calls=%async_computation.10 | async-start | bytes 7962624 | tf_op jit(solution)/shard_map/reduce_scatter | solution.py:405
  238.3 3.4 copy-start.16
  352.7 254.5 %reduce-scatter.3.cloned.1.call-start = ((), (), s32[]{:S(2)}) async-start(), calls=%async_computation.9 | async-start | bytes 7077888 | tf_op jit(solution)/shard_map/reduce_scatter | solution.py:405
  421.1 3.1 copy-start.10
  422.8 4.4 copy-start.27
  423.0 5.6 copy-start.30
  513.5 25.3 %all-to-all-start.3 = ((bf16[8,384,256]{1,2,0:T(8,128)(2,1)}), bf16[8,384,256]{1,2,0:T(8,128)(2,1)}, u32[]{:S(2)}, u32[]{:S(2)}) async-start(bf16[8,384,256]{1,2,0:T(8,128)(2,1)} %copy.116), calls=%async_computation.5 | async-start | bytes 3145728 | tf_op jit(solution)/shard_map/all_to_all | solution.py:409
  517.8 208.1 %all-reduce.3.cloned.1.call-start = ((), (), s32[]{:S(2)}) async-start(), calls=%async_computation.11 | async-start | bytes 13107200 | tf_op jit(solution)/shard_map/psum | solution.py:639
  519.5 3.5 copy-start.29
  542.5 5.4 copy-start.17
  544.9 3.3 copy-start.22
  547.9 4.5 copy-start.47
  548.2 4.1 copy-start.56
  558.5 48.8 %copy-start.8 = (f32[384,1024]{1,0:T(8,128)S(1)}, f32[384,1024]{1,0:T(8,128)}, u32[]{:S(2)}) copy-start(f32[384,1024]{1,0:T(8,128)} %copy-done.6) | copy-start | bytes 4718596
  612.8 4.1 copy-start.15
  612.8 4.1 copy-start.48
  725.9 4.3 copy-start.60
  725.9 5.0 copy-start.32
  (43 other events, 79.5 us)
Sparse Core Ops, SparseCore 0:
  11.4 73.3 all-gather.8
  86.8 59.6 all-gather.12
  238.3 50.6 all-gather.10
  352.9 65.5 reduce-scatter.4
  422.0 66.4 reduce-scatter.2
  558.6 167.2 all-reduce.2

commit v2 on v1

--- a/solution.py
+++ b/solution.py
@@ -1,4 +1,5 @@
 import functools
+import math
 
 import jax
 import jax.numpy as jnp
@@ -26,6 +27,7 @@
 
 BF = jnp.bfloat16
 F32 = jnp.float32
+MESH = pl.DeviceIdType.MESH
 
 
 def dot(a, b, ca=1, cb=0):
@@ -397,20 +399,327 @@
     )(first, n2, grad, mask, win, wout, wide, hid, down, spread, fold)
 
 
-def plane_gather(rows):
-    return lax.all_gather(rows, "fsdp", axis=0, tiled=True)
-
-
-def plane_scatter(rows):
-    return lax.psum_scatter(rows, "fsdp", scatter_dimension=0, tiled=True)
-
-
-def plane_swap(blocks):
-    return lax.all_to_all(blocks, "fsdp", split_axis=0, concat_axis=0, tiled=True)
-
-
-def gather_all(rows):
-    return lax.all_gather(rows, ("dp", "fsdp"), axis=0, tiled=True)
+def bits_of(count):
+    return [1 << k for k in range(count.bit_length() - 1)]
+
+
+def orders_of(count):
+    bits = bits_of(count)
+    far = bits[1:]
+    cut = (len(far) + 1) // 2
+    return (far + bits[:1], far[cut:] + far[:cut] + bits[:1])
+
+
+def span(bits):
+    masks = [0]
+    for bit in bits:
+        masks = masks + [m ^ bit for m in masks]
+    return masks
+
+
+def greet(meetings):
+    barrier = pltpu.get_barrier_semaphore()
+    count = 0
+    for axis, me, masks in meetings:
+        for mask in masks:
+            pl.semaphore_signal(
+                barrier, inc=1, device_id={axis: me ^ mask}, device_id_type=MESH
+            )
+            count += 1
+    pl.semaphore_wait(barrier, count)
+
+
+class Gather:
+    def __init__(self, axis, count, own, store, sems):
+        self.axis, self.count, self.own, self.store = axis, count, own, store
+        self.sends, self.recvs = sems
+        self.me = lax.axis_index(axis)
+        self.orders = orders_of(count)
+        self.half = store.shape[1] // 2
+
+    def copy(self, h, mask, bit):
+        rows = pl.ds(h * self.half, self.half)
+        there = self.store.at[self.me ^ mask, rows]
+        return pltpu.make_async_remote_copy(
+            src_ref=self.own.at[rows] if mask == 0 else there,
+            dst_ref=there,
+            send_sem=self.sends.at[h, mask ^ bit],
+            recv_sem=self.recvs.at[h, mask ^ bit],
+            device_id={self.axis: self.me ^ bit},
+            device_id_type=MESH,
+        )
+
+    def incoming(self, h, mask):
+        there = self.store.at[self.me ^ mask, pl.ds(h * self.half, self.half)]
+        return pltpu.make_async_remote_copy(
+            src_ref=there,
+            dst_ref=there,
+            send_sem=self.sends.at[h, mask],
+            recv_sem=self.recvs.at[h, mask],
+            device_id={self.axis: self.me ^ mask},
+            device_id_type=MESH,
+        )
+
+    def start(self):
+        for k in range(len(self.orders[0])):
+            for h in range(2):
+                self.copy(h, 0, self.orders[h][k]).start()
+
+    def stage(self, k):
+        for s in range(1 << k):
+            for h in range(2):
+                order = self.orders[h]
+                mask = order[k] ^ span(order[:k])[s]
+                self.incoming(h, mask).wait_recv()
+                for bit in order[k + 1 :]:
+                    self.copy(h, mask, bit).start()
+
+    def stages(self):
+        for k in range(len(self.orders[0])):
+            self.stage(k)
+
+    def finish(self):
+        for h in range(2):
+            for mask in range(1, self.count):
+                self.incoming(h, mask).wait_send()
+
+
+class Scatter:
+    def __init__(self, axis, count, part, land, sems):
+        self.axis, self.count, self.part, self.land = axis, count, part, land
+        self.sends, self.recvs = sems
+        self.me = lax.axis_index(axis)
+        self.orders = [order[::-1] for order in orders_of(count)]
+        self.half = part.shape[1] // 2
+
+    def depth(self, h, mask):
+        for k, bit in enumerate(self.orders[h]):
+            if mask & bit:
+                return k
+        return len(self.orders[h])
+
+    def copy(self, h, mask):
+        bit = self.orders[h][self.depth(h, mask)]
+        return pltpu.make_async_remote_copy(
+            src_ref=self.part.at[self.me ^ mask, pl.ds(h * self.half, self.half)],
+            dst_ref=self.land.at[h, mask],
+            send_sem=self.sends.at[h, mask],
+            recv_sem=self.recvs.at[h, mask],
+            device_id={self.axis: self.me ^ bit},
+            device_id_type=MESH,
+        )
+
+    def reduce(self, h, mask):
+        depth = self.depth(h, mask)
+        sources = [mask ^ bit for bit in self.orders[h][:depth]]
+        for source in sources:
+            self.copy(h, source).wait_recv()
+        if sources:
+            step = math.gcd(self.half, 64)
+            mine = self.me ^ mask
+
+            def add(c, carry):
+                here = pl.ds(pl.multiple_of(c * step, step), step)
+                at = pl.ds(pl.multiple_of(h * self.half + c * step, step), step)
+                total = self.part[mine, at].astype(F32)
+                for source in sources:
+                    total = total + self.land[h, source, here].astype(F32)
+                self.part[mine, at] = total.astype(BF)
+                return carry
+
+            lax.fori_loop(0, self.half // step, add, 0)
+        if mask:
+            self.copy(h, mask).start()
+
+    def run(self):
+        for k in range(len(self.orders[0]) + 1):
+            for mask in range(self.count):
+                for h in range(2):
+                    if self.depth(h, mask) == k:
+                        self.reduce(h, mask)
+
+    def finish(self):
+        for h in range(2):
+            for mask in range(1, self.count):
+                self.copy(h, mask).wait_send()
+
+
+def pair_of_sems(count):
+    return [pltpu.SemaphoreType.DMA((2, count)), pltpu.SemaphoreType.DMA((2, count))]
+
+
+ANYWHERE = pl.BlockSpec(memory_space=pl.ANY)
+IN_VMEM = pl.BlockSpec(memory_space=pltpu.VMEM)
+
+
+def remote(identity, limit=48):
+    return pltpu.CompilerParams(
+        collective_id=identity, has_side_effects=True, vmem_limit_bytes=limit << 20
+    )
+
+
+def gather_kernel(axis, count, own, store, sends, recvs, local_sem):
+    me = lax.axis_index(axis)
+    keep = pltpu.make_async_copy(own, store.at[me], local_sem)
+    keep.start()
+    greet([(axis, me, bits_of(count))])
+    moving = Gather(axis, count, own, store, (sends, recvs))
+    moving.start()
+    moving.stages()
+    moving.finish()
+    keep.wait()
+
+
+def gather(rows, axis, identity):
+    count = lax.axis_size(axis)
+    return pl.pallas_call(
+        functools.partial(gather_kernel, axis, count),
+        out_shape=jax.ShapeDtypeStruct((count,) + rows.shape, rows.dtype),
+        in_specs=[IN_VMEM],
+        out_specs=IN_VMEM,
+        scratch_shapes=pair_of_sems(count) + [pltpu.SemaphoreType.DMA(())],
+        compiler_params=remote(identity),
+        name="gather",
+    )(rows)
+
+
+def scatter_kernel(axis, count, given, total, part, land, sends, recvs, local_sem):
+    me = lax.axis_index(axis)
+    take = pltpu.make_async_copy(given, part, local_sem)
+    take.start()
+    greet([(axis, me, bits_of(count))])
+    moving = Scatter(axis, count, part, land, (sends, recvs))
+    take.wait()
+    moving.run()
+    total[...] = part[me]
+    moving.finish()
+
+
+def scatter(blocks, axis, identity):
+    count, rows, columns = blocks.shape
+    return pl.pallas_call(
+        functools.partial(scatter_kernel, axis, count),
+        out_shape=jax.ShapeDtypeStruct((rows, columns), BF),
+        in_specs=[ANYWHERE],
+        out_specs=IN_VMEM,
+        scratch_shapes=[
+            pltpu.VMEM(blocks.shape, BF),
+            pltpu.VMEM((2, count, rows // 2, columns), BF),
+        ]
+        + pair_of_sems(count)
+        + [pltpu.SemaphoreType.DMA(())],
+        compiler_params=remote(identity, 56),
+        name="scatter",
+    )(blocks)
+
+
+def swap_kernel(axis, count, given, taken, sends, recvs, local_sem):
+    me = lax.axis_index(axis)
+    keep = pltpu.make_async_copy(given.at[me], taken.at[me], local_sem)
+    keep.start()
+    greet([(axis, me, range(1, count))])
+
+    def copy(mask):
+        return pltpu.make_async_remote_copy(
+            src_ref=given.at[me ^ mask],
+            dst_ref=taken.at[me],
+            send_sem=sends.at[mask],
+            recv_sem=recvs.at[mask],
+            device_id={axis: me ^ mask},
+            device_id_type=MESH,
+        )
+
+    for mask in range(count - 1, 0, -1):
+        copy(mask).start()
+    for mask in range(1, count):
+        copy(mask).wait()
+    keep.wait()
+
+
+def swap(blocks, axis, identity):
+    count = lax.axis_size(axis)
+    return pl.pallas_call(
+        functools.partial(swap_kernel, axis, count),
+        out_shape=jax.ShapeDtypeStruct(blocks.shape, blocks.dtype),
+        in_specs=[IN_VMEM],
+        out_specs=IN_VMEM,
+        scratch_shapes=[pltpu.SemaphoreType.DMA((count,))] * 2 + [pltpu.SemaphoreType.DMA(())],
+        compiler_params=remote(identity),
+        name="swap",
+    )(blocks)
+
+
+def total_kernel(
+    shards, groups, given, out, part, land, zpart, zland, zall, s1, r1, s2, r2, s3, r3, s4, r4, sem
+):
+    me, plane = lax.axis_index("fsdp"), lax.axis_index("dp")
+    take = pltpu.make_async_copy(given, part, sem)
+    take.start()
+    greet([("fsdp", me, bits_of(shards)), ("dp", plane, bits_of(groups))])
+    take.wait()
+    down = Scatter("fsdp", shards, part, land, (s1, r1))
+    down.run()
+    piece = zpart.shape[1]
+    for g in range(groups):
+        zpart[g] = part[me, pl.ds(g * piece, piece)]
+    across = Scatter("dp", groups, zpart, zland, (s2, r2))
+    across.run()
+    zall[plane] = zpart[plane]
+    back = Gather("dp", groups, zall.at[plane], zall, (s3, r3))
+    back.start()
+    back.stages()
+    for g in range(groups):
+        out[me, pl.ds(g * piece, piece)] = zall[g]
+    up = Gather("fsdp", shards, out.at[me], out, (s4, r4))
+    up.start()
+    up.stages()
+    down.finish()
+    across.finish()
+    back.finish()
+    up.finish()
+
+
+def total_of(rows, identity):
+    shards, groups = lax.axis_size("fsdp"), lax.axis_size("dp")
+    unit = shards * groups * 2 * 16
+    length = -(-rows.shape[0] // unit) * unit
+    rows = jnp.pad(rows, ((0, length - rows.shape[0]), (0, 0)))
+    share = length // shards
+    piece = share // groups
+    columns = rows.shape[1]
+    out = pl.pallas_call(
+        functools.partial(total_kernel, shards, groups),
+        out_shape=jax.ShapeDtypeStruct((shards, share, columns), BF),
+        in_specs=[ANYWHERE],
+        out_specs=IN_VMEM,
+        scratch_shapes=[
+            pltpu.VMEM((shards, share, columns), BF),
+            pltpu.VMEM((2, shards, share // 2, columns), BF),
+            pltpu.VMEM((groups, piece, columns), BF),
+            pltpu.VMEM((2, groups, piece // 2, columns), BF),
+            pltpu.VMEM((groups, piece, columns), BF),
+        ]
+        + pair_of_sems(shards)
+        + pair_of_sems(groups) * 2
+        + pair_of_sems(shards)
+        + [pltpu.SemaphoreType.DMA(())],
+        compiler_params=remote(identity),
+        name="total",
+    )(rows.reshape(shards, share, columns))
+    return out.reshape(length, columns)
+
+
+def plane_gather(rows, identity):
+    return gather(rows, "fsdp", identity).reshape(-1, rows.shape[1])
+
+
+def plane_scatter(rows, identity):
+    count = lax.axis_size("fsdp")
+    return scatter(rows.reshape(count, -1, rows.shape[1]), "fsdp", identity)
+
+
+def plane_swap(blocks, identity):
+    return swap(blocks, "fsdp", identity)
 
 
 def rotate(tensor, cosine, sine):
@@ -492,7 +801,11 @@
         ],
         axis=1,
     )
-    packed = gather_all(packed)
+    packed = gather(packed, "dp", 1).reshape(-1, packed.shape[1])
+    packed = gather(packed, "fsdp", 2)
+    small = packed.shape[1] // groups
+    packed = packed.reshape(shards, groups, small, -1).transpose(1, 0, 2, 3)
+    packed = packed.reshape(MODEL_WIDTH, -1)
     in_width = 2 * MODEL_WIDTH
     in_weight = packed[:, :in_width]
     out_weight = packed[:, in_width : in_width + MODEL_WIDTH]
@@ -501,7 +814,7 @@
 
     win = jnp.transpose(expert_input_weight, (1, 0, 2))
     wout = jnp.transpose(expert_output_weight, (1, 0, 2))
-    all_grad = plane_gather(cotangent)
+    all_grad = plane_gather(cotangent, 3)
 
     x = tokens.astype(F32)
     r1 = lax.rsqrt(jnp.mean(x * x, axis=1, keepdims=True) + EPSILON)
@@ -524,11 +837,11 @@
         [query, by_head(keys, KEY_VALUE_HEADS, share), by_head(values, KEY_VALUE_HEADS, share)],
         axis=2,
     )
-    qkv = plane_swap(parts).reshape(total, -1)
+    qkv = plane_swap(parts, 4).reshape(total, -1)
     attended, q_kept, k_kept, v_kept = attend(lens, qkv, heads)
 
     def home(array, columns):
-        swapped = plane_swap(array.reshape(shards, rows, -1))
+        swapped = plane_swap(array.reshape(shards, rows, -1), 5)
         return swapped[:, :, :columns].transpose(1, 0, 2).reshape(rows, -1)
 
     mine = home(attended, heads * HEAD_WIDTH)
@@ -563,7 +876,7 @@
         ],
         axis=1,
     ).astype(BF)
-    everyone = plane_gather(jnp.concatenate([normed_two, side], axis=1))
+    everyone = plane_gather(jnp.concatenate([normed_two, side], axis=1), 6)
     local_experts = win.shape[0]
     out_part, back_part, g_down_a, g_ff = experts(
         (me * local_experts).astype(jnp.int32)[None],
@@ -577,8 +890,8 @@
         down_first,
         rows,
     )
-    out_sum = plane_scatter(out_part).astype(F32)
-    back_sum = plane_scatter(back_part).astype(F32)
+    out_sum = plane_scatter(out_part, 7).astype(F32)
+    back_sum = plane_scatter(back_part, 8).astype(F32)
 
     grad = cotangent.astype(F32)
     extra = back_sum[:, MODEL_WIDTH:]
@@ -609,9 +922,9 @@
     to_heads = by_head(attended_grad, shards, 1)
     if to_heads.shape[2] < LANES:
         to_heads = jnp.pad(to_heads, ((0, 0), (0, 0), (0, LANES - to_heads.shape[2])))
-    head_grad = plane_swap(to_heads).reshape(total, -1)
+    head_grad = plane_swap(to_heads, 9).reshape(total, -1)
     qkv_grad = attend_back(lens, q_kept, k_kept, v_kept, attended, head_grad, heads)
-    qkv_grad = plane_swap(qkv_grad.reshape(shards, rows, -1)).astype(F32)
+    qkv_grad = plane_swap(qkv_grad.reshape(shards, rows, -1), 10).astype(F32)
 
     def joined(array):
         array = array.reshape(shards // share, share, rows, -1).sum(1)
@@ -636,18 +949,41 @@
     w1 = gains[:, 0] * normed_grad
     input_grad = hidden_grad + r1 * w1 - x * r1**3 * jnp.mean(w1 * x, axis=1, keepdims=True)
 
-    sums = lax.psum(
-        (
-            jnp.stack(g_first + g_second + [g_factor_out]),
-            g_down_a,
-            jnp.stack([g_wide_query, g_wide_out, g_wide_down]),
-            jnp.stack(g_kv),
-            g_ff,
-            g_route,
-        ),
-        ("dp", "fsdp"),
+    def tall(array):
+        return [array[:, c : c + LANES] for c in range(0, array.shape[1], LANES)]
+
+    pieces = g_first + g_second + [g_factor_out, g_down_a]
+    for array in [g_wide_query, g_wide_out, g_wide_down] + g_kv + [g_ff[0], g_ff[1]]:
+        pieces = pieces + tall(array)
+    pieces = pieces + [jnp.pad(g_route, ((0, 0), (0, LANES - EXPERT_COUNT)))]
+    sums = total_of(jnp.concatenate([p.astype(BF) for p in pieces], axis=0), 11).astype(F32)
+
+    def wide_sum(start, count, parts):
+        block = sums[start : start + count * parts * STACKED]
+        block = block.reshape(count, parts, STACKED, LANES).transpose(0, 2, 1, 3)
+        return block.reshape(count, STACKED, parts * LANES)
+
+    edge = 7 * MODEL_WIDTH
+    factor_sum = sums[:edge].reshape(7, MODEL_WIDTH, STACKED)
+    down_sum = sums[edge : edge + HIDDEN_UNITS]
+    edge += HIDDEN_UNITS
+    wide_total = wide_sum(edge, 3, 8)
+    edge += 24 * STACKED
+    kv_total = wide_sum(edge, 2, 4)
+    edge += 8 * STACKED
+    ff_total = wide_sum(edge, 2, 4)
+    edge += 8 * STACKED
+    route_total = sums[edge : edge + STACKED, :EXPERT_COUNT]
+    return (
+        layer_out,
+        input_grad,
+        factor_sum,
+        down_sum,
+        wide_total,
+        kv_total,
+        ff_total,
+        route_total,
     )
-    return (layer_out, input_grad) + tuple(sums)
 
 
 def solution(mesh):

time: 743 us -> 702 us (0.945); the launches traced: 741 us -> 692 us
  Pallas kernels: 164 us -> 494 us
  waiting for transfers between devices: 263 us -> 0 us
  blocking collectives: 147 us -> 33.7 us
  local copies, waits for them, and re-layouts: 47 us -> 82.1 us
  starting transfers between devices: 19.9 us -> 0 us
  between operations: 17.4 us -> 4.38 us
    pallas_call x0 -> x11, Pallas kernels: none -> 318 us  [the longest x4 116 us: gather(): pl.pallas_call(functools.partial(gather_kernel, axis, count), out_shape=j...]
    psum x1 -> x0, waiting for transfers between devices: 106 us -> none  [local(): lax.psum((jnp.stack(g_first + g_second + [g_factor_out]), g_down_a, jnp.s...]
    all_gather x3 -> x0, waiting for transfers between devices: 87.1 us -> none  [the longest x1 46.3 us: gather_all(): return lax.all_gather(rows, ('dp', 'fsdp'), axis=0, tiled=True)]
    all_to_all x2 -> x0, blocking collectives: 60.2 us -> none  [plane_swap(): lax.all_to_all(blocks, 'fsdp', split_axis=0, concat_axis=0, tiled=True)]
    reduce_scatter x2 -> x0, waiting for transfers between devices: 53.8 us -> none  [plane_scatter(): return lax.psum_scatter(rows, 'fsdp', scatter_dimension=0, tiled=True)]
    psum x1 -> x0, blocking collectives: 47.5 us -> none  [local(): lax.psum((jnp.stack(g_first + g_second + [g_factor_out]), g_down_a, jnp.s...]
    all_to_all x2 -> x0, waiting for transfers between devices: 15.9 us -> none  [plane_swap(): lax.all_to_all(blocks, 'fsdp', split_axis=0, concat_axis=0, tiled=True)]
    reduce_scatter x2 -> x0, starting transfers between devices: 11.9 us -> none  [plane_scatter(): return lax.psum_scatter(rows, 'fsdp', scatter_dimension=0, tiled=True)]
  transfers between devices with their start and end apart: 8 -> 0, of which waited for: 5 -> 0; matrix products, arithmetic and copies ran while one was open for 15% -> 0% of each run, Pallas kernels for 13% -> 0%
where the time goes in v2:
time: 702 us; the launch traced here: 692 us
  Pallas kernels  494 us (70%)
  local copies, waits for them, and re-layouts  82.1 us (12%)
  matrix products  58.2 us (8%)
  blocking collectives  33.7 us (5%)
  other arithmetic  19.6 us (3%)
    pallas_call x4, Pallas kernels, gather(): pl.pallas_call(functools.partial(gather_kernel, axis, count), out_shape=j...  116 us
    pallas_call x2, Pallas kernels, scatter(): pl.pallas_call(functools.partial(scatter_kernel, axis, count), out_shape=...  78.4 us
    pallas_call x4, Pallas kernels, swap(): pl.pallas_call(functools.partial(swap_kernel, axis, count), out_shape=jax...  66.6 us
    pallas_call x1, Pallas kernels, experts(): pl.pallas_call(experts_kernel, grid=(total // rows,), out_shape=(jax.Shap...  63.7 us
    pallas_call x1, Pallas kernels, attend_back(): pl.pallas_call(functools.partial(attend_back_kernel, heads), out_shape=ja...  58.5 us
    dot_general x44, matrix products, dot(): lax.dot_general(a, b, (((ca,), (cb,)), ((), ())), preferred_element_type=...  58.2 us
    pallas_call x1, Pallas kernels, total_of(): pl.pallas_call(functools.partial(total_kernel, shards, groups), out_shape...  57.2 us
    pallas_call x1, Pallas kernels, attend(): pl.pallas_call(functools.partial(attend_kernel, heads), out_shape=(jax.Sh...  53.8 us

profile of v2, /device:TPU:0, one launch (start us, length us, event | category | flops | bytes accessed | tf_op | source)
XLA Modules:
  0.0 691.9 jit_solution(17838442832005749394)
XLA Ops:
  4.0 12.7 %all-gather.3 = s32[4,1,4]{2,1,0:T(1,128)S(1)} all-gather(s32[1,1,4]{2,1,0:T(1,128)} %bitcast.249), channel_id=2, replica_groups=mesh['dp'=4,'fsdp'=8] {'dp'}, dimensions={0}, use_global_device_ids=true | all-gather | bytes 80 | tf_op jit(solution)/shard_map/all_gather | solution.py:768
  16.9 7.7 %all-gather.4 = s32[4,1,4]{2,1,0:T(1,128)S(1)} all-gather(s32[1,1,4]{2,1,0:T(1,128)} %bitcast.250), channel_id=3, replica_groups=mesh['dp'=4,'fsdp'=8] {'dp'}, dimensions={0}, use_global_device_ids=true | all-gather | bytes 80 | tf_op jit(solution)/shard_map/all_gather | solution.py:768
  29.9 13.3 %all-gather.2 = s32[1536,8]{0,1:T(8,128)S(1)} all-gather(s32[384,8]{0,1:T(8,128)} %param.24), channel_id=4, replica_groups=mesh['dp'=4,'fsdp'=8] {'dp'}, dimensions={0}, use_global_device_ids=true | all-gather | bytes 61440 | tf_op jit(solution)/shard_map/all_gather | solution.py:768
  46.7 11.4 %gather.4 = bf16[4,32,3200]{2,1,0:T(8,128)(2,1)S(1)} custom-call(bf16[32,3200]{1,0:T(8,128)(2,1)S(1)} %concatenate.24.own), custom_call_target="tpu_custom_call" | custom-call | tf_op jit(solution)/shard_map/gather/pallas_call | solution.py:575
  59.5 3.5 copy.201
  63.1 3.4 copy.200
  66.4 34.3 %gather.5 = bf16[8,128,3200]{2,1,0:T(8,128)(2,1)} custom-call(bf16[128,3200]{1,0:T(8,128)(2,1)S(1)} %bitcast.192), custom_call_target="tpu_custom_call" | custom-call | tf_op jit(solution)/shard_map/gather/pallas_call | solution.py:575
  100.7 3.5 copy.154
  106.5 2.1 fusion.37
  115.2 2.3 convolution_add_fusion.1
  117.5 2.9 slice_add_fusion.1
  127.1 21.3 %swap.4 = bf16[8,384,256]{2,1,0:T(8,128)(2,1)S(1)} custom-call(bf16[8,384,256]{2,1,0:T(8,128)(2,1)S(1)} %pad_maximum_fusion.given), custom_call_target="tpu_custom_call" | custom-call | tf_op jit(solution)/shard_map/swap/pallas_call | solution.py:641
  148.4 53.8 %attend.1 = (bf16[3072,128]{1,0:T(8,128)(2,1)S(1)}, bf16[6144,256]{1,0:T(8,128)(2,1)}, bf16[3072,256]{1,0:T(8,128)(2,1)S(1)}, bf16[3072,256]{1,0:T(8,128)(2,1)S(1)}) custom-call(s32[1,4]{1,0:T(1,128)S(1)} %get-tuple-element.56.lens_ref, bf16[3072,256]{1,0:T(8,128)(2,1)S(1)} %bitcast.191), custom_call_target="tpu_custom_call" | custom-call | tf_op jit(solution)/shard_map/attend/pallas_call | solution.py:137
  204.5 12.1 %swap.5 = bf16[8,384,128]{2,1,0:T(8,128)(2,1)S(1)} custom-call(bf16[8,384,128]{2,1,0:T(8,128)(2,1)S(1)} %bitcast.193), custom_call_target="tpu_custom_call" | custom-call | tf_op jit(solution)/shard_map/swap/pallas_call | solution.py:641
  221.4 2.9 multiply_reduce_fusion.1
  232.9 36.7 %gather.6 = bf16[8,384,1152]{2,1,0:T(8,128)(2,1)} custom-call(bf16[384,1152]{1,0:T(8,128)(2,1)S(1)} %concatenate.26.own), custom_call_target="tpu_custom_call" | custom-call | tf_op jit(solution)/shard_map/gather/pallas_call | solution.py:575
  269.6 33.2 %gather.7 = bf16[8,384,1024]{2,1,0:T(8,128)(2,1)} custom-call(bf16[384,1024]{1,0:T(8,128)(2,1)S(1)} %copy-done.2), custom_call_target="tpu_custom_call" | custom-call | tf_op jit(solution)/shard_map/gather/pallas_call | solution.py:575
  302.8 63.7 %experts.1 = (bf16[3072,1024]{1,0:T(8,128)(2,1)}, bf16[3072,1152]{1,0:T(8,128)(2,1)}, f32[512,128]{1,0:T(8,128)}, f32[2,128,512]{2,1,0:T(8,128)}) custom-call(s32[1]{0:T(128)} %bitcast.32.first_expert_ref, bf16[3072,1152]{1,0:T(8,128)(2,1)} %bitcast.197, bf16[3072,1024]{1,0:T(8,128)(2,1)} %bitcast.200, bf16[3072,128]{1,0:T(8,128)(2,1)} %copy-done.18, ...), custom_call_target="tpu_custom_call" | custom-call | tf_op jit(solution)/shard_map/experts/pallas_call | solution.py:369
  366.6 37.4 %scatter.2 = bf16[384,1024]{1,0:T(8,128)(2,1)} custom-call(bf16[8,384,1024]{2,1,0:T(8,128)(2,1)} %bitcast.212), custom_call_target="tpu_custom_call" | custom-call | tf_op jit(solution)/shard_map/scatter/pallas_call | solution.py:600
  403.9 41.1 %scatter.3 = bf16[384,1152]{1,0:T(8,128)(2,1)} custom-call(bf16[8,384,1152]{2,1,0:T(8,128)(2,1)} %bitcast.211), custom_call_target="tpu_custom_call" | custom-call | tf_op jit(solution)/shard_map/scatter/pallas_call | solution.py:600
  454.2 2.5 add_convert_fusion.1
  477.6 2.6 add_convert_fusion
  482.9 12.5 %swap.6 = bf16[8,384,128]{2,1,0:T(8,128)(2,1)S(1)} custom-call(bf16[8,384,128]{2,1,0:T(8,128)(2,1)S(1)} %bitcast.195), custom_call_target="tpu_custom_call" | custom-call | tf_op jit(solution)/shard_map/swap/pallas_call | solution.py:641
  496.3 58.5 %attend_back.1 = bf16[3072,256]{1,0:T(8,128)(2,1)} custom-call(s32[1,4]{1,0:T(1,128)} %copy-done.8, bf16[6144,256]{1,0:T(8,128)(2,1)} %get-tuple-element.19.q_ref, bf16[3072,256]{1,0:T(8,128)(2,1)} %copy-done.6, bf16[3072,256]{1,0:T(8,128)(2,1)} %copy-done.7, bf16[3072,128]{1,0:T(8,128)(2,1)} %copy-done.4, bf16[3072,128]{1,0:T(8,128)(2,1)} %bitcast.194), custom_call_target="tpu_custom_call" | custom-call | tf_op jit(solution)/shard_map/attend_back/pallas_call | solution.py:234
  556.2 20.7 %swap.7 = bf16[8,384,256]{2,1,0:T(8,128)(2,1)S(1)} custom-call(bf16[8,384,256]{2,1,0:T(8,128)(2,1)S(1)} %bitcast.190), custom_call_target="tpu_custom_call" | custom-call | tf_op jit(solution)/shard_map/swap/pallas_call | solution.py:641
  585.3 2.7 slice_bitcast_fusion
  589.2 2.7 copy.182
  594.0 3.0 copy.181
  598.8 4.1 fusion
  618.1 57.2 %total.1 = bf16[8,1664,128]{2,1,0:T(8,128)(2,1)S(1)} custom-call(bf16[8,1664,128]{2,1,0:T(8,128)(2,1)} %bitcast.202), custom_call_target="tpu_custom_call" | custom-call | tf_op jit(solution)/shard_map/total/pallas_call | solution.py:690
  676.0 2.8 copy-done.9
  685.1 4.2 slice.470
  (314 shorter events, 114.8 us)
Async XLA Ops:
  0.6 231.0 %copy-start = (bf16[128,16]{0,1:T(8,128)(2,1)S(1)}, bf16[128,16]{0,1:T(8,128)(2,1)}, u32[]{:S(2)}) copy-start(bf16[128,16]{0,1:T(8,128)(2,1)} %param.39) | copy-start | bytes 12292
  0.6 45.3 %copy-start.30 = (bf16[3,128,1024]{2,1,0:T(8,128)(2,1)S(1)}, bf16[3,128,1024]{2,1,0:T(8,128)(2,1)}, u32[]{:S(2)}) copy-start(bf16[3,128,1024]{2,1,0:T(8,128)(2,1)} %param.36) | copy-start | bytes 2359300
  16.7 131.7 %copy-start.8 = (s32[1,4]{1,0:T(1,128)}, s32[1,4]{1,0:T(1,128)S(1)}, u32[]{:S(2)}) copy-start(s32[1,4]{1,0:T(1,128)S(1)} %get-tuple-element.56.lens_ref) | copy-start | bytes 52
  26.6 83.3 %copy-start.66 = (f32[384]{0:T(512)}, f32[384]{0:T(512)S(1)}, u32[]{:S(2)}) copy-start(f32[384]{0:T(512)S(1)} %get-tuple-element.52) | copy-start | bytes 4612
  59.5 169.2 %copy-start.18 = (bf16[3072,128]{1,0:T(8,128)(2,1)}, bf16[3072,128]{1,0:T(8,128)(2,1)S(1)}, u32[]{:S(2)}) copy-start(bf16[3072,128]{1,0:T(8,128)(2,1)S(1)} %compare_convert_fusion.mask_ref) | copy-start | bytes 2359300
  59.5 3.6 copy-start.22
  100.7 4.1 copy-start.20
  104.2 5.7 copy-start.15
  104.9 5.1 copy-start.64
  106.5 11.0 %copy-start.52 = (bf16[384,128]{1,0:T(8,128)(2,1)}, bf16[384,128]{1,0:T(8,128)(2,1)S(1)}, u32[]{:S(2)}) copy-start(bf16[384,128]{1,0:T(8,128)(2,1)S(1)} %fusion.36) | copy-start | bytes 294916
  110.0 3.6 copy-start.39
  204.5 15.0 %copy-start.4 = (bf16[3072,128]{1,0:T(8,128)(2,1)}, bf16[3072,128]{1,0:T(8,128)(2,1)S(1)}, u32[]{:S(2)}) copy-start(bf16[3072,128]{1,0:T(8,128)(2,1)S(1)} %get-tuple-element.16.out_ref) | copy-start | bytes 2359300
  217.8 3.6 copy-start.26
  226.9 4.7 copy-start.55
  227.0 4.7 copy-start.46
  232.9 36.7 %copy-start.2 = (bf16[384,1024]{1,0:T(8,128)(2,1)S(1)}, bf16[384,1024]{1,0:T(8,128)(2,1)}, u32[]{:S(2)}) copy-start(bf16[384,1024]{1,0:T(8,128)(2,1)} %own.1) | copy-start | bytes 2359300
  403.9 41.1 %copy-start.61 = (f32[2,128,512]{2,1,0:T(8,128)S(1)}, f32[2,128,512]{2,1,0:T(8,128)}, u32[]{:S(2)}) copy-start(f32[2,128,512]{2,1,0:T(8,128)} %get-tuple-element.23) | copy-start | bytes 1572868
  445.0 9.1 %copy-start.11 = (f32[384,1024]{1,0:T(8,128)S(1)}, f32[384,1024]{1,0:T(8,128)}, u32[]{:S(2)}) copy-start(f32[384,1024]{1,0:T(8,128)} %copy-done.10) | copy-start | bytes 4718596
  454.2 4.5 copy-start.63
  460.4 10.6 %copy-start.32 = (f32[384,128]{1,0:T(8,128)}, f32[384,128]{1,0:T(8,128)S(1)}, u32[]{:S(2)}) copy-start(f32[384,128]{1,0:T(8,128)S(1)} %copy.176) | copy-start | bytes 589828
  463.6 3.4 copy-start.56
  467.9 2.7 copy-start.31
  578.8 4.6 copy-start.19
  581.4 6.5 copy-start.14
  598.7 4.1 copy-start.54
  598.8 4.4 copy-start.40
  605.2 2.8 copy-start.21
  605.3 2.8 copy-start.51
  605.3 2.8 copy-start.65
  676.0 2.8 copy-start.9
  685.1 4.2 slice-start
  689.4 2.3 copy-start.1
  (39 other events, 57.9 us)

commit v3 on v2

v3 whole, which is shorter than its diff:
```python
import functools
import math

import jax
import jax.numpy as jnp
import numpy as np
from jax import lax
from jax.experimental import pallas as pl
from jax.experimental.pallas import tpu as pltpu
from jax.sharding import PartitionSpec as P

MODEL_WIDTH = 1024
HEADS = 16
KEY_VALUE_HEADS = 8
HEAD_WIDTH = 64
HIDDEN_UNITS = 512
TOPK = 8
EXPERT_COUNT = 16
ADAPTER_COUNT = 8
ADAPTER_RANK = 16
STACKED = ADAPTER_COUNT * ADAPTER_RANK

EPSILON = 1e-06
ROPE_BASE = 10000.0
MASKED = -1e30
LANES = 128

BF = jnp.bfloat16
F32 = jnp.float32
MESH = pl.DeviceIdType.MESH


def dot(a, b, ca=1, cb=0):
    return lax.dot_general(a, b, (((ca,), (cb,)), ((), ())), preferred_element_type=F32)


def splits(v):
    hi = v.astype(BF).astype(F32)
    rest = v - hi
    mid = rest.astype(BF).astype(F32)
    return hi, mid, rest - mid


def lane_of(shape):
    return lax.broadcasted_iota(jnp.int32, shape, len(shape) - 1)


def row_of(shape):
    return lax.broadcasted_iota(jnp.int32, shape, 0)


def attend_kernel(heads, lens_ref, qkv_ref, out_ref, q_ref, k_ref, v_ref):
    total = qkv_ref.shape[0]
    nseq = lens_ref.shape[1]
    half = HEAD_WIDTH
    side = 256

    def prepare(i, carry):
        at = pl.ds(pl.multiple_of(i * side, side), side)
        low = lane_of((side, LANES)) < half
        lane = lane_of((side, LANES))
        row = row_of((side, LANES)) + i * side
        first = jnp.int32(0)
        seq = jnp.zeros((side, LANES), jnp.bool_)
        for s in range(nseq):
            last = first + lens_ref[0, s]
            seq = seq | ((lane == s) & (row >= first) & (row < last))
            first = last
        queries = qkv_ref[at, 0:LANES].astype(F32) * (HEAD_WIDTH ** -0.5)
        pair = qkv_ref[at, LANES : 2 * LANES].astype(F32)
        swapped = pltpu.roll(pair, half, 1)
        marks = jnp.where(seq, 1.0, 0.0).astype(BF)
        for h in range(heads):
            mine = jnp.where(low if h == 0 else ~low, queries, 0.0).astype(BF)
            q_ref[h, at, 0:LANES] = mine
            q_ref[h, at, LANES : 2 * LANES] = marks
        k_ref[at, 0:LANES] = jnp.where(low, pair, swapped).astype(BF)
        far = jnp.where(lane < nseq, jnp.where(seq, 0.0, MASKED), 0.0)
        k_ref[at, LANES : 2 * LANES] = jnp.where(
            (lane >= nseq) & (lane < nseq + 3), 1.0, far
        ).astype(BF)
        v_ref[at, 0:LANES] = jnp.where(low, swapped, pair).astype(BF)
        v_ref[at, LANES : 2 * LANES] = jnp.ones((side, LANES), BF)
        return carry

    lax.fori_loop(0, total // side, prepare, 0)

    rows = math.gcd(total, 384)
    block = rows
    low = lane_of((rows, LANES)) < half
    lane = lane_of((rows, LANES))
    for i in range(total // block):
        keys = (i + 1) * block

        def chunk(c, carry, i=i, keys=keys):
            first = i * block + c * rows
            at = pl.ds(pl.multiple_of(first, rows), rows)
            visible = lane_of((rows, block)) <= row_of((rows, block)) + c * rows
            mixed = []
            for h in range(heads):
                scores = dot(q_ref[h, at, :], k_ref[0:keys, :], 1, 1)
                final = jnp.where(visible, scores[:, keys - block :], MASKED)
                if i:
                    scores = jnp.concatenate([scores[:, : keys - block], final], axis=1)
                else:
                    scores = final
                top = jnp.max(scores, axis=1, keepdims=True)
                weights = jnp.exp(scores - top).astype(BF)
                acc = dot(weights, v_ref[0:keys, :])
                weight = acc[:, LANES:]
                mixed.append(acc[:, :LANES] / weight)
                hi, mid, lo = splits(-(top + jnp.log(weight)))
                marks = q_ref[h, at, LANES : 2 * LANES].astype(F32)
                marks = jnp.where(lane == nseq, hi, marks)
                marks = jnp.where(lane == nseq + 1, mid, marks)
                marks = jnp.where(lane == nseq + 2, lo, marks)
                q_ref[h, at, LANES : 2 * LANES] = marks.astype(BF)
            value = mixed[0] if heads == 1 else jnp.where(low, mixed[0], mixed[1])
            out_ref[at, :] = value.astype(BF)
            return carry

        lax.fori_loop(0, block // rows, chunk, 0)


def attend(lens, qkv, heads):
    total = qkv.shape[0]
    vmem = pl.BlockSpec(memory_space=pltpu.VMEM)
    return pl.pallas_call(
        functools.partial(attend_kernel, heads),
        out_shape=(
            jax.ShapeDtypeStruct((total, LANES), BF),
            jax.ShapeDtypeStruct((heads, total, 2 * LANES), BF),
            jax.ShapeDtypeStruct((total, 2 * LANES), BF),
            jax.ShapeDtypeStruct((total, 2 * LANES), BF),
        ),
        in_specs=[pl.BlockSpec(memory_space=pltpu.SMEM), vmem],
        out_specs=(vmem,) * 4,
        compiler_params=pltpu.CompilerParams(vmem_limit_bytes=56 << 20),
        name="attend",
    )(lens, qkv)


def attend_back_kernel(
    heads, lens_ref, q_ref, k_ref, v_ref, out_ref, grad_ref, back_ref, g_ref, dq_ref, dk_ref, dv_ref
):
    total = out_ref.shape[0]
    half = HEAD_WIDTH
    side = 256
    low = lane_of((side, LANES)) < half
    lane = lane_of((side, LANES))

    def prepare(i, carry):
        at = pl.ds(pl.multiple_of(i * side, side), side)
        grad = grad_ref[at, :].astype(F32)
        both = grad * out_ref[at, :].astype(F32)
        for h in range(heads):
            part = low if h == 0 else ~low
            delta = jnp.sum(jnp.where(part, both, 0.0), axis=1, keepdims=True)
            hi, mid, lo = splits(-delta)
            extra = jnp.where(lane == 0, hi, jnp.where(lane == 1, mid, jnp.where(lane == 2, lo, 0.0)))
            g_ref[h, at, 0:LANES] = jnp.where(part, grad, 0.0).astype(BF)
            g_ref[h, at, LANES : 2 * LANES] = extra.astype(BF)
            dq_ref[h, at, :] = jnp.zeros((side, LANES), F32)
        return carry

    lax.fori_loop(0, total // side, prepare, 0)
    cols = 256
    block = total
    count = 1

    def one_block(j, carry):
        here = pl.ds(pl.multiple_of(j * block, block), block)
        dk_ref[...] = jnp.zeros(dk_ref.shape, F32)
        dv_ref[...] = jnp.zeros(dv_ref.shape, F32)

        def step(i, state, diagonal):
            for h in range(heads):
                for c in range(block // cols):
                    at = pl.ds(pl.multiple_of(i * block + c * cols, cols), cols)
                    size = (c + 1) * cols if diagonal else block
                    mine = pl.ds(pl.multiple_of(j * block, block), size)
                    keys = k_ref[mine, :]
                    queries = q_ref[h, at, :]
                    grads = g_ref[h, at, :]
                    weights = jnp.exp(dot(keys, queries, 1, 1))
                    if diagonal:
                        seen = row_of((size, cols)) <= lane_of((size, cols)) + c * cols
                        weights = jnp.where(seen, weights, 0.0)
                    slope = (weights * dot(v_ref[mine, :], grads, 1, 1)).astype(BF)
                    dv_ref[:size, :] += dot(weights.astype(BF), grads[:, :LANES])
                    dk_ref[:size, :] += dot(slope, queries[:, :LANES])
                    dq_ref[h, at, :] += dot(slope, keys[:, :LANES], 0, 0)
            return state

        step(j, 0, True)
        lax.fori_loop(j + 1, count, lambda i, s: step(i, s, False), 0)
        dk, dv = dk_ref[...], dv_ref[...]
        back_ref[here, LANES : 2 * LANES] = jnp.where(
            lane_of((block, LANES)) < half, dk + pltpu.roll(dk, half, 1), dv + pltpu.roll(dv, half, 1)
        ).astype(BF)
        return carry

    lax.fori_loop(0, count, one_block, 0)

    def finish(i, carry):
        at = pl.ds(pl.multiple_of(i * side, side), side)
        mine = dq_ref[0, at, :]
        if heads == 2:
            mine = jnp.where(low, mine, dq_ref[1, at, :])
        back_ref[at, 0:LANES] = (mine * (HEAD_WIDTH ** -0.5)).astype(BF)
        return carry

    lax.fori_loop(0, total // side, finish, 0)


def attend_back(lens, q, k, v, out, grad, heads):
    total = out.shape[0]
    vmem = pl.BlockSpec(memory_space=pltpu.VMEM)
    return pl.pallas_call(
        functools.partial(attend_back_kernel, heads),
        out_shape=jax.ShapeDtypeStruct((total, 2 * LANES), BF),
        in_specs=[pl.BlockSpec(memory_space=pltpu.SMEM)] + [vmem] * 5,
        out_specs=vmem,
        scratch_shapes=[
            pltpu.VMEM((heads, total, 2 * LANES), BF),
            pltpu.VMEM((heads, total, LANES), F32),
            pltpu.VMEM((total, LANES), F32),
            pltpu.VMEM((total, LANES), F32),
        ],
        compiler_params=pltpu.CompilerParams(vmem_limit_bytes=56 << 20),
        name="attend_back",
    )(lens, q, k, v, out, grad)


def bits_of(count):
    return [1 << k for k in range(count.bit_length() - 1)]


def orders_of(count):
    bits = bits_of(count)
    far = bits[1:]
    cut = (len(far) + 1) // 2
    return (far + bits[:1], far[cut:] + far[:cut] + bits[:1])


def span(bits):
    masks = [0]
    for bit in bits:
        masks = masks + [m ^ bit for m in masks]
    return masks


def greet(meetings):
    barrier = pltpu.get_barrier_semaphore()
    count = 0
    for axis, me, masks in meetings:
        for mask in masks:
            pl.semaphore_signal(
                barrier, inc=1, device_id={axis: me ^ mask}, device_id_type=MESH
            )
            count += 1
    pl.semaphore_wait(barrier, count)


class Gather:
    def __init__(self, axis, count, own, store, sems):
        self.axis, self.count, self.own, self.store = axis, count, own, store
        self.sends, self.recvs = sems
        self.me = lax.axis_index(axis)
        self.orders = orders_of(count)
        self.half = store.shape[1] // 2

    def copy(self, h, mask, bit):
        rows = pl.ds(h * self.half, self.half)
        there = self.store.at[self.me ^ mask, rows]
        return pltpu.make_async_remote_copy(
            src_ref=self.own.at[rows] if mask == 0 else there,
            dst_ref=there,
            send_sem=self.sends.at[h, mask ^ bit],
            recv_sem=self.recvs.at[h, mask ^ bit],
            device_id={self.axis: self.me ^ bit},
            device_id_type=MESH,
        )

    def incoming(self, h, mask):
        there = self.store.at[self.me ^ mask, pl.ds(h * self.half, self.half)]
        return pltpu.make_async_remote_copy(
            src_ref=there,
            dst_ref=there,
            send_sem=self.sends.at[h, mask],
            recv_sem=self.recvs.at[h, mask],
            device_id={self.axis: self.me ^ mask},
            device_id_type=MESH,
        )

    def start(self):
        for k in range(len(self.orders[0])):
            for h in range(2):
                self.copy(h, 0, self.orders[h][k]).start()

    def take(self, h, mask):
        order = self.orders[h]
        self.incoming(h, mask).wait_recv()
        k = max(i for i, bit in enumerate(order) if mask & bit)
        for bit in order[k + 1 :]:
            self.copy(h, mask, bit).start()

    def stage(self, k):
        for s in range(1 << k):
            for h in range(2):
                order = self.orders[h]
                mask = order[k] ^ span(order[:k])[s]
                self.incoming(h, mask).wait_recv()
                for bit in order[k + 1 :]:
                    self.copy(h, mask, bit).start()

    def held(self, k):
        sets = [set(span(order[: k + 1])) for order in self.orders]
        return sets[0] & sets[1]

    def stages(self):
        for k in range(len(self.orders[0])):
            self.stage(k)

    def finish(self):
        for h in range(2):
            for mask in range(1, self.count):
                self.incoming(h, mask).wait_send()


class Scatter:
    def __init__(self, axis, count, part, land, sems):
        self.axis, self.count, self.part, self.land = axis, count, part, land
        self.sends, self.recvs = sems
        self.me = lax.axis_index(axis)
        self.orders = [order[::-1] for order in orders_of(count)]
        self.half = part.shape[1] // 2

    def depth(self, h, mask):
        for k, bit in enumerate(self.orders[h]):
            if mask & bit:
                return k
        return len(self.orders[h])

    def copy(self, h, mask):
        bit = self.orders[h][self.depth(h, mask)]
        return pltpu.make_async_remote_copy(
            src_ref=self.part.at[self.me ^ mask, pl.ds(h * self.half, self.half)],
            dst_ref=self.land.at[h, mask - 1],
            send_sem=self.sends.at[h, mask],
            recv_sem=self.recvs.at[h, mask],
            device_id={self.axis: self.me ^ bit},
            device_id_type=MESH,
        )

    def reduce(self, h, mask):
        depth = self.depth(h, mask)
        sources = [mask ^ bit for bit in self.orders[h][:depth]]
        for source in sources:
            self.copy(h, source).wait_recv()
        if sources:
            step = math.gcd(self.half, 64)
            mine = self.me ^ mask

            def add(c, carry):
                here = pl.ds(pl.multiple_of(c * step, step), step)
                at = pl.ds(pl.multiple_of(h * self.half + c * step, step), step)
                total = self.part[mine, at].astype(F32)
                for source in sources:
                    total = total + self.land[h, source - 1, here].astype(F32)
                self.part[mine, at] = total.astype(BF)
                return carry

            lax.fori_loop(0, self.half // step, add, 0)
        if mask:
            self.copy(h, mask).start()

    def run(self):
        for k in range(len(self.orders[0]) + 1):
            for mask in range(self.count):
                for h in range(2):
                    if self.depth(h, mask) == k:
                        self.reduce(h, mask)

    def finish(self):
        for h in range(2):
            for mask in range(1, self.count):
                self.copy(h, mask).wait_send()


def pair_of_sems(count):
    return [pltpu.SemaphoreType.DMA((2, count)), pltpu.SemaphoreType.DMA((2, count))]


ANYWHERE = pl.BlockSpec(memory_space=pl.ANY)
IN_VMEM = pl.BlockSpec(memory_space=pltpu.VMEM)


def remote(identity, limit=48):
    return pltpu.CompilerParams(
        collective_id=identity, has_side_effects=True, vmem_limit_bytes=limit << 20
    )


def gather_kernel(axis, count, own, store, sends, recvs, local_sem):
    me = lax.axis_index(axis)
    keep = pltpu.make_async_copy(own, store.at[me], local_sem)
    keep.start()
    greet([(axis, me, bits_of(count))])
    moving = Gather(axis, count, own, store, (sends, recvs))
    moving.start()
    moving.stages()
    moving.finish()
    keep.wait()


def gather(rows, axis, identity):
    count = lax.axis_size(axis)
    return pl.pallas_call(
        functools.partial(gather_kernel, axis, count),
        out_shape=jax.ShapeDtypeStruct((count,) + rows.shape, rows.dtype),
        in_specs=[IN_VMEM],
        out_specs=IN_VMEM,
        scratch_shapes=pair_of_sems(count) + [pltpu.SemaphoreType.DMA(())],
        compiler_params=remote(identity),
        name="gather",
    )(rows)


def scatter_kernel(axis, count, given, total, part, land, sends, recvs, local_sem):
    me = lax.axis_index(axis)
    take = pltpu.make_async_copy(given, part, local_sem)
    take.start()
    greet([(axis, me, bits_of(count))])
    moving = Scatter(axis, count, part, land, (sends, recvs))
    take.wait()
    moving.run()
    total[...] = part[me]
    moving.finish()


def scatter(blocks, axis, identity):
    count, rows, columns = blocks.shape
    return pl.pallas_call(
        functools.partial(scatter_kernel, axis, count),
        out_shape=jax.ShapeDtypeStruct((rows, columns), BF),
        in_specs=[ANYWHERE],
        out_specs=IN_VMEM,
        scratch_shapes=[
            pltpu.VMEM(blocks.shape, BF),
            pltpu.VMEM((2, count - 1, rows // 2, columns), BF),
        ]
        + pair_of_sems(count)
        + [pltpu.SemaphoreType.DMA(())],
        compiler_params=remote(identity, 56),
        name="scatter",
    )(blocks)


def swap_kernel(axis, count, given, taken, sends, recvs, local_sem):
    me = lax.axis_index(axis)
    keep = pltpu.make_async_copy(given.at[me], taken.at[me], local_sem)
    keep.start()
    greet([(axis, me, range(1, count))])

    def copy(mask):
        return pltpu.make_async_remote_copy(
            src_ref=given.at[me ^ mask],
            dst_ref=taken.at[me],
            send_sem=sends.at[mask],
            recv_sem=recvs.at[mask],
            device_id={axis: me ^ mask},
            device_id_type=MESH,
        )

    for mask in range(count - 1, 0, -1):
        copy(mask).start()
    for mask in range(1, count):
        copy(mask).wait()
    keep.wait()


def swap(blocks, axis, identity):
    count = lax.axis_size(axis)
    return pl.pallas_call(
        functools.partial(swap_kernel, axis, count),
        out_shape=jax.ShapeDtypeStruct(blocks.shape, blocks.dtype),
        in_specs=[IN_VMEM],
        out_specs=IN_VMEM,
        scratch_shapes=[pltpu.SemaphoreType.DMA((count,))] * 2 + [pltpu.SemaphoreType.DMA(())],
        compiler_params=remote(identity),
        name="swap",
    )(blocks)


def total_kernel(
    shards, groups, given, out, part, land, zpart, zland, zall, s1, r1, s2, r2, s3, r3, s4, r4, sem
):
    me, plane = lax.axis_index("fsdp"), lax.axis_index("dp")
    take = pltpu.make_async_copy(given, part, sem)
    take.start()
    greet([("fsdp", me, bits_of(shards)), ("dp", plane, bits_of(groups))])
    take.wait()
    down = Scatter("fsdp", shards, part, land, (s1, r1))
    down.run()
    piece = zpart.shape[1]
    for g in range(groups):
        zpart[g] = part[me, pl.ds(g * piece, piece)]
    across = Scatter("dp", groups, zpart, zland, (s2, r2))
    across.run()
    zall[plane] = zpart[plane]
    back = Gather("dp", groups, zall.at[plane], zall, (s3, r3))
    back.start()
    back.stages()
    for g in range(groups):
        out[me, pl.ds(g * piece, piece)] = zall[g]
    up = Gather("fsdp", shards, out.at[me], out, (s4, r4))
    up.start()
    up.stages()
    down.finish()
    across.finish()
    back.finish()
    up.finish()


def total_of(rows, identity):
    shards, groups = lax.axis_size("fsdp"), lax.axis_size("dp")
    unit = shards * groups * 2 * 16
    length = -(-rows.shape[0] // unit) * unit
    rows = jnp.pad(rows, ((0, length - rows.shape[0]), (0, 0)))
    share = length // shards
    piece = share // groups
    columns = rows.shape[1]
    out = pl.pallas_call(
        functools.partial(total_kernel, shards, groups),
        out_shape=jax.ShapeDtypeStruct((shards, share, columns), BF),
        in_specs=[ANYWHERE],
        out_specs=IN_VMEM,
        scratch_shapes=[
            pltpu.VMEM((shards, share, columns), BF),
            pltpu.VMEM((2, shards - 1, share // 2, columns), BF),
            pltpu.VMEM((groups, piece, columns), BF),
            pltpu.VMEM((2, groups - 1, piece // 2, columns), BF),
            pltpu.VMEM((groups, piece, columns), BF),
        ]
        + pair_of_sems(shards)
        + pair_of_sems(groups) * 2
        + pair_of_sems(shards)
        + [pltpu.SemaphoreType.DMA(())],
        compiler_params=remote(identity),
        name="total",
    )(rows.reshape(shards, share, columns))
    return out.reshape(length, columns)


def plane_gather(rows, identity):
    return gather(rows, "fsdp", identity).reshape(-1, rows.shape[1])


def plane_scatter(rows, identity):
    count = lax.axis_size("fsdp")
    return scatter(rows.reshape(count, -1, rows.shape[1]), "fsdp", identity)


def plane_swap(blocks, identity):
    return swap(blocks, "fsdp", identity)


def sequences(meta, first, rows, heads_of):
    row = row_of((rows, LANES)) + first
    start = jnp.zeros((1, 1), jnp.int32)
    picked = [jnp.zeros((rows, LANES), part[0].dtype) for part in heads_of]
    for s in range(len(heads_of[0])):
        inside = row >= start
        picked = [jnp.where(inside, part[s], value) for part, value in zip(heads_of, picked)]
        start = start + meta[8:9, s : s + 1]
    return picked


def turned(tensor, cosine, sine):
    lower = lane_of(tensor.shape) % HEAD_WIDTH < HEAD_WIDTH // 2
    other = jnp.where(lower, pltpu.roll(tensor, LANES - 32, 1), pltpu.roll(tensor, 32, 1))
    return tensor * cosine + other * sine


def head_columns(wide, narrow, pick_wide, pick_narrow, heads):
    low = lane_of((1, LANES)) < HEAD_WIDTH
    queries = wide
    if heads == 1:
        queries = jnp.where(low, jnp.where(pick_wide, pltpu.roll(wide, HEAD_WIDTH, 1), wide), 0.0)
    keys, values = narrow
    keys = jnp.where(pick_narrow, pltpu.roll(keys, HEAD_WIDTH, 1), keys)
    values = jnp.where(pick_narrow, values, pltpu.roll(values, HEAD_WIDTH, 1))
    return queries, jnp.where(low, keys, values)


def enter_kernel(
    shards,
    groups,
    deal_ref,
    x_ref,
    wq_ref,
    wk_ref,
    wv_ref,
    small_ref,
    meta_ref,
    factors_ref,
    wide_ref,
    kv_ref,
    cos_ref,
    sin_ref,
    freq_ref,
    qkv_ref,
    low_ref,
    mask_ref,
    small_out,
    meta_out,
    xs,
    slices,
    weights,
    metas,
    merged,
    second,
    xsend,
    xrecv,
    wsend,
    wrecv,
    zsend,
    zrecv,
    msend,
    mrecv,
):
    me, plane = lax.axis_index("fsdp"), lax.axis_index("dp")
    heads = HEADS // shards
    share = max(1, shards // KEY_VALUE_HEADS)
    rows = x_ref.shape[0]
    part = wq_ref.shape[0]
    order = [mask for mask in range(1, shards)]

    for f in range(shards):
        chunk = f * heads * HEAD_WIDTH // LANES
        head = f // share
        pair = head // 2
        queries, others = head_columns(
            wq_ref[:, chunk * LANES : (chunk + 1) * LANES].astype(F32),
            (
                wk_ref[:, pair * LANES : (pair + 1) * LANES].astype(F32),
                wv_ref[:, pair * LANES : (pair + 1) * LANES].astype(F32),
            ),
            f % 2 == 1,
            head % 2 == 1,
            heads,
        )
        slices[f, :, 0:LANES] = queries.astype(BF)
        slices[f, :, LANES : 2 * LANES] = others.astype(BF)
        slices[f, :, 2 * LANES :] = small_ref[...]
    metas[plane] = meta_ref[...]

    greet([("fsdp", me, order), ("dp", plane, range(1, groups))])

    moving = Gather("fsdp", shards, x_ref, xs, (xsend, xrecv))
    plane_rows = shards * part

    def column_copy(mask):
        return pltpu.make_async_remote_copy(
            src_ref=slices.at[me ^ mask],
            dst_ref=weights.at[plane, me],
            send_sem=wsend.at[mask],
            recv_sem=wrecv.at[mask],
            device_id={"fsdp": me ^ mask},
            device_id_type=MESH,
        )

    def plane_copy(mask):
        return pltpu.make_async_remote_copy(
            src_ref=weights.at[plane],
            dst_ref=weights.at[plane],
            send_sem=zsend.at[mask],
            recv_sem=zrecv.at[mask],
            device_id={"dp": plane ^ mask},
            device_id_type=MESH,
        )

    def meta_copy(mask):
        return pltpu.make_async_remote_copy(
            src_ref=meta_ref,
            dst_ref=metas.at[plane],
            send_sem=msend.at[mask],
            recv_sem=mrecv.at[mask],
            device_id={"dp": plane ^ mask},
            device_id_type=MESH,
        )

    for mask in order:
        column_copy(mask).start()
    for mask in range(1, groups):
        meta_copy(mask).start()
    moving.start()
    weights[plane, me] = slices[me]

    half = HEAD_WIDTH
    at = pl.ds(pl.multiple_of(me * heads * half // LANES * LANES, LANES), LANES)
    head = me // share
    pair_at = pl.ds(pl.multiple_of(head // 2 * LANES, LANES), LANES)
    queries, others = head_columns(
        wide_ref[:, at].astype(F32),
        (kv_ref[0, :, pair_at].astype(F32), kv_ref[1, :, pair_at].astype(F32)),
        me % 2 == 1,
        head % 2 == 1,
        heads,
    )
    low_lane = lane_of((STACKED, LANES)) < half
    second[...] = jnp.zeros(second.shape, BF)
    second[0:STACKED, 0:LANES] = queries.astype(BF)
    second[STACKED : 2 * STACKED, LANES:] = jnp.where(low_lane, others, 0.0).astype(BF)
    second[2 * STACKED :, LANES:] = jnp.where(low_lane, 0.0, others).astype(BF)

    for mask in order:
        column_copy(mask).wait_recv()
    for mask in range(1, groups):
        plane_copy(mask).start()
    for mask in range(1, groups):
        meta_copy(mask).wait_recv()
    dealt = jnp.int32(0)
    for g in range(groups):
        dealt = dealt + jnp.where(deal_ref[g] == plane, g, 0)
    meta = jnp.zeros(meta_ref.shape, jnp.int32)
    for g in range(groups):
        meta = jnp.where(dealt == g, metas[g], meta)
    meta_out[...] = meta
    moving.stage(0)
    for mask in range(1, groups):
        plane_copy(mask).wait_recv()

    for g in range(groups):
        for f in range(shards):
            here = pl.ds((g * shards + f) * part, part)
            block = weights[g, f]
            small_out[here, :] = block[:, 2 * LANES :]
            merged[here, 0 : 2 * LANES] = block[:, : 2 * LANES]
    for s in range(3):
        merged[:, (2 + s) * LANES : (3 + s) * LANES] = factors_ref[s]
    gain = gain_row(small_out[...], 16)

    nseq = 4
    lanes = lane_of((1, LANES))
    starts, first = [], jnp.zeros((1, 1), jnp.int32)
    for s in range(nseq):
        starts.append(first)
        first = first + meta[8:9, s : s + 1]
    angles = [start.astype(F32) * freq_ref[...] for start in starts]
    start_cos = [jnp.cos(angle) for angle in angles]
    start_sin = [jnp.sin(angle) for angle in angles]
    adapters = [jnp.broadcast_to(meta[9:10, s : s + 1], (1, LANES)) for s in range(nseq)]
    keyed = lanes < half
    sign = jnp.where(lanes % half < half // 2, -1.0, 1.0)

    def compute(mask):
        block = me ^ mask
        at = pl.ds(pl.multiple_of(block * rows, rows), rows)
        x = x_ref[...] if mask == 0 else xs[block]
        full = x.astype(F32)
        r1 = lax.rsqrt(jnp.mean(full * full, axis=1, keepdims=True) + EPSILON)
        product = dot((full * r1 * gain).astype(BF), merged[...])
        base_cos, base_sin, pick = sequences(
            meta, block * rows, rows, (start_cos, start_sin, adapters)
        )
        masked = lane_of((rows, LANES)) // ADAPTER_RANK == pick
        mask_ref[at, :] = jnp.where(masked, 1.0, 0.0).astype(BF)
        lows = [
            jnp.where(masked, product[:, (2 + s) * LANES : (3 + s) * LANES], 0.0).astype(BF)
            for s in range(3)
        ]
        lows = jnp.concatenate(lows, axis=1)
        low_ref[at, :] = lows
        product = product[:, : 2 * LANES] + dot(lows, second[...])
        row_cos, row_sin = cos_ref[at, :], sin_ref[at, :]
        cosine = row_cos * base_cos + row_sin * base_sin
        sine = (row_sin * base_cos - row_cos * base_sin) * sign
        qkv_ref[at, :LANES] = turned(product[:, :LANES], cosine, sine).astype(BF)
        others = product[:, LANES:]
        qkv_ref[at, LANES:] = turned(
            others, jnp.where(keyed, cosine, 1.0), jnp.where(keyed, sine, 0.0)
        ).astype(BF)

    compute(0)
    done = [0]
    for k in range(1, len(bits_of(shards))):
        moving.stage(k)
        for mask in range(1, shards):
            if mask not in done and mask in moving.held(k):
                compute(mask)
                done.append(mask)
    moving.finish()
    for mask in order:
        column_copy(mask).wait_send()
    for mask in range(1, groups):
        plane_copy(mask).wait_send()
        meta_copy(mask).wait_send()


def enter(deal, x, wq, wk, wv, small, meta, factors, wide, kv_second, identity):
    shards, groups = lax.axis_size("fsdp"), lax.axis_size("dp")
    rows, part = x.shape[0], wq.shape[0]
    total = rows * shards
    half = HEAD_WIDTH // 2
    frequency = ROPE_BASE ** (-np.arange(half, dtype=np.float64) / half)
    frequency = frequency.astype(np.float32)
    angles = np.arange(total, dtype=np.float64)[:, None] * frequency.astype(np.float64)[None, :]
    cosine = jnp.asarray(np.tile(np.cos(angles).astype(np.float32), (1, 4)))
    sine = jnp.asarray(np.tile(np.sin(angles).astype(np.float32), (1, 4)))
    frequency = jnp.asarray(np.tile(frequency, 4)[None, :])
    return pl.pallas_call(
        functools.partial(enter_kernel, shards, groups),
        out_shape=(
            jax.ShapeDtypeStruct((total, 2 * LANES), BF),
            jax.ShapeDtypeStruct((total, 3 * STACKED), BF),
            jax.ShapeDtypeStruct((total, STACKED), BF),
            jax.ShapeDtypeStruct((MODEL_WIDTH, LANES), BF),
            jax.ShapeDtypeStruct(meta.shape, jnp.int32),
        ),
        in_specs=[pl.BlockSpec(memory_space=pltpu.SMEM)] + [IN_VMEM] * 12,
        out_specs=(IN_VMEM,) * 5,
        scratch_shapes=[
            pltpu.VMEM((shards, rows, MODEL_WIDTH), BF),
            pltpu.VMEM((shards, part, 3 * LANES), BF),
            pltpu.VMEM((groups, shards, part, 3 * LANES), BF),
            pltpu.VMEM((groups,) + meta.shape, jnp.int32),
            pltpu.VMEM((MODEL_WIDTH, 2 * LANES + 3 * STACKED), BF),
            pltpu.VMEM((3 * STACKED, 2 * LANES), BF),
        ]
        + pair_of_sems(shards)
        + [pltpu.SemaphoreType.DMA((shards,))] * 2
        + [pltpu.SemaphoreType.DMA((groups,))] * 4,
        compiler_params=remote(identity, 60),
        name="enter",
    )(deal, x, wq, wk, wv, small, meta, factors, wide, kv_second, cosine, sine, frequency)


def gain_row(small, lane):
    pick = jnp.where(lane_of((8, LANES)) == lane, 1.0, 0.0).astype(BF)
    return dot(pick, small, 1, 1)[0:1, :]


def turn_of(step, shards):
    late = (step + shards - 4) // shards
    return step + late * (shards + 3 - 2 * step)


def scatter_plan(moving, shards):
    place = {turn_of(t, shards): t for t in range(shards)}
    sent, plan = {}, []
    for t in range(shards):
        now = []
        for mask in range(1, shards):
            for h in range(2):
                sources = [mask ^ bit for bit in moving.orders[h][: moving.depth(h, mask)]]
                ready = all((h, s) in sent and sent[h, s] < t for s in sources)
                if (h, mask) not in sent and place[mask] <= t and ready:
                    now.append((h, mask))
        for item in now:
            sent[item] = t
        plan.append(now)
    rest = [(h, m) for m in range(1, shards) for h in range(2) if (h, m) not in sent]
    rest.sort(key=lambda item: moving.depth(*item))
    return plan, rest + [(0, 0), (1, 0)]


def experts_block(first_expert, n2, side, grad, mask, win, wout, wide_down, hid, down, spread, fold):
    rows = n2.shape[0]
    width = HIDDEN_UNITS
    lane = lane_of((rows, LANES))
    lows = dot(side, spread[:, : 2 * STACKED])
    low_gate = (lows[:, :STACKED] * mask).astype(BF)
    low_up = (lows[:, STACKED:] * mask).astype(BF)
    lift_gate = dot(low_gate, hid[0])
    lift_up = dot(low_up, hid[1])
    down_grad = (dot(grad, wide_down, 1, 1) * mask).astype(BF)
    from_down = dot(down_grad, down[...], 1, 1)
    side_full = side.astype(F32)
    total_inner = jnp.zeros((rows, width), F32)
    total_gate = jnp.zeros((rows, width), F32)
    total_up = jnp.zeros((rows, width), F32)
    extra = jnp.zeros((rows, LANES), F32)
    gated_parts, slope_parts = [], []
    for e in range(win.shape[1] // (2 * width)):
        name = first_expert + e
        at_high, at_low = lane == name, lane == name + EXPERT_COUNT
        gate = jnp.sum(jnp.where(at_high | at_low, side_full, 0.0), axis=1, keepdims=True)
        first = 2 * e * width
        pre_gate = dot(n2, win[:, first : first + width]) + lift_gate
        pre_up = dot(n2, win[:, first + width : first + 2 * width]) + lift_up
        pulled = dot(grad, wout[:, e * width : (e + 1) * width]) + from_down
        squashed = jax.nn.sigmoid(pre_gate)
        active = pre_gate * squashed
        inner = active * pre_up
        gate_grad = jnp.sum(inner * pulled, axis=1, keepdims=True)
        high = gate_grad.astype(BF).astype(F32)
        extra = extra + jnp.where(at_high, high, 0.0) + jnp.where(at_low, gate_grad - high, 0.0)
        gated = inner * gate
        pulled = pulled * gate
        grad_gate = pulled * pre_up * (squashed + active * (1.0 - squashed))
        grad_up = pulled * active
        gated_parts.append(gated.astype(BF))
        slope_parts += [grad_gate.astype(BF), grad_up.astype(BF)]
        total_inner = total_inner + gated
        total_gate = total_gate + grad_gate
        total_up = total_up + grad_up
    out = dot(jnp.concatenate(gated_parts, axis=1), wout[...], 1, 1)
    back = dot(jnp.concatenate(slope_parts, axis=1), win[...], 1, 1)
    total_inner = total_inner.astype(BF)
    total_gate = total_gate.astype(BF)
    total_up = total_up.astype(BF)
    shrunk = jnp.concatenate(
        [
            (dot(total_gate, hid[0], 1, 1) * mask).astype(BF),
            (dot(total_up, hid[1], 1, 1) * mask).astype(BF),
            (dot(total_inner, down[...]) * mask).astype(BF),
        ],
        axis=1,
    )
    extra = extra + dot(shrunk, fold[...])
    sums = (
        dot(total_inner, down_grad, 0, 0),
        dot(low_gate, total_gate, 0, 0),
        dot(low_up, total_up, 0, 0),
    )
    return out.astype(BF), back.astype(BF), extra.astype(BF), sums


def middle_kernel(
    shards,
    mine_ref,
    x_ref,
    cot_ref,
    small_ref,
    meta_ref,
    mask_ref,
    wo_ref,
    factors_ref,
    wide_ref,
    router2_ref,
    hid_ref,
    down_ref,
    spread_ref,
    fold_ref,
    cots_ref,
    win_ref,
    wout_ref,
    outs_ref,
    base_ref,
    hgrad_ref,
    heads_ref,
    gdown_ref,
    ghid_ref,
    gsecond_ref,
    gfactor_ref,
    gwide_ref,
    groute_ref,
    *scratch,
):
    near = shards <= 8
    store, block_in, scratch = (scratch[0], None, scratch[1:]) if near else (scratch[0], scratch[1], scratch[2:])
    middle_body(
        shards,
        near,
        (
            mine_ref,
            x_ref,
            cot_ref,
            small_ref,
            meta_ref,
            mask_ref,
            wo_ref,
            factors_ref,
            wide_ref,
            router2_ref,
            hid_ref,
            down_ref,
            spread_ref,
            fold_ref,
            cots_ref,
            win_ref,
            wout_ref,
        ),
        (
            outs_ref,
            base_ref,
            hgrad_ref,
            heads_ref,
            gdown_ref,
            ghid_ref,
            gsecond_ref,
            gfactor_ref,
            gwide_ref,
            groute_ref,
        ),
        store,
        block_in,
        *scratch,
    )


def middle_body(
    shards,
    near,
    given,
    results,
    store,
    block_in,
    own_in,
    part,
    land,
    win,
    wout,
    cots,
    outs,
    attended,
    gsend,
    grecv,
    ssend,
    srecv,
    wsem,
    csem,
    osem,
    bsem,
):
    (
        mine_ref,
        x_ref,
        cot_ref,
        small_ref,
        meta_ref,
        mask_ref,
        wo_ref,
        factors_ref,
        wide_ref,
        router2_ref,
        hid_ref,
        down_ref,
        spread_ref,
        fold_ref,
        cots_ref,
        win_ref,
        wout_ref,
    ) = given
    (
        outs_ref,
        base_ref,
        hgrad_ref,
        heads_ref,
        gdown_ref,
        ghid_ref,
        gsecond_ref,
        gfactor_ref,
        gwide_ref,
        groute_ref,
    ) = results
    me = lax.axis_index("fsdp")
    rows = x_ref.shape[0]
    if near:
        own_in = store.at[me]
    width = MODEL_WIDTH
    heads = HEADS // shards
    lane = lane_of((rows, LANES))
    loads = [
        pltpu.make_async_copy(win_ref, win, wsem.at[0]),
        pltpu.make_async_copy(wout_ref, wout, wsem.at[1]),
    ]
    for load in loads:
        load.start()

    def cot_copy(step):
        return pltpu.make_async_copy(
            cots_ref.at[me ^ turn_of(step, shards)], cots.at[step % 2], csem.at[step % 2]
        )

    cot_copy(0).start()
    greet([("fsdp", me, bits_of(shards))])

    for s in range(shards):
        if heads == 2:
            attended[:, s * LANES : (s + 1) * LANES] = mine_ref[s]
        elif s % 2 == 0:
            second = pltpu.roll(mine_ref[s + 1].astype(F32), HEAD_WIDTH, 1)
            both = jnp.where(lane < HEAD_WIDTH, mine_ref[s].astype(F32), second)
            attended[:, s // 2 * LANES : (s // 2 + 1) * LANES] = both.astype(BF)
    own = pl.ds(pl.multiple_of(me * rows, rows), rows)
    mask = mask_ref[own, :].astype(F32)
    small = small_ref[...]
    gain = gain_row(small, 17)
    out_low = (dot(attended[...], factors_ref[3]) * mask).astype(BF)
    hidden = (
        x_ref[...].astype(F32) + dot(attended[...], wo_ref[...], 1, 1) + dot(out_low, wide_ref[1])
    )
    base_ref[...] = hidden
    r2 = lax.rsqrt(jnp.mean(hidden * hidden, axis=1, keepdims=True) + EPSILON)
    n2 = (hidden * r2 * gain).astype(BF)
    own_in[:, :width] = n2
    lows = [(dot(n2, factors_ref[s]) * mask).astype(BF) for s in range(3)]
    logits = dot(n2, small) + dot(lows[0], router2_ref[...])
    named = jnp.zeros((LANES, rows), jnp.bool_)
    for k in range(TOPK):
        named = named | (row_of((LANES, rows)) == meta_ref[k : k + 1, :])
    eye = jnp.where(row_of((LANES, LANES)) == lane_of((LANES, LANES)), 1.0, 0.0).astype(BF)
    picked = dot(jnp.where(named, 1.0, 0.0).astype(BF), eye, 0, 0) > 0.5
    peak = jnp.max(jnp.where(picked, logits, MASKED), axis=1, keepdims=True)
    lifted = jnp.where(picked, jnp.exp(jnp.where(picked, logits, peak) - peak), 0.0)
    gates = lifted / jnp.sum(lifted, axis=1, keepdims=True)
    high = gates.astype(BF).astype(F32)
    shrunk = dot(jnp.concatenate(lows[1:], axis=1), fold_ref[: 2 * STACKED, :])
    side = high + pltpu.roll(gates - high, EXPERT_COUNT, 1) + shrunk
    own_in[:, width:] = side.astype(BF)

    going = Gather("fsdp", shards, own_in, store, (gsend, grecv))
    coming = Scatter("fsdp", shards, part, land, (ssend, srecv))
    going.start()
    for load in loads:
        load.wait()

    last = len(bits_of(shards)) - 1
    early, late = [], []
    for k in range(last):
        for s in range(1 << k):
            for h in range(2):
                order = going.orders[h]
                (late if shards == 8 and k == 1 and s else early).append(
                    (h, order[k] ^ span(order[:k])[s])
                )
    plan, rest = scatter_plan(coming, shards)
    first_expert = me * (EXPERT_COUNT // shards)

    def step(t, carry):
        turn = turn_of(t, shards)
        block = me ^ turn
        slot = t % 2

        @pl.when(t == 2)
        def _():
            for h, m in early:
                going.take(h, m)

        @pl.when(t == 3)
        def _():
            for h, m in late:
                going.take(h, m)

        for k in range(1, shards):
            m = turn_of(k, shards)
            if m % 2:

                @pl.when(t == k)
                def _(m=m):
                    for h in range(2):
                        going.take(h, m)

        @pl.when(t + 1 < shards)
        def _():
            cot_copy(t + 1).start()

        cot_copy(t).wait()

        def out_copy(at):
            return pltpu.make_async_copy(
                outs.at[at % 2], outs_ref.at[me ^ turn_of(at, shards)], osem.at[at % 2]
            )

        @pl.when(t >= 2)
        def _():
            out_copy(t - 2).wait()

        block_rows = pl.ds(pl.multiple_of(block * rows, rows), rows)
        if near:
            here = store.at[block]
        else:
            here = block_in

            @pl.when(t == 0)
            def _():
                block_in[...] = own_in[...]

            @pl.when(t != 0)
            def _():
                fetch = pltpu.make_async_copy(store.at[block], block_in, bsem)
                fetch.start()
                fetch.wait()

        out, back, extra, sums = experts_block(
            first_expert,
            here[:, :width],
            here[:, width:],
            cots[slot],
            mask_ref[block_rows, :].astype(F32),
            win,
            wout,
            wide_ref[2],
            hid_ref,
            down_ref,
            spread_ref,
            fold_ref,
        )
        outs[slot] = out
        out_copy(t).start()
        part[block, :, :width] = back
        part[block, :, width:] = extra

        @pl.when(t == 0)
        def _():
            gdown_ref[...] = sums[0]
            ghid_ref[0] = sums[1]
            ghid_ref[1] = sums[2]

        @pl.when(t != 0)
        def _():
            gdown_ref[...] += sums[0]
            ghid_ref[0] += sums[1]
            ghid_ref[1] += sums[2]

        for k in range(shards):
            if plan[k]:

                @pl.when(t == k)
                def _(k=k):
                    for h, m in plan[k]:
                        coming.reduce(h, m)

        @pl.when(t == shards - 1)
        def _():
            out_copy(shards - 2).wait()
            out_copy(shards - 1).wait()

        return carry

    lax.fori_loop(0, shards, step, 0)
    for h, m in rest:
        coming.reduce(h, m)

    hidden = base_ref[...]
    mask = mask_ref[own, :].astype(F32)
    r2 = lax.rsqrt(jnp.mean(hidden * hidden, axis=1, keepdims=True) + EPSILON)
    n2 = own_in[:, :width]
    cot = cot_ref[...]
    grad = cot.astype(F32)
    extra = part[me, :, width:]
    extra_full = extra.astype(F32)
    gate_grad = extra_full + pltpu.roll(extra_full, LANES - EXPERT_COUNT, 1)
    logit_grad = gates * (gate_grad - jnp.sum(gates * gate_grad, axis=1, keepdims=True))
    logit_grad = jnp.where(lane < EXPERT_COUNT, logit_grad, 0.0).astype(BF)
    wider = dot(extra, spread_ref[...])
    second_grad = [
        (dot(logit_grad, router2_ref[...], 1, 1) * mask).astype(BF),
        (wider[:, :STACKED] * mask).astype(BF),
        (wider[:, STACKED : 2 * STACKED] * mask).astype(BF),
    ]
    down_low = (wider[:, 2 * STACKED :] * mask).astype(BF)
    base_ref[...] = hidden + dot(down_low, wide_ref[2])
    gwide_ref[1] = dot(down_low, cot, 0, 0)
    groute_ref[...] = dot(lows[0], logit_grad, 0, 0)
    n2_grad = part[me, :, :width].astype(F32) + dot(logit_grad, small, 1, 1)
    for s in range(3):
        n2_grad = n2_grad + dot(second_grad[s], factors_ref[s], 1, 1)
    gsecond_ref[...] = dot(n2, jnp.concatenate(second_grad, axis=1), 0, 0)
    w2 = gain * n2_grad
    hidden_grad = grad + r2 * w2 - hidden * (r2 * r2 * r2) * jnp.mean(w2 * hidden, axis=1, keepdims=True)
    hgrad_ref[...] = hidden_grad
    out_grad = hidden_grad.astype(BF)
    gwide_ref[0] = dot(out_low, out_grad, 0, 0)
    out_low_grad = (dot(out_grad, wide_ref[1], 1, 1) * mask).astype(BF)
    gfactor_ref[...] = dot(attended[...], out_low_grad, 0, 0)
    attended_grad = dot(out_grad, wo_ref[...]) + dot(out_low_grad, factors_ref[3], 1, 1)
    for s in range(shards):
        if heads == 2:
            heads_ref[s] = attended_grad[:, s * LANES : (s + 1) * LANES].astype(BF)
        else:
            pair = attended_grad[:, s // 2 * LANES : (s // 2 + 1) * LANES]
            if s % 2:
                pair = pltpu.roll(pair, HEAD_WIDTH, 1)
            heads_ref[s] = jnp.where(lane < HEAD_WIDTH, pair, 0.0).astype(BF)
    going.finish()
    coming.finish()


def middle(mine, x, cot, small, meta, mask, wo, factors, wide, router2, hid, down, cots, win, wout, identity):
    shards = lax.axis_size("fsdp")
    rows = x.shape[0]
    side = MODEL_WIDTH + LANES
    source = np.arange(LANES)
    place = np.arange(STACKED) % ADAPTER_RANK
    spread = np.concatenate([source[:, None] == o + place[None, :] for o in (32, 48, 64)], axis=1)
    fold = np.concatenate([source[None, :] == o + place[:, None] for o in (32, 48, 64)], axis=0)
    spread, fold = jnp.asarray(spread, BF), jnp.asarray(fold, BF)
    gathered = (shards, rows, side)
    near = shards <= 8
    results = pl.pallas_call(
        functools.partial(middle_kernel, shards),
        out_shape=(
            jax.ShapeDtypeStruct((shards, rows, MODEL_WIDTH), BF),
            jax.ShapeDtypeStruct((rows, MODEL_WIDTH), F32),
            jax.ShapeDtypeStruct((rows, MODEL_WIDTH), F32),
            jax.ShapeDtypeStruct((shards, rows, LANES), BF),
            jax.ShapeDtypeStruct((HIDDEN_UNITS, STACKED), F32),
            jax.ShapeDtypeStruct((2, STACKED, HIDDEN_UNITS), F32),
            jax.ShapeDtypeStruct((MODEL_WIDTH, 3 * STACKED), F32),
            jax.ShapeDtypeStruct((MODEL_WIDTH, STACKED), F32),
            jax.ShapeDtypeStruct((2, STACKED, MODEL_WIDTH), F32),
            jax.ShapeDtypeStruct((STACKED, LANES), F32),
        )
        + (() if near else (jax.ShapeDtypeStruct(gathered, BF),)),
        in_specs=[IN_VMEM] * 14 + [ANYWHERE] * 3,
        out_specs=(ANYWHERE,) + (IN_VMEM,) * 9 + (() if near else (ANYWHERE,)),
        scratch_shapes=[
            pltpu.VMEM(gathered if near else gathered[1:], BF),
            pltpu.VMEM((16, LANES) if near else gathered[1:], BF),
            pltpu.VMEM((shards, rows, side), BF),
            pltpu.VMEM((2, shards - 1, rows // 2, side), BF),
            pltpu.VMEM(win.shape, BF),
            pltpu.VMEM(wout.shape, BF),
            pltpu.VMEM((2, rows, MODEL_WIDTH), BF),
            pltpu.VMEM((2, rows, MODEL_WIDTH), BF),
            pltpu.VMEM((rows, MODEL_WIDTH), BF),
        ]
        + pair_of_sems(shards) * 2
        + [pltpu.SemaphoreType.DMA((2,))] * 3
        + [pltpu.SemaphoreType.DMA(())],
        compiler_params=remote(identity, 62),
        name="middle",
    )(mine, x, cot, small, meta, mask, wo, factors, wide, router2, hid, down, spread, fold, cots, win, wout)
    return results[:10]


def rotate(tensor, cosine, sine):
    rows = tensor.shape[0]
    view = tensor.reshape(rows, -1, 2, HEAD_WIDTH // 2)
    first, second = view[:, :, 0], view[:, :, 1]
    c, s = cosine[:, None, :], sine[:, None, :]
    turned = jnp.stack([first * c - second * s, second * c + first * s], axis=2)
    return turned.reshape(rows, -1)


def local(
    tokens,
    cotangent,
    lengths,
    adapter_index,
    routes,
    deal,
    norm_gain_pair,
    query_weight,
    key_weight,
    value_weight,
    output_weight_transposed,
    router_weight,
    expert_input_weight,
    expert_output_weight,
    factors,
    down_first,
    wide,
    kv_second,
    hidden_second,
    router_second,
):
    shards = lax.axis_size("fsdp")
    groups = lax.axis_size("dp")
    rows = tokens.shape[0]
    total = rows * shards
    heads = HEADS // shards
    share = max(1, shards // KEY_VALUE_HEADS)
    me = lax.axis_index("fsdp")

    padded = ((0, 0), (0, rows - lengths.shape[1]))
    meta = jnp.concatenate(
        [
            routes.T,
            jnp.pad(lengths, padded),
            jnp.pad(adapter_index, padded),
            jnp.zeros((6, rows), jnp.int32),
        ],
        axis=0,
    )
    small = jnp.concatenate(
        [
            router_weight,
            norm_gain_pair,
            jnp.zeros((router_weight.shape[0], LANES - EXPERT_COUNT - 2), BF),
        ],
        axis=1,
    )
    qkv, low_all, group_mask, small, meta = enter(
        deal,
        tokens,
        query_weight,
        key_weight,
        value_weight,
        small,
        meta,
        factors[0:3],
        wide[0],
        kv_second,
        1,
    )
    lens = meta[8:9, : lengths.shape[1]]
    gains = small[:, EXPERT_COUNT : EXPERT_COUNT + 2].astype(F32)
    mask_low = lax.dynamic_slice_in_dim(group_mask, me * rows, rows, 0)
    mask = mask_low.astype(F32)
    win = expert_input_weight.reshape(MODEL_WIDTH, -1)
    wout = expert_output_weight.reshape(MODEL_WIDTH, -1)
    all_grad = lax.all_gather(cotangent, "fsdp", axis=0, tiled=True)
    out_weight = lax.all_gather(output_weight_transposed, ("dp", "fsdp"), axis=0, tiled=True)

    x = tokens.astype(F32)
    r1 = lax.rsqrt(jnp.mean(x * x, axis=1, keepdims=True) + EPSILON)
    normed = (x * r1 * gains[:, 0]).astype(BF)
    first_low = lax.dynamic_slice_in_dim(low_all, me * rows, rows, 0)
    first_low = [first_low[:, s * STACKED : (s + 1) * STACKED] for s in range(3)]

    def by_head(array, count, repeat):
        array = array.astype(BF).reshape(rows, count, -1).transpose(1, 0, 2)
        return jnp.repeat(array, repeat, axis=0) if repeat > 1 else array

    in_weight = lax.all_gather(
        jnp.concatenate([query_weight, key_weight, value_weight], axis=1),
        ("dp", "fsdp"),
        axis=0,
        tiled=True,
    )
    offsets = jnp.cumsum(lens[0]) - lens[0]
    index = me * rows + jnp.arange(rows, dtype=jnp.int32)
    inside = (index[:, None] >= offsets[None, :]) & (index[:, None] < (offsets + lens[0])[None, :])
    begin = jnp.sum(jnp.where(inside, offsets[None, :], 0), axis=1)
    half = HEAD_WIDTH // 2
    frequency = ROPE_BASE ** (-jnp.arange(half, dtype=F32) / half)
    angles = (index - begin).astype(F32)[:, None] * frequency[None, :]
    cosine, sine = jnp.cos(angles), jnp.sin(angles)
    attended, q_kept, k_kept, v_kept = attend(lens, qkv, heads)

    mine = plane_swap(attended.reshape(shards, rows, -1), 5)
    router2 = jnp.pad(router_second, ((0, 0), (0, LANES - EXPERT_COUNT)))
    (
        out_part,
        base,
        hidden_grad,
        to_heads,
        g_down_a,
        g_ff,
        g_second,
        g_factor_out,
        g_wide,
        g_route,
    ) = middle(
        mine,
        tokens,
        cotangent,
        small,
        meta,
        group_mask,
        out_weight,
        factors[3:7],
        wide,
        router2,
        hidden_second,
        down_first,
        all_grad.reshape(shards, rows, -1),
        win,
        wout,
        6,
    )
    layer_out = (base + scatter(out_part, "fsdp", 7).astype(F32)).astype(BF)
    g_second = [g_second[:, s * STACKED : (s + 1) * STACKED] for s in range(3)]
    g_wide_out, g_wide_down = g_wide[0], g_wide[1]
    head_grad = plane_swap(to_heads, 9).reshape(total, -1)
    qkv_grad = attend_back(lens, q_kept, k_kept, v_kept, attended, head_grad, heads)
    qkv_grad = plane_swap(qkv_grad.reshape(shards, rows, -1), 10).astype(F32)

    def joined(array):
        array = array.reshape(shards // share, share, rows, -1).sum(1)
        return array.transpose(1, 0, 2).reshape(rows, -1)

    query_grad = qkv_grad[:, :, : heads * HEAD_WIDTH].transpose(1, 0, 2).reshape(rows, -1)
    query_grad = rotate(query_grad, cosine, -sine).astype(BF)
    keys_grad = rotate(joined(qkv_grad[:, :, LANES : LANES + 64]), cosine, -sine).astype(BF)
    values_grad = joined(qkv_grad[:, :, LANES + 64 :]).astype(BF)
    mixed_grad = jnp.concatenate([query_grad, keys_grad, values_grad], axis=1)
    normed_grad = dot(mixed_grad, in_weight, 1, 1)
    first_grad = [
        (dot(query_grad, wide[0], 1, 1) * mask).astype(BF),
        (dot(keys_grad, kv_second[0], 1, 1) * mask).astype(BF),
        (dot(values_grad, kv_second[1], 1, 1) * mask).astype(BF),
    ]
    for s in range(3):
        normed_grad = normed_grad + dot(first_grad[s], factors[s], 1, 1)
    g_first = [dot(normed, first_grad[s], 0, 0) for s in range(3)]
    g_wide_query = dot(first_low[0], query_grad, 0, 0)
    g_kv = [dot(first_low[1], keys_grad, 0, 0), dot(first_low[2], values_grad, 0, 0)]
    w1 = gains[:, 0] * normed_grad
    input_grad = hidden_grad + r1 * w1 - x * r1**3 * jnp.mean(w1 * x, axis=1, keepdims=True)

    def tall(array):
        return [array[:, c : c + LANES] for c in range(0, array.shape[1], LANES)]

    pieces = g_first + g_second + [g_factor_out, g_down_a]
    for array in [g_wide_query, g_wide_out, g_wide_down] + g_kv + [g_ff[0], g_ff[1]]:
        pieces = pieces + tall(array)
    pieces = pieces + [g_route]
    sums = total_of(jnp.concatenate([p.astype(BF) for p in pieces], axis=0), 11).astype(F32)

    def wide_sum(start, count, parts):
        block = sums[start : start + count * parts * STACKED]
        block = block.reshape(count, parts, STACKED, LANES).transpose(0, 2, 1, 3)
        return block.reshape(count, STACKED, parts * LANES)

    edge = 7 * MODEL_WIDTH
    factor_sum = sums[:edge].reshape(7, MODEL_WIDTH, STACKED)
    down_sum = sums[edge : edge + HIDDEN_UNITS]
    edge += HIDDEN_UNITS
    wide_total = wide_sum(edge, 3, 8)
    edge += 24 * STACKED
    kv_total = wide_sum(edge, 2, 4)
    edge += 8 * STACKED
    ff_total = wide_sum(edge, 2, 4)
    edge += 8 * STACKED
    route_total = sums[edge : edge + STACKED, :EXPERT_COUNT]
    return (
        layer_out,
        input_grad,
        factor_sum,
        down_sum,
        wide_total,
        kv_total,
        ff_total,
        route_total,
    )


def solution(mesh):
    rows = P(("dp", "fsdp"), None)
    placed = (
        (rows, rows, P("dp", None), P("dp", None), rows, P())
        + (rows,) * 6
        + (P(None, "fsdp", None),) * 2
        + (P(),) * 6
    )
    return jax.shard_map(
        local,
        mesh=mesh,
        in_specs=placed,
        out_specs=(rows, rows) + (P(),) * 6,
        check_vma=False,
    )
```

time: 702 us -> 463 us (0.66)
  Pallas kernels: 494 us -> 361 us
  local copies, waits for them, and re-layouts: 82.1 us -> 41.9 us
  matrix products: 58.2 us -> 20.3 us
  blocking collectives: 33.7 us -> 0 us
  between operations: 4.38 us -> 14.7 us
  other arithmetic: 19.6 us -> 10.6 us
    pallas_call x2 -> x1, Pallas kernels: 78.4 us -> 37.4 us  [scatter(): pl.pallas_call(functools.partial(scatter_kernel, axis, count), out_shape=...]
    dot_general x44 -> x13, matrix products: 58.2 us -> 20.3 us  [dot(): lax.dot_general(a, b, (((ca,), (cb,)), ((), ())), preferred_element_type=...]
    all_gather x3 -> x0, blocking collectives: 33.7 us -> none  [of_group(): everything = lax.all_gather(array, 'dp', axis=0, tiled=False)]
    pallas_call x1, Pallas kernels: 53.8 us -> 23.2 us  [attend(): pl.pallas_call(functools.partial(attend_kernel, heads), out_shape=(jax.Sh...]
    pallas_call x1, Pallas kernels: 58.5 us -> 34.7 us  [attend_back(): pl.pallas_call(functools.partial(attend_back_kernel, heads), out_shape=ja...]
    pallas_call x5 -> x2, Pallas kernels: 179 us -> 160 us  [the longest x1 111 us: middle(): pl.pallas_call(functools.partial(middle_kernel, shards), out_shape=(jax.S...]
    pallas_call x4 -> x3, Pallas kernels: 66.6 us -> 49.6 us  [swap(): pl.pallas_call(functools.partial(swap_kernel, axis, count), out_shape=jax...]
    unnamed x186 -> x107, local copies, waits for them, and re-layouts: 24.3 us -> 14.6 us
  transfers between devices with their start and end apart: 0 -> 3, of which waited for: 0 -> 1; matrix products, arithmetic and copies ran while one was open for 0% -> 9% of each run, Pallas kernels for 0% -> 59%
where the time goes in v3:
time: 463 us; the launch traced here: 456 us
  Pallas kernels  361 us (78%)
  local copies, waits for them, and re-layouts  41.9 us (9%)
  matrix products  20.3 us (4%)
  between operations  14.7 us (3%)
  other arithmetic  10.6 us (2%)
  waiting for transfers between devices  6.62 us (1%)
    pallas_call x1, Pallas kernels, middle(): pl.pallas_call(functools.partial(middle_kernel, shards), out_shape=(jax.S...  111 us
    pallas_call x1, Pallas kernels, total_of(): pl.pallas_call(functools.partial(total_kernel, shards, groups), out_shape...  56.6 us
    pallas_call x3, Pallas kernels, swap(): pl.pallas_call(functools.partial(swap_kernel, axis, count), out_shape=jax...  49.6 us
    pallas_call x1, Pallas kernels, enter(): pl.pallas_call(functools.partial(enter_kernel, shards, groups), out_shape...  48.7 us
    pallas_call x1, Pallas kernels, scatter(): pl.pallas_call(functools.partial(scatter_kernel, axis, count), out_shape=...  37.4 us
    pallas_call x1, Pallas kernels, attend_back(): pl.pallas_call(functools.partial(attend_back_kernel, heads), out_shape=ja...  34.7 us
    pallas_call x1, Pallas kernels, attend(): pl.pallas_call(functools.partial(attend_kernel, heads), out_shape=(jax.Sh...  23.2 us
    dot_general x13, matrix products, dot(): lax.dot_general(a, b, (((ca,), (cb,)), ((), ())), preferred_element_type=...  20.3 us
  transfers between devices with their start and end apart: 3, of which 1 were waited for; matrix products, arithmetic and copies ran while one was open for 9% of the time, Pallas kernels for 59%

profile of v3, /device:TPU:0, one launch (start us, length us, event | category | flops | bytes accessed | tf_op | source)
XLA Modules:
  0.0 455.6 jit_solution(341465238272830467)
XLA Ops:
  8.8 1.5 pad_maximum_fusion
  10.3 2.1 slice.267.factors_ref
  15.2 1.7 slice_bitcast_fusion.2.wide_ref
  16.9 48.7 %enter.1 = (bf16[3072,256]{1,0:T(8,128)(2,1)}, bf16[3072,384]{1,0:T(8,128)(2,1)}, bf16[3072,128]{1,0:T(8,128)(2,1)}, bf16[1024,128]{1,0:T(8,128)(2,1)}, s32[16,384]{1,0:T(8,128)}) custom-call(s32[4]{0:T(128)} %deal_ref.1, bf16[384,1024]{1,0:T(8,128)(2,1)} %x_ref.3, bf16[32,1024]{1,0:T(8,128)(2,1)} %wq_ref.1, bf16[32,512]{1,0:T(8,128)(2,1)} %wk_ref.1, ...), custom_call_target="tpu_custom_call" | custom-call | tf_op jit(solution)/shard_map/enter/pallas_call | solution.py:813
  67.7 23.2 %attend.1 = (bf16[3072,128]{1,0:T(8,128)(2,1)}, bf16[2,3072,256]{2,1,0:T(8,128)(2,1)}, bf16[3072,256]{1,0:T(8,128)(2,1)}, bf16[3072,256]{1,0:T(8,128)(2,1)}) custom-call(s32[1,4]{1,0:T(1,128)} %get-tuple-element.59.lens_ref, bf16[3072,256]{1,0:T(8,128)(2,1)} %get-tuple-element.28.qkv_ref), custom_call_target="tpu_custom_call" | custom-call | tf_op jit(solution)/shard_map/attend/pallas_call | solution.py:128
  92.0 16.5 %swap.3.mine_ref = bf16[8,384,128]{2,1,0:T(8,128)(2,1)S(1)} custom-call(bf16[8,384,128]{2,1,0:T(8,128)(2,1)S(1)} %bitcast.90), custom_call_target="tpu_custom_call" | custom-call | tf_op jit(solution)/shard_map/swap/pallas_call | solution.py:485
  108.6 5.9 %copy.61 = bf16[128,8,2,1024]{3,1,2,0:T(8,128)(2,1)} copy(bf16[128,8,2,1024]{3,2,1,0:T(2,128)(2,1)} %bitcast.99) | data formatting | bytes 8388608
  114.5 1.9 copy.62
  117.8 5.2 %all-gather.6.cloned.1.call-done = bf16[3072,1024]{1,0:T(8,128)(2,1)} async-done(((bf16[384,1024]{1,0:T(8,128)(2,1)}), bf16[3072,1024]{1,0:T(8,128)(2,1)}) %all-gather.6.cloned.1.call-update) | async-done | bytes 6291472 | tf_op jit(solution)/shard_map/all_gather | solution.py:1407
  123.1 111.1 %middle.1 = (bf16[8,384,1024]{2,1,0:T(8,128)(2,1)}, f32[384,1024]{1,0:T(8,128)}, f32[384,1024]{1,0:T(8,128)}, bf16[8,384,128]{2,1,0:T(8,128)(2,1)}, f32[512,128]...) custom-call(bf16[8,384,128]{2,1,0:T(8,128)(2,1)} %copy-done.1, ...), custom_call_target="tpu_custom_call" | custom-call | tf_op jit(solution)/shard_map/middle/pallas_call | solution.py:1294
  235.3 11.8 %swap.4 = bf16[8,384,128]{2,1,0:T(8,128)(2,1)S(1)} custom-call(bf16[8,384,128]{2,1,0:T(8,128)(2,1)S(1)} %copy-done.4), custom_call_target="tpu_custom_call" | custom-call | tf_op jit(solution)/shard_map/swap/pallas_call | solution.py:485
  248.0 34.7 %attend_back.1 = bf16[3072,256]{1,0:T(8,128)(2,1)} custom-call(s32[1,4]{1,0:T(1,128)} %get-tuple-element.59.lens_ref, bf16[2,3072,256]{2,1,0:T(8,128)(2,1)} %get-tuple-element.35.q_ref, bf16[3072,256]{1,0:T(8,128)(2,1)} %get-tuple-element.36.k_ref, bf16[3072,256]{1,0:T(8,128)(2,1)} %get-tuple-element.37.v_ref, bf16[3072,128]{1,0:T(8,128)(2,1)} %get-tuple-element.29.out_ref, ...), custom_call_target="tpu_custom_call" | custom-call | tf_op jit(solution)/shard_map/attend_back/pallas_call | solution.py:219
  282.7 1.4 copy-done
  284.1 21.2 %swap.5 = bf16[8,384,256]{2,1,0:T(8,128)(2,1)S(1)} custom-call(bf16[8,384,256]{2,1,0:T(8,128)(2,1)S(1)} %bitcast.89), custom_call_target="tpu_custom_call" | custom-call | tf_op jit(solution)/shard_map/swap/pallas_call | solution.py:485
  305.6 1.2 slice_bitcast_fusion.1
  306.9 3.0 copy.53
  311.2 2.7 copy.54
  315.1 1.5 copy.55
  316.6 1.3 multiply_subtract_fusion.1
  318.3 1.3 fusion.16
  320.8 1.4 fusion.15
  322.2 1.3 fusion.24
  323.6 2.5 fusion.22
  326.0 4.4 fusion.6
  330.5 2.8 fusion
  335.6 1.3 convolution_convert_fusion
  340.5 2.0 pad.18
  342.5 56.6 %total.1 = bf16[8,1664,128]{2,1,0:T(8,128)(2,1)S(1)} custom-call(bf16[8,1664,128]{2,1,0:T(8,128)(2,1)} %bitcast.93), custom_call_target="tpu_custom_call" | custom-call | tf_op jit(solution)/shard_map/total/pallas_call | solution.py:534
  399.9 2.1 slice.390
  403.7 1.4 reshape.189
  408.5 37.4 %scatter.1 = bf16[384,1024]{1,0:T(8,128)(2,1)} custom-call(bf16[8,384,1024]{2,1,0:T(8,128)(2,1)} %get-tuple-element.33.given), custom_call_target="tpu_custom_call" | custom-call | tf_op jit(solution)/shard_map/scatter/pallas_call | solution.py:444
  445.9 2.9 fusion.2
  (159 shorter events, 26.5 us)
Async XLA Ops:
  7.2 5.2 %copy-start.9 = (bf16[7,1024,128]{2,1,0:T(8,128)(2,1)S(1)}, bf16[7,1024,128]{2,1,0:T(8,128)(2,1)}, u32[]{:S(2)}) copy-start(bf16[7,1024,128]{2,1,0:T(8,128)(2,1)} %param.39) | copy-start | bytes 5505028
  7.2 6.4 %copy-start.24 = (bf16[32,16]{0,1:T(8,128)(2,1)S(1)}, bf16[32,16]{0,1:T(8,128)(2,1)}, u32[]{:S(2)}) copy-start(bf16[32,16]{0,1:T(8,128)(2,1)} %param.36) | copy-start | bytes 3076
  7.2 6.5 %copy-start.28 = (bf16[32,2]{0,1:T(2,128)(2,1)S(1)}, bf16[32,2]{0,1:T(2,128)(2,1)}, u32[]{:S(2)}) copy-start(bf16[32,2]{0,1:T(2,128)(2,1)} %param.31) | copy-start | bytes 388
  7.2 7.3 %copy-start.23 = (s32[384,8]{0,1:T(8,128)S(1)}, s32[384,8]{0,1:T(8,128)}, u32[]{:S(2)}) copy-start(s32[384,8]{0,1:T(8,128)} %param.29) | copy-start | bytes 36868
  7.2 7.3 %copy-start.27 = (s32[1,4]{1,0:T(1,128)S(1)}, s32[1,4]{1,0:T(1,128)}, u32[]{:S(2)}) copy-start(s32[1,4]{1,0:T(1,128)} %param.27) | copy-start | bytes 52
  7.2 7.3 %copy-start.26 = (s32[1,4]{1,0:T(1,128)S(1)}, s32[1,4]{1,0:T(1,128)}, u32[]{:S(2)}) copy-start(s32[1,4]{1,0:T(1,128)} %param.28) | copy-start | bytes 52
  7.2 110.6 %all-gather.4.cloned.1.call-start = ((), (), s32[]{:S(2)}) async-start(), calls=%async_computation | async-start | bytes 2162688 | tf_op jit(solution)/shard_map/all_gather | solution.py:1408
  8.0 115.1 %all-gather.6.cloned.1.call-start = ((), (), s32[]{:S(2)}) async-start(), calls=%async_computation.1 | async-start | bytes 7077888 | tf_op jit(solution)/shard_map/all_gather | solution.py:1407
  8.7 317.3 %all-gather.8.cloned.1.call-start = ((), (), s32[]{:S(2)}) async-start(), calls=%async_computation.2 | async-start | bytes 4325376 | tf_op jit(solution)/shard_map/all_gather | solution.py:1420
  90.9 1.1 copy-start.2
  108.6 6.0 %copy-start.1 = (bf16[8,384,128]{2,1,0:T(8,128)(2,1)}, bf16[8,384,128]{2,1,0:T(8,128)(2,1)S(1)}, u32[]{:S(2)}) copy-start(bf16[8,384,128]{2,1,0:T(8,128)(2,1)S(1)} %swap.3.mine_ref) | copy-start | bytes 2359300
  108.6 6.0 %copy-start.12 = (bf16[1024,2,512]{2,1,0:T(2,128)(2,1)S(1)}, bf16[1024,2,512]{2,1,0:T(2,128)(2,1)}, u32[]{:S(2)}) copy-start(bf16[1024,2,512]{2,1,0:T(2,128)(2,1)} %param.38) | copy-start | bytes 6291460
  114.5 1.9 copy-start.25
  114.5 2.8 copy-start.16
  234.2 1.1 copy-start.4
  247.1 0.9 copy-start.3
  282.7 1.4 copy-start
  315.1 2.9 copy-start.6
  316.6 1.7 copy-start.17
  318.3 5.3 %copy-start.10 = (bf16[384,16,2,32]{0,3,2,1:T(8,128)(2,1)}, bf16[384,16,2,32]{0,3,2,1:T(8,128)(2,1)S(1)}, u32[]{:S(2)}) copy-start(bf16[384,16,2,32]{0,3,2,1:T(8,128)(2,1)S(1)} %maximum_convert_fusion) | copy-start | bytes 2359300
  326.0 4.4 copy-start.5
  326.0 4.4 copy-start.7
  333.3 1.8 copy-start.13
  334.4 1.2 copy-start.11
  334.4 2.5 copy-start.18
  335.0 2.0 copy-start.19
  335.0 2.2 copy-start.20
  335.6 4.6 %copy-start.21 = (f32[2,128,512]{2,1,0:T(8,128)S(1)}, f32[2,128,512]{2,1,0:T(8,128)}, u32[]{:S(2)}) copy-start(f32[2,128,512]{2,1,0:T(8,128)} %get-tuple-element.44) | copy-start | bytes 1572868
  337.0 3.5 copy-start.22
  408.5 37.5 %copy-start.8 = (f32[384,1024]{1,0:T(8,128)S(1)}, f32[384,1024]{1,0:T(8,128)}, u32[]{:S(2)}) copy-start(f32[384,1024]{1,0:T(8,128)} %get-tuple-element.64) | copy-start | bytes 4718596
  408.5 37.5 %copy-start.14 = (f32[384,1024]{1,0:T(8,128)S(1)}, f32[384,1024]{1,0:T(8,128)}, u32[]{:S(2)}) copy-start(f32[384,1024]{1,0:T(8,128)} %get-tuple-element.32) | copy-start | bytes 4718596
  408.5 37.5 %copy-start.15 = (f32[384,1024]{1,0:T(8,128)S(1)}, f32[384,1024]{1,0:T(8,128)}, u32[]{:S(2)}) copy-start(f32[384,1024]{1,0:T(8,128)} %get-tuple-element.34) | copy-start | bytes 4718596
Sparse Core Ops, SparseCore 0:
  10.9 62.5 all-gather.3
  75.4 47.5 all-gather.5
  126.5 63.4 all-gather.7
